TPU v7x, 32 devices: a whole 2x2x4 slice. The times are simulated.
32 devices in a mesh: node: 8 (over z, y), local: 4 (over x, core).
Axes of the slice: x: 2, y: 2, z: 4, core: 2. Of those that a mesh axis runs over, the one named last changes fastest.
Arguments:
- hidden_in: bfloat16 [1024, 7168], P('node', 'local'), may hold values from -6 to 6
- out_grad: bfloat16 [1024, 7168], P('node', 'local'), may hold values from -0.59765625 to 0.59765625
- expert_ids: int32 [1024, 6], P('node'), may hold values from 0 to 15, as said below
- group_ids: int32 [1024, 4], P('node'), may hold values from 0 to 7, as said below
- expert_slot: int32 [1024, 6], P('node'), may hold values from 0 to 63, as said below
- gate_weight: bfloat16 [1024, 6], P('node'), may hold values from 0.099609375 to 1
- w_gate: bfloat16 [16, 7168, 1024], P('node', 'local'), may hold values from -0.0625 to 0.0625
- w_up: bfloat16 [16, 7168, 1024], P('node', 'local'), may hold values from -0.0625 to 0.0625
- w_down: bfloat16 [16, 1024, 7168], P('node', None, 'local'), may hold values from -0.1875 to 0.1875
Outputs:
- grad_input: bfloat16 [1024, 7168], P('node', 'local')
- grad_gate: bfloat16 [1024, 6], P('node')
- grad_w_gate: bfloat16 [16, 7168, 1024], P('node', 'local')
- grad_w_up: bfloat16 [16, 7168, 1024], P('node', 'local')
- grad_w_down: bfloat16 [16, 1024, 7168], P('node', None, 'local')
Inputs may be any that keep to these rules, and one draw needn't show every extreme that they name: `expert_ids`: each row names 6 different experts; expert e sits on node e // 2. A row names both experts of two of its nodes and one expert of each of the other two, and only experts on the nodes that group_ids names in the same row. `group_ids`: the 4 nodes of a row differ. In each aligned block of 128 rows every node is named by exactly 64 rows. `expert_slot`: within each aligned block of 128 rows, the entries that name one expert carry the slots 0, 1, 2, ... in row order; some experts fill all 64 slots in every block.
All inputs are finite; a program needn't handle non-finite values.
Results may differ from a plain program's by a relative error of at most 0.008.
Values may be sent and summed in bfloat16 or wider, within the bound.
No kernel may reach another device: no remote copies, remote signals or barrier semaphores. Data moves between devices by JAX's collectives and lax.ppermute only.
A program may use at most 192 MiB of HBM per device.

v0:
```python
import jax
import jax.numpy as jnp
from jax import lax
from jax.sharding import PartitionSpec as P


def contract_rows(operand_left, operand_right):
    return lax.dot_general(
        operand_left, operand_right, (((0,), (0,)), ((), ())), preferred_element_type=jnp.float32
    )


def contract_last(operand_left, operand_right):
    return lax.dot_general(
        operand_left, operand_right, (((1,), (1,)), ((), ())), preferred_element_type=jnp.float32
    )


def project(rows_in, rows_grad, gate_mat, up_mat, down_mat):
    return jnp.concatenate(
        [
            jnp.dot(rows_in, gate_mat, preferred_element_type=jnp.float32),
            jnp.dot(rows_in, up_mat, preferred_element_type=jnp.float32),
            contract_last(rows_grad, down_mat),
        ],
        axis=1,
    )


def activation(summed, rows_gate):
    width_hidden = summed.shape[1] // 3
    pre_gate = summed[:, :width_hidden]
    pre_up = summed[:, width_hidden : 2 * width_hidden]
    back_proj = summed[:, 2 * width_hidden :]
    gate_scale = rows_gate.astype(jnp.float32)[:, None]
    sigmoid_gate = jax.nn.sigmoid(pre_gate)
    silu_gate = pre_gate * sigmoid_gate
    hidden = (silu_gate * pre_up).astype(jnp.bfloat16)
    grad_hidden = gate_scale * back_proj
    grad_gate_pre = (
        grad_hidden * pre_up * sigmoid_gate * (1.0 + pre_gate * (1.0 - sigmoid_gate))
    ).astype(jnp.bfloat16)
    grad_up_pre = (grad_hidden * silu_gate).astype(jnp.bfloat16)
    gate_term = jnp.sum(hidden.astype(jnp.float32) * back_proj, axis=1).astype(jnp.bfloat16)
    return (hidden, grad_gate_pre, grad_up_pre, gate_term)


def scale_rows(rows_grad, rows_gate):
    return (rows_gate.astype(jnp.float32)[:, None] * rows_grad.astype(jnp.float32)).astype(
        jnp.bfloat16
    )


def full_expert(summed, rows_in, rows_grad, rows_gate, gate_mat, up_mat):
    hidden, grad_gate_pre, grad_up_pre, gate_term = activation(summed, rows_gate)
    scaled_grad = scale_rows(rows_grad, rows_gate)
    input_part = contract_last(grad_gate_pre, gate_mat) + contract_last(grad_up_pre, up_mat)
    return (
        contract_rows(rows_in, grad_gate_pre),
        contract_rows(rows_in, grad_up_pre),
        contract_rows(hidden, scaled_grad),
        input_part,
        gate_term,
    )


def local(
    hidden_in, out_grad, expert_ids, group_ids, expert_slot, gate_weight, w_gate, w_up, w_down
):
    node_count = lax.axis_size("node")
    tok_rows, width_part = hidden_in.shape
    experts_here = w_gate.shape[0]
    capacity = 4 * tok_rows // node_count
    row_total = node_count * capacity
    node_of = expert_ids // experts_here
    within = expert_ids % experts_here
    token_index = jnp.arange(tok_rows, dtype=jnp.int32)
    padded_in = jnp.concatenate([hidden_in, jnp.zeros((1, width_part), jnp.bfloat16)], axis=0)
    padded_grad = jnp.concatenate([out_grad, jnp.zeros((1, width_part), jnp.bfloat16)], axis=0)
    expert_flat = (expert_ids * capacity + expert_slot).reshape(-1)
    send_gate = (
        jnp.zeros((node_count * experts_here * capacity,), jnp.bfloat16)
        .at[expert_flat]
        .set(gate_weight.reshape(-1))
    )
    send_gate = send_gate.reshape(node_count, experts_here, capacity)
    node_hot = (
        group_ids[:, :, None] == jnp.arange(node_count, dtype=jnp.int32)[None, None, :]
    ).astype(jnp.int32)
    per_token = jnp.sum(node_hot, axis=1)
    before = jnp.cumsum(per_token, axis=0) - per_token
    node_slot = jnp.take_along_axis(before, group_ids, axis=1)
    node_flat = group_ids * capacity + node_slot
    sender = jnp.full((node_count * capacity,), tok_rows, jnp.int32)
    sender = sender.at[node_flat.reshape(-1)].set(
        jnp.broadcast_to(token_index[:, None], group_ids.shape).reshape(-1)
    )
    send_in = padded_in[sender].reshape(node_count, capacity, width_part)
    send_grad = padded_grad[sender].reshape(node_count, capacity, width_part)
    matches = node_of[:, None, :] == group_ids[:, :, None]
    row_pick = jnp.sum(jnp.where(matches, node_slot[:, :, None], 0), axis=1)
    row_map = jnp.full((node_count * experts_here * capacity,), capacity, jnp.int32)
    row_map = (
        row_map.at[expert_flat]
        .set(row_pick.reshape(-1))
        .reshape(node_count, experts_here, capacity)
    )
    slot_flat = ((node_of * capacity + row_pick) * experts_here + within).reshape(-1)
    slot_map = jnp.full((node_count * capacity * experts_here,), capacity, jnp.int32)
    slot_map = (
        slot_map.at[slot_flat]
        .set(expert_slot.reshape(-1))
        .reshape(node_count, capacity, experts_here)
    )
    recv_in, recv_grad, expert_gate = (
        lax.all_to_all(send_in, "node", split_axis=0, concat_axis=0, tiled=True),
        lax.all_to_all(send_grad, "node", split_axis=0, concat_axis=0, tiled=True),
        lax.all_to_all(send_gate, "node", split_axis=0, concat_axis=0, tiled=True),
    )
    recv_rows, recv_slots = (
        lax.all_to_all(row_map, "node", split_axis=0, concat_axis=0, tiled=True),
        lax.all_to_all(slot_map, "node", split_axis=0, concat_axis=0, tiled=True),
    )
    zero_row = jnp.zeros((node_count, 1, width_part), jnp.bfloat16)
    lookup = recv_rows.reshape(node_count, experts_here * capacity, 1)
    expert_in = jnp.take_along_axis(jnp.concatenate([recv_in, zero_row], axis=1), lookup, axis=1)
    expert_in = expert_in.reshape(node_count, experts_here, capacity, width_part)
    expert_grad = jnp.take_along_axis(
        jnp.concatenate([recv_grad, zero_row], axis=1), lookup, axis=1
    )
    expert_grad = expert_grad.reshape(node_count, experts_here, capacity, width_part)
    inputs_list = [
        expert_in[:, expert_index].reshape(row_total, width_part)
        for expert_index in range(experts_here)
    ]
    grads_list = [
        expert_grad[:, expert_index].reshape(row_total, width_part)
        for expert_index in range(experts_here)
    ]
    gates_list = [
        expert_gate[:, expert_index].reshape(row_total) for expert_index in range(experts_here)
    ]
    partials = jnp.stack(
        [
            project(
                inputs_list[expert_index],
                grads_list[expert_index],
                w_gate[expert_index],
                w_up[expert_index],
                w_down[expert_index],
            )
            for expert_index in range(experts_here)
        ]
    )
    summed_all = lax.psum(partials, "local")
    outcomes = [
        full_expert(
            summed_all[expert_index],
            inputs_list[expert_index],
            grads_list[expert_index],
            gates_list[expert_index],
            w_gate[expert_index],
            w_up[expert_index],
        )
        for expert_index in range(experts_here)
    ]
    grad_w_gate = jnp.stack([outcome[0] for outcome in outcomes]).astype(jnp.bfloat16)
    grad_w_up = jnp.stack([outcome[1] for outcome in outcomes]).astype(jnp.bfloat16)
    grad_w_down = jnp.stack([outcome[2] for outcome in outcomes]).astype(jnp.bfloat16)
    dx_exp = jnp.stack(
        [outcome[3].reshape(node_count, capacity, width_part) for outcome in outcomes], axis=1
    )
    dg_exp = jnp.stack([outcome[4].reshape(node_count, capacity) for outcome in outcomes], axis=1)
    padded_dx = jnp.concatenate(
        [dx_exp, jnp.zeros((node_count, experts_here, 1, width_part), jnp.float32)], axis=2
    )
    node_sum = jnp.zeros((node_count, capacity, width_part), jnp.float32)
    for expert_index in range(experts_here):
        node_sum = node_sum + jnp.take_along_axis(
            padded_dx[:, expert_index], recv_slots[:, :, expert_index][:, :, None], axis=1
        )
    back_rows, back_gate = (
        lax.all_to_all(
            node_sum.astype(jnp.bfloat16), "node", split_axis=0, concat_axis=0, tiled=True
        ),
        lax.all_to_all(dg_exp, "node", split_axis=0, concat_axis=0, tiled=True),
    )
    picked = back_rows.reshape(node_count * capacity, width_part)[node_flat]
    grad_input = jnp.sum(picked.astype(jnp.float32), axis=1).astype(jnp.bfloat16)
    grad_gate = back_gate.reshape(-1)[expert_flat].reshape(expert_ids.shape)
    return (grad_input, grad_gate, grad_w_gate, grad_w_up, grad_w_down)


def solution(mesh):
    return jax.shard_map(
        local,
        mesh=mesh,
        in_specs=(
            P("node", "local"),
            P("node", "local"),
            P("node", None),
            P("node", None),
            P("node", None),
            P("node", None),
            P("node", "local", None),
            P("node", "local", None),
            P("node", None, "local"),
        ),
        out_specs=(
            P("node", "local"),
            P("node", None),
            P("node", "local", None),
            P("node", "local", None),
            P("node", None, "local"),
        ),
        check_vma=False,
    )
```

profile of v0, /device:TPU:0, one launch (start us, length us, event | category | flops | bytes accessed | tf_op | source)
XLA Modules:
  0.0 584.7 jit_solution(10123435899089692351)
XLA Ops:
  9.1 3.8 gather_fusion.4
  17.8 7.3 %all-to-all-start.2 = ((s32[8,1,128]{2,1,0:T(1,128)}), s32[8,1,128]{2,1,0:T(1,128)S(1)}, u32[]{:S(2)}, u32[]{:S(2)}) async-start(s32[8,1,128]{2,1,0:T(1,128)} %reshape.362), calls=%async_computation.2 | async-start | bytes 8192 | tf_op jit(solution)/shard_map/all_to_all | solution.py:121
  31.5 5.8 all-to-all-start.1
  40.4 38.9 %all-to-all-done.1 = bf16[8,64,1792]{2,1,0:T(8,128)(2,1)S(1)} async-done(((bf16[8,64,1792]{2,1,0:T(8,128)(2,1)}), bf16[8,64,1792]{2,1,0:T(8,128)(2,1)S(1)}, u32[]{:S(2)}, u32[]{:S(2)}) %all-to-all-start.1) | async-done | bytes 1835040 | tf_op jit(solution)/shard_map/all_to_all | solution.py:116
  79.3 4.3 all-to-all-start.3
  86.2 39.7 %all-to-all-done.3 = bf16[8,64,1792]{2,1,0:T(8,128)(2,1)} async-done(((bf16[8,64,1792]{2,1,0:T(8,128)(2,1)}), bf16[8,64,1792]{2,1,0:T(8,128)(2,1)}, u32[]{:S(2)}, u32[]{:S(2)}) %all-to-all-start.3) | async-done | bytes 1835040 | tf_op jit(solution)/shard_map/all_to_all | solution.py:117
  129.8 20.2 %gather_fusion.5 = bf16[1024,1792]{1,0:T(8,128)(2,1)} fusion(bf16[8,65,1792]{2,0,1:T(8,128)(2,1)S(1)} %concatenate.22, s32[1024]{0:T(1024)S(1)} %or_bitcast_fusion), kind=kCustom, calls=%fused_computation.clone | custom fusion | bytes 7348224 | tf_op jit(solution)/shard_map/jit(take_along_axis)/gather | solution.py:126
  149.9 31.6 %gather_fusion.6 = bf16[1024,1792]{1,0:T(8,128)(2,1)} fusion(bf16[8,65,1792]{2,0,1:T(8,128)(2,1)} %concatenate.24, s32[1024]{0:T(1024)S(1)} %or_bitcast_fusion), kind=kCustom, calls=%fused_computation.2.clone | custom fusion | bytes 7348224 | tf_op jit(solution)/shard_map/jit(take_along_axis)/gather | solution.py:128
  185.6 5.6 fusion.14
  195.5 4.2 fusion.8
  208.0 8.6 %pad_maximum_fusion = f32[2,512,3072]{2,1,0:T(8,128)} fusion(f32[1,512,3072]{2,1,0:T(8,128)} %get-tuple-element.64, f32[1,512,3072]{2,1,0:T(8,128)S(1)} %get-tuple-element.63), kind=kLoop, calls=%fused_computation.13 | loop fusion | flops 3145728 | bytes 25165824 | tf_op jit(solution)/shard_map/stack | solution.py:143
  217.5 8.6 %scatter_custom_fusion = bf16[1024]{0:T(1024)(128)(2,1)S(1)} fusion(s32[768]{0:T(1024)S(1)} %fusion.51, bf16[768]{0:T(1024)(128)(2,1)S(1)} %reshape.287, bf16[]{:T(256)} %constant.45.clone.1), kind=kCustom, calls=%fused_computation.139 | custom fusion | bytes 2050 | tf_op jit(solution)/shard_map/scatter | solution.py:84
  236.5 5.0 all-to-all-start.4
  241.7 6.2 %all-to-all-done.4 = s32[8,1,128]{2,1,0:T(1,128)S(1)} async-done(((s32[8,1,128]{2,1,0:T(1,128)}), s32[8,1,128]{2,1,0:T(1,128)S(1)}, u32[]{:S(2)}, u32[]{:S(2)}) %all-to-all-start.4) | async-done | bytes 4128 | tf_op jit(solution)/shard_map/all_to_all | solution.py:122
  248.8 186.8 %all-reduce.7.cloned.1.call-done = f32[2,512,3072]{2,1,0:T(8,128)} async-done(((f32[2,512,3072]{2,1,0:T(8,128)}), f32[2,512,3072]{2,1,0:T(8,128)}) %all-reduce.7.cloned.1.call-update) | async-done | bytes 12582928 | tf_op jit(solution)/shard_map/psum | solution.py:155
  435.6 11.0 %slice_bitcast_fusion.1 = (f32[512,3072]{1,0:T(8,128)}, f32[512,3072]{1,0:T(8,128)}) fusion(f32[2,512,3072]{2,1,0:T(8,128)} %all-reduce.7.cloned.1.call-done), kind=kLoop, calls=%fused_computation.20 | loop fusion | bytes 25165824 | tf_op jit(solution)/shard_map/squeeze | solution.py:158
  446.6 3.7 multiply_reduce_fusion
  450.3 4.9 fusion.2
  464.6 4.1 fusion.37
  475.7 5.5 all-to-all-start.6
  481.2 14.1 %gather_fusion.8 = f32[512,1792]{1,0:T(8,128)} fusion(f32[8,65,1792]{2,0,1:T(8,128)} %get-tuple-element.43, s32[512]{0:T(512)S(1)} %reshape.336), kind=kCustom, calls=%fused_computation.3.clone | custom fusion | bytes 7344128 | tf_op jit(solution)/shard_map/jit(take_along_axis)/gather | solution.py:179
  495.3 15.6 %gather_fusion.7 = f32[512,1792]{1,0:T(8,128)} fusion(f32[8,65,1792]{2,0,1:T(8,128)} %get-tuple-element.42, s32[512]{0:T(512)S(1)} %reshape.332), kind=kCustom, calls=%fused_computation.1.clone | custom fusion | bytes 7344128 | tf_op jit(solution)/shard_map/jit(take_along_axis)/gather | solution.py:179
  510.9 5.1 fusion.20
  516.0 4.0 fusion.24
  519.9 6.5 %all-to-all-start.5 = ((bf16[8,64,1792]{2,1,0:T(8,128)(2,1)}), bf16[8,64,1792]{2,1,0:T(8,128)(2,1)S(1)}, u32[]{:S(2)}, u32[]{:S(2)}) async-start(bf16[8,64,1792]{2,1,0:T(8,128)(2,1)} %fusion.20), calls=%async_computation.5 | async-start | bytes 3670016 | tf_op jit(solution)/shard_map/all_to_all | solution.py:183
  526.4 4.0 fusion.23
  530.5 3.7 pad_maximum_fusion.1
  534.2 4.0 fusion.26
  540.3 3.7 pad_maximum_fusion.2
  544.0 3.9 fusion.28
  553.9 5.1 gather_fusion.3
  559.9 8.3 %all-to-all-done.5 = bf16[8,64,1792]{2,1,0:T(8,128)(2,1)S(1)} async-done(((bf16[8,64,1792]{2,1,0:T(8,128)(2,1)}), bf16[8,64,1792]{2,1,0:T(8,128)(2,1)S(1)}, u32[]{:S(2)}, u32[]{:S(2)}) %all-to-all-start.5) | async-done | bytes 1835040 | tf_op jit(solution)/shard_map/all_to_all | solution.py:183
  (176 shorter events, 85.9 us)
Async XLA Ops:
  9.1 4.0 copy-start.17
  9.1 4.0 copy-start.19
  9.1 4.2 copy-start.18
  9.1 18.8 %copy-start.15 = (bf16[128,1792]{1,0:T(8,128)(2,1)S(1)}, bf16[128,1792]{1,0:T(8,128)(2,1)}, u32[]{:S(2)}) copy-start(bf16[128,1792]{1,0:T(8,128)(2,1)} %param.13) | copy-start | bytes 1376260
  17.8 13.7 %all-to-all-start.2 = ((s32[8,1,128]{2,1,0:T(1,128)}), s32[8,1,128]{2,1,0:T(1,128)S(1)}, u32[]{:S(2)}, u32[]{:S(2)}) async-start(s32[8,1,128]{2,1,0:T(1,128)} %reshape.362), calls=%async_computation.2 | async-start | bytes 8192 | tf_op jit(solution)/shard_map/all_to_all | solution.py:121
  31.1 6.1 %copy-start.16 = (bf16[128,1792]{1,0:T(8,128)(2,1)S(1)}, bf16[128,1792]{1,0:T(8,128)(2,1)}, u32[]{:S(2)}) copy-start(bf16[128,1792]{1,0:T(8,128)(2,1)} %param.14) | copy-start | bytes 1376260
  31.5 47.8 %all-to-all-start.1 = ((bf16[8,64,1792]{2,1,0:T(8,128)(2,1)}), bf16[8,64,1792]{2,1,0:T(8,128)(2,1)S(1)}, u32[]{:S(2)}, u32[]{:S(2)}) async-start(bf16[8,64,1792]{2,1,0:T(8,128)(2,1)} %bitcast.4), calls=%async_computation.1 | async-start | bytes 3670016 | tf_op jit(solution)/shard_map/all_to_all | solution.py:116
  79.3 46.6 %all-to-all-start.3 = ((bf16[8,64,1792]{2,1,0:T(8,128)(2,1)}), bf16[8,64,1792]{2,1,0:T(8,128)(2,1)}, u32[]{:S(2)}, u32[]{:S(2)}) async-start(bf16[8,64,1792]{2,1,0:T(8,128)(2,1)} %bitcast.12), calls=%async_computation.3 | async-start | bytes 3670016 | tf_op jit(solution)/shard_map/all_to_all | solution.py:117
  83.7 351.9 %all-reduce.7.cloned.1.call-start = ((), (), s32[]{:S(2)}) async-start(), calls=%async_computation.7 | async-start | bytes 25165824 | tf_op jit(solution)/shard_map/psum | solution.py:155
  185.1 6.1 %slice-start.8 = ((s8[7340032]{0:T(1024)(128)(4,1)}), s8[4194304]{0:T(1024)(128)(4,1)S(1)}, s32[]{:S(2)}) async-start(s8[7340032]{0:T(1024)(128)(4,1)} %bitcast.148), calls=%async_computation.16 | async-start | bytes 8388608
  185.5 5.7 copy-start.3
  185.5 9.9 %copy-start.5 = (bf16[8,1,64,1792]{3,2,1,0:T(8,128)(2,1)}, bf16[8,1,64,1792]{3,2,1,0:T(8,128)(2,1)S(1)}, u32[]{:S(2)}) copy-start(bf16[8,1,64,1792]{3,2,1,0:T(8,128)(2,1)S(1)} %get-tuple-element.53) | copy-start | bytes 5505028
  185.5 5.7 slice-start.9
  185.6 7.8 %slice-start.4 = ((s8[7340032]{0:T(1024)(128)(4,1)}), s8[4194304]{0:T(1024)(128)(4,1)S(1)}, s32[]{:S(2)}) async-start(s8[7340032]{0:T(1024)(128)(4,1)} %bitcast.144), calls=%async_computation.12 | async-start | bytes 8388608
  193.3 6.8 %slice-start.2 = ((s8[7340032]{0:T(1024)(128)(4,1)}), s8[4194304]{0:T(1024)(128)(4,1)S(1)}, s32[]{:S(2)}) async-start(s8[7340032]{0:T(1024)(128)(4,1)} %bitcast.142), calls=%async_computation.10 | async-start | bytes 8388608
  195.5 4.7 slice-start.3
  226.8 9.6 %all-to-all-start = ((bf16[8,2,64]{2,1,0:T(2,128)(2,1)}), bf16[8,2,64]{2,1,0:T(2,128)(2,1)S(1)}, u32[]{:S(2)}, u32[]{:S(2)}) async-start(bf16[8,2,64]{2,1,0:T(2,128)(2,1)} %reshape.202), calls=%async_computation | async-start | bytes 8192 | tf_op jit(solution)/shard_map/all_to_all | solution.py:118
  236.5 11.4 %all-to-all-start.4 = ((s32[8,1,128]{2,1,0:T(1,128)}), s32[8,1,128]{2,1,0:T(1,128)S(1)}, u32[]{:S(2)}, u32[]{:S(2)}) async-start(s32[8,1,128]{2,1,0:T(1,128)} %reshape.364), calls=%async_computation.4 | async-start | bytes 8192 | tf_op jit(solution)/shard_map/all_to_all | solution.py:122
  446.6 8.7 %slice-start.10 = ((s8[7340032]{0:T(1024)(128)(4,1)}), s8[4194304]{0:T(1024)(128)(4,1)S(1)}, s32[]{:S(2)}) async-start(s8[7340032]{0:T(1024)(128)(4,1)} %bitcast.150), calls=%async_computation.18 | async-start | bytes 8388608
  450.3 5.0 copy-start.9
  450.3 5.0 copy-start.12
  450.3 5.0 slice-start.11
  450.3 9.3 %slice-start = ((s8[6291456]{0:T(1024)(128)(4,1)}), s8[4194304]{0:T(1024)(128)(4,1)S(1)}, s32[]{:S(2)}) async-start(s8[6291456]{0:T(1024)(128)(4,1)} %bitcast.113), calls=%async_computation.8 | async-start | bytes 8388608
  455.3 4.3 slice-start.1
  457.4 5.0 slice-start.6
  475.7 44.3 %all-to-all-start.6 = ((bf16[8,2,64]{2,1,0:T(2,128)(2,1)}), bf16[8,2,64]{2,1,0:T(2,128)(2,1)S(1)}, u32[]{:S(2)}, u32[]{:S(2)}) async-start(bf16[8,2,64]{2,1,0:T(2,128)(2,1)} %copy.129), calls=%async_computation.6 | async-start | bytes 8192 | tf_op jit(solution)/shard_map/all_to_all | solution.py:186
  510.9 5.1 copy-start.6
  510.9 5.1 copy-start.13
  519.9 48.3 %all-to-all-start.5 = ((bf16[8,64,1792]{2,1,0:T(8,128)(2,1)}), bf16[8,64,1792]{2,1,0:T(8,128)(2,1)S(1)}, u32[]{:S(2)}, u32[]{:S(2)}) async-start(bf16[8,64,1792]{2,1,0:T(8,128)(2,1)} %fusion.20), calls=%async_computation.5 | async-start | bytes 3670016 | tf_op jit(solution)/shard_map/all_to_all | solution.py:183
  526.4 4.0 copy-start
  534.2 4.0 copy-start.4
  534.2 4.0 copy-start.11
  (9 other events, 22.0 us)
Sparse Core Ops, SparseCore 0:
  216.7 218.8 all-reduce.6
where the time goes:
time: 594 us; the launch traced here: 585 us
  waiting for transfers between devices  281 us (47%)
  local copies, waits for them, and re-layouts  154 us (26%)
  matrix products  51.7 us (9%)
  other arithmetic  45.1 us (8%)
  starting transfers between devices  37.7 us (6%)
  between operations  15.1 us (3%)
    psum x1, waiting for transfers between devices, local(): summed_all = lax.psum(partials, 'local')  187 us
    all_to_all x1, waiting for transfers between devices, local(): lax.all_to_all(send_grad, 'node', split_axis=0, concat_axis=0, tiled=True)  39.7 us
    all_to_all x1, waiting for transfers between devices, local(): lax.all_to_all(send_in, 'node', split_axis=0, concat_axis=0, tiled=True)  38.9 us
    gather x1, local copies, waits for them, and re-layouts, local(): jnp.take_along_axis(jnp.concatenate([recv_grad, zero_row], axis=1), looku...  31.6 us
    gather x4, local copies, waits for them, and re-layouts, local(): jnp.take_along_axis(padded_dx[:, expert_index], recv_slots[:, :, expert_i...  29.9 us
    dot_general x6, matrix products, contract_rows(): lax.dot_general(operand_left, operand_right, (((0,), (0,)), ((), ())), pr...  20.2 us
    gather x1, local copies, waits for them, and re-layouts, local(): jnp.take_along_axis(jnp.concatenate([recv_in, zero_row], axis=1), lookup,...  20.2 us
    dot_general x6, matrix products, contract_last(): lax.dot_general(operand_left, operand_right, (((1,), (1,)), ((), ())), pr...  17.5 us
  transfers between devices with their start and end apart: 8, of which 7 were waited for; matrix products, arithmetic and copies ran while one was open for 17% of the time, Pallas kernels for 0%

commit v1 on v0

v1 whole, which is shorter than its diff:
```python
import functools

import jax
import jax.numpy as jnp
from jax import lax
from jax.experimental import pallas as pl
from jax.experimental.pallas import tpu as pltpu
from jax.sharding import PartitionSpec as P

BF = jnp.bfloat16
F32 = jnp.float32
CHUNKS = 2
VMEM = 40 * 1024 * 1024


def params(limit=VMEM):
    return pltpu.CompilerParams(vmem_limit_bytes=limit)


def cost(flops, moved):
    return pl.CostEstimate(flops=int(flops), bytes_accessed=int(moved), transcendentals=0)


def tile_of(size, want):
    tile = min(size, want)
    while size % tile:
        tile //= 2
    return tile


def dot_nn(left, right):
    return lax.dot_general(left, right, (((1,), (0,)), ((), ())), preferred_element_type=F32)


def dot_nt(left, right):
    return lax.dot_general(left, right, (((1,), (1,)), ((), ())), preferred_element_type=F32)


def proj_kernel(transposed, count, *refs):
    rows_ref, mats, own_ref, other_ref = refs[0], refs[1 : 1 + count], refs[-2], refs[-1]
    blocks, _, half, width = rows_ref.shape
    rows = rows_ref[...].reshape(blocks * 2 * half, width)
    for index, mat_ref in enumerate(mats):
        out = dot_nt(rows, mat_ref[0]) if transposed else dot_nn(rows, mat_ref[0])
        out = out.reshape(blocks, 2, half, out.shape[-1])
        own_ref[0, index] = out[:, 0].reshape(blocks * half, out.shape[-1])
        other_ref[0, index] = out[:, 1].reshape(blocks * half, out.shape[-1])


def project(rows, mats, transposed):
    blocks, _, half, width = rows.shape
    experts = mats[0].shape[0]
    hid = mats[0].shape[1] if transposed else mats[0].shape[2]
    count, kept = len(mats), blocks * half
    tile = tile_of(hid, 256)
    if transposed:
        mat_spec = pl.BlockSpec((1, tile, width), lambda e, j: (e, j, 0))
    else:
        mat_spec = pl.BlockSpec((1, width, tile), lambda e, j: (e, 0, j))
    out_spec = pl.BlockSpec((1, count, kept, tile), lambda e, j: (e, 0, 0, j))
    shape = jax.ShapeDtypeStruct((experts, count, kept, hid), F32)
    return pl.pallas_call(
        functools.partial(proj_kernel, transposed, count),
        grid=(experts, hid // tile),
        in_specs=[pl.BlockSpec(rows.shape, lambda e, j: (0, 0, 0, 0))] + [mat_spec] * count,
        out_specs=[out_spec, out_spec],
        out_shape=[shape, shape],
        compiler_params=params(),
        cost_estimate=cost(
            4 * kept * width * hid * experts * count, 2 * width * hid * experts * count
        ),
        name="project",
    )(rows, *mats)


def act_kernel(in_a, in_b, grad_a, grad_b, gate_ref, acts_ref, term_ref):
    pre_gate = in_a[0, 0].astype(F32) + in_b[0, 0].astype(F32)
    pre_up = in_a[0, 1].astype(F32) + in_b[0, 1].astype(F32)
    back = grad_a[0, 0].astype(F32) + grad_b[0, 0].astype(F32)
    scale = gate_ref[0]
    sig = jax.nn.sigmoid(pre_gate)
    silu = pre_gate * sig
    hidden = (silu * pre_up).astype(BF)
    grad_hidden = scale * back
    acts_ref[0, 0] = (grad_hidden * pre_up * sig * (1.0 + pre_gate * (1.0 - sig))).astype(BF)
    acts_ref[0, 1] = (grad_hidden * silu).astype(BF)
    acts_ref[0, 2] = hidden
    term_ref[0] = jnp.sum(hidden.astype(F32) * back, axis=1, keepdims=True)


def activate(in_a, in_b, grad_a, grad_b, gates):
    experts, _, kept, hid = in_a.shape
    tile = tile_of(kept, 64)
    two = pl.BlockSpec((1, 2, tile, hid), lambda e, r: (e, 0, r, 0))
    one = pl.BlockSpec((1, 1, tile, hid), lambda e, r: (e, 0, r, 0))
    col = pl.BlockSpec((1, tile, 1), lambda e, r: (e, r, 0))
    return pl.pallas_call(
        act_kernel,
        grid=(experts, kept // tile),
        in_specs=[two, two, one, one, col],
        out_specs=[pl.BlockSpec((1, 3, tile, hid), lambda e, r: (e, 0, r, 0)), col],
        out_shape=[
            jax.ShapeDtypeStruct((experts, 3, kept, hid), BF),
            jax.ShapeDtypeStruct((experts, kept, 1), F32),
        ],
        compiler_params=params(),
        cost_estimate=cost(30 * experts * kept * hid, 18 * experts * kept * hid),
        name="activate",
    )(in_a, in_b, grad_a, grad_b, gates)


def back_kernel(own_ref, other_ref, gate_ref, up_ref, out_ref):
    experts, _, kept, hid = own_ref.shape
    blocks, _, half, tile = out_ref.shape
    for place, acts_ref in enumerate((own_ref, other_ref)):
        total = jnp.zeros((kept, tile), F32)
        for e in range(experts):
            total = total + dot_nt(acts_ref[e, 0], gate_ref[e])
            total = total + dot_nt(acts_ref[e, 1], up_ref[e])
        out_ref[:, place] = total.astype(BF).reshape(blocks, half, tile)


def back(own, other, w_gate, w_up, blocks):
    experts, _, kept, hid = own.shape
    width = w_gate.shape[1]
    tile = tile_of(width, 256)
    acts = pl.BlockSpec((experts, 2, kept, hid), lambda j: (0, 0, 0, 0))
    mat = pl.BlockSpec((experts, tile, hid), lambda j: (0, j, 0))
    half = kept // blocks
    return pl.pallas_call(
        back_kernel,
        grid=(width // tile,),
        in_specs=[acts, acts, mat, mat],
        out_specs=pl.BlockSpec((blocks, 2, half, tile), lambda j: (0, 0, 0, j)),
        out_shape=jax.ShapeDtypeStruct((blocks, 2, half, width), BF),
        compiler_params=params(),
        cost_estimate=cost(8 * kept * width * hid * experts, 4 * width * hid * experts),
        name="back",
    )(own, other, w_gate, w_up)


def grads_kernel(chunks, *refs):
    ins, grads = refs[:chunks], refs[chunks : 2 * chunks]
    acts = refs[2 * chunks : 4 * chunks]
    gate_ref, out_gate, out_up, out_down, hidden_t = refs[4 * chunks :]
    kept = acts[0].shape[2]

    def pieces(which):
        return jnp.concatenate([ref[0, which] for ref in acts], axis=0)

    @pl.when(pl.program_id(1) == 0)
    def _():
        hidden_t[...] = pieces(2).T

    def rows_of(refs_in):
        out = []
        for ref in refs_in:
            for place in range(2):
                out.append(ref[:, place].reshape(kept, ref.shape[-1]))
        return jnp.concatenate(out, axis=0)

    rows_t = rows_of(ins).T
    out_gate[0] = dot_nn(rows_t, pieces(0)).astype(BF)
    out_up[0] = dot_nn(rows_t, pieces(1)).astype(BF)
    scaled = (gate_ref[0] * rows_of(grads).astype(F32)).astype(BF)
    out_down[0] = dot_nn(hidden_t[...], scaled).astype(BF)


def weight_grads(ins, grads, acts, gates):
    chunks = len(ins)
    blocks, _, half, width = ins[0].shape
    experts, _, kept, hid = acts[0].shape
    rows = 2 * kept * chunks
    tile = tile_of(width, 256)
    row_spec = pl.BlockSpec((blocks, 2, half, tile), lambda e, j: (0, 0, 0, j))
    act_spec = pl.BlockSpec((1, 3, kept, hid), lambda e, j: (e, 0, 0, 0))
    wide = pl.BlockSpec((1, tile, hid), lambda e, j: (e, j, 0))
    down = pl.BlockSpec((1, hid, tile), lambda e, j: (e, 0, j))
    wide_shape = jax.ShapeDtypeStruct((experts, width, hid), BF)
    return pl.pallas_call(
        functools.partial(grads_kernel, chunks),
        grid=(experts, width // tile),
        in_specs=[row_spec] * (2 * chunks)
        + [act_spec] * (2 * chunks)
        + [pl.BlockSpec((1, rows, 1), lambda e, j: (e, 0, 0))],
        out_specs=[wide, wide, down],
        out_shape=[wide_shape, wide_shape, jax.ShapeDtypeStruct((experts, hid, width), BF)],
        scratch_shapes=[pltpu.VMEM((hid, rows), BF)],
        compiler_params=params(),
        cost_estimate=cost(6 * rows * width * hid * experts, 6 * width * hid * experts),
        name="weight_grads",
    )(*ins, *grads, *acts, gates)


def local(
    hidden_in, out_grad, expert_ids, group_ids, expert_slot, gate_weight, w_gate, w_up, w_down
):
    nodes = lax.axis_size("node")
    shares = lax.axis_size("local")
    tokens, width = hidden_in.shape
    experts = w_gate.shape[0]
    capacity = 4 * tokens // nodes
    size = capacity // CHUNKS
    half = size // 2
    kept = nodes * half
    core = lax.axis_index("local") % 2

    def swap(value, step):
        return lax.ppermute(value, "local", [(i, i ^ step) for i in range(shares)])

    def spread(value):
        return lax.all_to_all(value, "node", split_axis=0, concat_axis=0, tiled=True)

    node_iota = lax.broadcasted_iota(jnp.int32, (nodes, tokens), 0)
    groups_t = group_ids.T
    member = jnp.zeros((nodes, tokens), jnp.bool_)
    for index in range(group_ids.shape[1]):
        member = member | (groups_t[index][None, :] == node_iota)
    earlier = lax.broadcasted_iota(jnp.int32, (tokens, tokens), 0) < lax.broadcasted_iota(
        jnp.int32, (tokens, tokens), 1
    )
    rank = dot_nn(member.astype(BF), earlier.astype(BF)).astype(jnp.int32)
    place = jnp.where(member, rank ^ (core * half), -1)
    hot = (
        place[:, None, :] == lax.broadcasted_iota(jnp.int32, (nodes, capacity, tokens), 1)
    ).astype(BF)
    hot_parts = [
        hot[:, index * size : (index + 1) * size].reshape(nodes * size, tokens)
        for index in range(CHUNKS)
    ]
    expert_iota = lax.broadcasted_iota(jnp.int32, (nodes * experts, tokens), 0)
    ids_t, gate_t = expert_ids.T, gate_weight.T
    table = jnp.zeros((nodes * experts, tokens), BF)
    for index in range(expert_ids.shape[1]):
        table = jnp.where(ids_t[index][None, :] == expert_iota, gate_t[index][None, :], table)
    send_gate = jnp.einsum(
        "njt,npt->njp",
        table.reshape(nodes, experts, tokens),
        hot,
        preferred_element_type=F32,
    ).astype(BF)
    recv_gate = spread(send_gate)

    def pack(values, index):
        sent = dot_nn(hot_parts[index], values).astype(BF)
        return spread(sent.reshape(nodes, size, width)).reshape(nodes, 2, half, width)

    rows_in = [pack(hidden_in, index) for index in range(CHUNKS)]
    rows_grad = [pack(out_grad, index) for index in range(CHUNKS)]
    gates = (
        recv_gate.astype(F32)
        .reshape(nodes, experts, CHUNKS, 2, half)
        .transpose(1, 2, 3, 0, 4)
        .reshape(experts, CHUNKS, 2, kept)
    )

    def summed(rows, mats, transposed):
        own, other = project(rows, mats, transposed)
        mine = (own + swap(other, 1)).astype(BF)
        step = 2
        while 2 * step < shares:
            mine = (mine.astype(F32) + swap(mine, step).astype(F32)).astype(BF)
            step *= 2
        return mine, swap(mine, step)

    sums_in = [summed(rows, (w_gate, w_up), False) for rows in rows_in]
    sums_grad = [summed(rows, (w_down,), True) for rows in rows_grad]

    acts, terms, returned = [], [], []
    for index in range(CHUNKS):
        own, term = activate(
            *sums_in[index], *sums_grad[index], gates[:, index, 0][:, :, None]
        )
        other = swap(own, 1)
        acts += [own, other]
        mine = term[:, :, 0].astype(BF)
        terms.append(jnp.stack([mine, swap(mine, 1)], axis=1))
        sent = back(own, other, w_gate, w_up, nodes)
        returned.append(spread(sent.reshape(nodes, size, width)).reshape(nodes * size, width))

    grad_w_gate, grad_w_up, grad_w_down = weight_grads(
        rows_in, rows_grad, acts, gates.reshape(experts, nodes * capacity)[:, :, None]
    )

    total = jnp.zeros((tokens, width), F32)
    for index in range(CHUNKS):
        total = total + lax.dot_general(
            hot_parts[index],
            returned[index],
            (((0,), (0,)), ((), ())),
            preferred_element_type=F32,
        )
    grad_input = total.astype(BF)

    all_terms = (
        jnp.stack(terms, axis=1)
        .reshape(experts, CHUNKS, 2, nodes, half)
        .transpose(3, 0, 1, 2, 4)
        .reshape(nodes, experts, capacity)
    )
    home = jnp.einsum("njp,npt->njt", spread(all_terms), hot, preferred_element_type=F32)
    home = home.reshape(nodes * experts, tokens)
    picked = [
        jnp.sum(jnp.where(ids_t[index][None, :] == expert_iota, home, 0.0), axis=0)
        for index in range(expert_ids.shape[1])
    ]
    grad_gate = jnp.stack(picked, axis=1).astype(BF)
    return (grad_input, grad_gate, grad_w_gate, grad_w_up, grad_w_down)


def solution(mesh):
    return jax.shard_map(
        local,
        mesh=mesh,
        in_specs=(
            P("node", "local"),
            P("node", "local"),
            P("node", None),
            P("node", None),
            P("node", None),
            P("node", None),
            P("node", "local", None),
            P("node", "local", None),
            P("node", None, "local"),
        ),
        out_specs=(
            P("node", "local"),
            P("node", None),
            P("node", "local", None),
            P("node", "local", None),
            P("node", None, "local"),
        ),
        check_vma=False,
    )
```

time: 594 us -> 288 us (0.48); the launches traced: 585 us -> 286 us
  waiting for transfers between devices: 281 us -> 101 us
  local copies, waits for them, and re-layouts: 154 us -> 34 us
  Pallas kernels: 0 us -> 82.3 us
  matrix products: 51.7 us -> 8.53 us
  other arithmetic: 45.1 us -> 6.89 us
  between operations: 15.1 us -> 1.19 us
  blocking collectives: 0 us -> 12.3 us
    psum x1 -> x0, waiting for transfers between devices: 187 us -> none  [local(): summed_all = lax.psum(partials, 'local')]
    gather x16 -> x0, local copies, waits for them, and re-layouts: 104 us -> none  [the longest x1 31.6 us: local(): jnp.take_along_axis(jnp.concatenate([recv_grad, zero_row], axis=1), looku...]
    pallas_call x0 -> x9, Pallas kernels: none -> 82.4 us  [the longest x4 28.8 us: project(): pl.pallas_call(functools.partial(proj_kernel, transposed, count), grid=(e...]
    ppermute x0 -> x12, waiting for transfers between devices: none -> 44.7 us  [swap(): return lax.ppermute(value, 'local', [(i, i ^ step) for i in range(shares)])]
    dot_general x16 -> x9, matrix products: 51.7 us -> 8.53 us  [the longest x5 5.49 us: dot_nn(): lax.dot_general(left, right, (((1,), (0,)), ((), ())), preferred_element_...]
    all_to_all x7, waiting for transfers between devices: 94.5 us -> 56.5 us  [spread(): lax.all_to_all(value, 'node', split_axis=0, concat_axis=0, tiled=True)]
    unnamed x73 -> x94, local copies, waits for them, and re-layouts: 3.28 us -> 30.7 us
    another operation x8 -> x0, other arithmetic: 23.9 us -> none  [the longest x2 12.2 us: local(): jnp.stack([project(inputs_list[expert_index], grads_list[expert_index], w...]
  transfers between devices with their start and end apart: 8 -> 19, of which waited for: 7 -> 8; matrix products, arithmetic and copies ran while one was open for 17% -> 5% of each run, Pallas kernels for 0% -> 29%
where the time goes in v1:
time: 288 us; the launch traced here: 286 us
  waiting for transfers between devices  101 us (35%)
  Pallas kernels  82.3 us (29%)
  starting transfers between devices  39.9 us (14%)
  local copies, waits for them, and re-layouts  34 us (12%)
  blocking collectives  12.3 us (4%)
  matrix products  8.53 us (3%)
  other arithmetic  6.89 us (2%)
    all_to_all x7, waiting for transfers between devices, spread(): lax.all_to_all(value, 'node', split_axis=0, concat_axis=0, tiled=True)  56.5 us
    ppermute x12, waiting for transfers between devices, swap(): return lax.ppermute(value, 'local', [(i, i ^ step) for i in range(shares)])  44.7 us
    all_to_all x7, starting transfers between devices, spread(): lax.all_to_all(value, 'node', split_axis=0, concat_axis=0, tiled=True)  34.3 us
    unnamed x94, local copies, waits for them, and re-layouts  30.7 us
    pallas_call x4, Pallas kernels, project(): pl.pallas_call(functools.partial(proj_kernel, transposed, count), grid=(e...  28.8 us
    pallas_call x2, Pallas kernels, back(): pl.pallas_call(back_kernel, grid=(width // tile,), in_specs=[acts, acts,...  26.8 us
    pallas_call x1, Pallas kernels, weight_grads(): pl.pallas_call(functools.partial(grads_kernel, chunks), grid=(experts, wi...  19.7 us
    all_to_all x1, blocking collectives, spread(): lax.all_to_all(value, 'node', split_axis=0, concat_axis=0, tiled=True)  12.3 us
  transfers between devices with their start and end apart: 19, of which 8 were waited for; matrix products, arithmetic and copies ran while one was open for 5% of the time, Pallas kernels for 29%

profile of v1, /device:TPU:0, one launch (start us, length us, event | category | flops | bytes accessed | tf_op | source)
XLA Modules:
  0.0 286.2 jit_solution(14393089964525099741)
XLA Ops:
  3.7 7.4 %all-to-all-start = ((bf16[8,32,1792]{2,1,0:T(8,128)(2,1)}), bf16[8,32,1792]{2,1,0:T(8,128)(2,1)S(1)}, u32[]{:S(2)}, u32[]{:S(2)}) async-start(bf16[8,32,1792]{2,1,0:T(8,128)(2,1)} %bitcast.6), calls=%async_computation | async-start | bytes 1835008 | tf_op jit(solution)/shard_map/all_to_all | solution.py:212
  12.4 21.7 %all-to-all-done = bf16[8,32,1792]{2,1,0:T(8,128)(2,1)S(1)} async-done(((bf16[8,32,1792]{2,1,0:T(8,128)(2,1)}), bf16[8,32,1792]{2,1,0:T(8,128)(2,1)S(1)}, u32[]{:S(2)}, u32[]{:S(2)}) %all-to-all-start) | async-done | bytes 917536 | tf_op jit(solution)/shard_map/all_to_all | solution.py:212
  34.1 3.6 %all-to-all-start.4 = ((bf16[8,32,1792]{2,1,0:T(8,128)(2,1)}), bf16[8,32,1792]{2,1,0:T(8,128)(2,1)S(1)}, u32[]{:S(2)}, u32[]{:S(2)}) async-start(bf16[8,32,1792]{2,1,0:T(8,128)(2,1)} %bitcast.109), calls=%async_computation.4 | async-start | bytes 1835008 | tf_op jit(solution)/shard_map/all_to_all | solution.py:212
  39.0 21.8 %all-to-all-done.4 = bf16[8,32,1792]{2,1,0:T(8,128)(2,1)S(1)} async-done(((bf16[8,32,1792]{2,1,0:T(8,128)(2,1)}), bf16[8,32,1792]{2,1,0:T(8,128)(2,1)S(1)}, u32[]{:S(2)}, u32[]{:S(2)}) %all-to-all-start.4) | async-done | bytes 917536 | tf_op jit(solution)/shard_map/all_to_all | solution.py:212
  60.8 3.6 %all-to-all-start.5 = ((bf16[8,32,1792]{2,1,0:T(8,128)(2,1)}), bf16[8,32,1792]{2,1,0:T(8,128)(2,1)S(1)}, u32[]{:S(2)}, u32[]{:S(2)}) async-start(bf16[8,32,1792]{2,1,0:T(8,128)(2,1)} %bitcast.108), calls=%async_computation.5 | async-start | bytes 1835008 | tf_op jit(solution)/shard_map/all_to_all | solution.py:212
  64.4 3.1 %copy-done.2 = bf16[2,1792,1024]{2,1,0:T(8,128)(2,1)S(1)} copy-done((bf16[2,1792,1024]{2,1,0:T(8,128)(2,1)S(1)}, bf16[2,1792,1024]{2,1,0:T(8,128)(2,1)}, u32[]{:S(2)}) %copy-start.2) | copy-done | bytes 7340056
  67.5 9.6 %project.6 = (f32[2,2,128,1024]{3,2,1,0:T(8,128)S(1)}, f32[2,2,128,1024]{3,2,1,0:T(8,128)}) custom-call(bf16[8,2,16,1792]{3,2,1,0:T(8,128)(2,1)S(1)} %bitcast.105, bf16[2,1792,1024]{2,1,0:T(8,128)(2,1)S(1)} %copy-done.2, bf16[2,1792,1024]{2,1,0:T(8,128)(2,1)} %up_ref.3), custom_call_target="tpu_custom_call" | custom-call | flops 3758096384 | bytes 14680064 | tf_op jit(solution)/shard_map/project/pallas_call | solution.py:62
  79.7 7.8 %all-to-all-done.5 = bf16[8,32,1792]{2,1,0:T(8,128)(2,1)S(1)} async-done(((bf16[8,32,1792]{2,1,0:T(8,128)(2,1)}), bf16[8,32,1792]{2,1,0:T(8,128)(2,1)S(1)}, u32[]{:S(2)}, u32[]{:S(2)}) %all-to-all-start.5) | async-done | bytes 917536 | tf_op jit(solution)/shard_map/all_to_all | solution.py:212
  87.5 3.6 %all-to-all-start.1 = ((bf16[8,32,1792]{2,1,0:T(8,128)(2,1)}), bf16[8,32,1792]{2,1,0:T(8,128)(2,1)S(1)}, u32[]{:S(2)}, u32[]{:S(2)}) async-start(bf16[8,32,1792]{2,1,0:T(8,128)(2,1)} %bitcast.107), calls=%async_computation.1 | async-start | bytes 1835008 | tf_op jit(solution)/shard_map/all_to_all | solution.py:212
  91.1 3.1 %copy-done.3 = bf16[2,1792,1024]{2,1,0:T(8,128)(2,1)S(1)} copy-done((bf16[2,1792,1024]{2,1,0:T(8,128)(2,1)S(1)}, bf16[2,1792,1024]{2,1,0:T(8,128)(2,1)}, u32[]{:S(2)}) %copy-start.3) | copy-done | bytes 7340056
  94.2 9.6 %project.4 = (f32[2,2,128,1024]{3,2,1,0:T(8,128)S(1)}, f32[2,2,128,1024]{3,2,1,0:T(8,128)}) custom-call(bf16[8,2,16,1792]{3,2,1,0:T(8,128)(2,1)S(1)} %bitcast.103, bf16[2,1792,1024]{2,1,0:T(8,128)(2,1)S(1)} %copy-done.3, bf16[2,1792,1024]{2,1,0:T(8,128)(2,1)} %up_ref.3), custom_call_target="tpu_custom_call" | custom-call | flops 3758096384 | bytes 14680064 | tf_op jit(solution)/shard_map/project/pallas_call | solution.py:62
  105.1 3.1 %copy-done.6 = bf16[2,1024,1792]{2,1,0:T(8,128)(2,1)S(1)} copy-done((bf16[2,1024,1792]{2,1,0:T(8,128)(2,1)S(1)}, bf16[2,1024,1792]{2,1,0:T(8,128)(2,1)}, u32[]{:S(2)}) %copy-start.6) | copy-done | bytes 7340056
  108.2 4.9 %project.7 = (f32[2,1,128,1024]{3,2,1,0:T(8,128)S(1)}, f32[2,1,128,1024]{3,2,1,0:T(8,128)}) custom-call(bf16[8,2,16,1792]{3,2,1,0:T(8,128)(2,1)S(1)} %bitcast.99, bf16[2,1024,1792]{2,1,0:T(8,128)(2,1)S(1)} %copy-done.6), custom_call_target="tpu_custom_call" | custom-call | flops 1879048192 | bytes 7340032 | tf_op jit(solution)/shard_map/project/pallas_call | solution.py:62
  113.7 1.9 add_convert_fusion.in_a
  117.2 3.1 %copy-done.7 = bf16[2,1024,1792]{2,1,0:T(8,128)(2,1)S(1)} copy-done((bf16[2,1024,1792]{2,1,0:T(8,128)(2,1)S(1)}, bf16[2,1024,1792]{2,1,0:T(8,128)(2,1)}, u32[]{:S(2)}) %copy-start.7) | copy-done | bytes 7340056
  120.3 4.8 %project.5 = (f32[2,1,128,1024]{3,2,1,0:T(8,128)S(1)}, f32[2,1,128,1024]{3,2,1,0:T(8,128)}) custom-call(bf16[8,2,16,1792]{3,2,1,0:T(8,128)(2,1)S(1)} %bitcast.101, bf16[2,1024,1792]{2,1,0:T(8,128)(2,1)S(1)} %copy-done.7), custom_call_target="tpu_custom_call" | custom-call | flops 1879048192 | bytes 7340032 | tf_op jit(solution)/shard_map/project/pallas_call | solution.py:62
  128.4 12.3 %all_to_all.40 = bf16[8,2,64]{2,1,0:T(2,128)(2,1)S(1)} all-to-all(bf16[8,2,64]{2,1,0:T(2,128)(2,1)S(1)} %convolution_convert_fusion.4), channel_id=1, replica_groups=mesh['node'=8,'local'=4] {'node'}, dimensions={0} | all-to-all | bytes 4096 | tf_op jit(solution)/shard_map/all_to_all | solution.py:212
  141.5 10.9 %collective-permute-done.8.grad_b = bf16[2,1,128,1024]{3,2,1,0:T(8,128)(2,1)} collective-permute-done((bf16[2,1,128,1024]{3,2,1,0:T(8,128)(2,1)S(1)}, bf16[2,1,128,1024]{3,2,1,0:T(8,128)(2,1)}, u32[]{:S(2)}, u32[]{:S(2)}) %collective-permute-start.8) | collective-permute-done | bytes 524320 | tf_op jit(solution)/shard_map/ppermute | solution.py:209
  152.4 4.1 %activate.3 = (bf16[2,3,128,1024]{3,2,1,0:T(8,128)(2,1)}, f32[2,128,1]{2,1,0:T(8,128)S(1)}) custom-call(bf16[2,2,128,1024]{3,2,1,0:T(8,128)(2,1)S(1)} %add_convert_fusion.in_a, bf16[2,2,128,1024]{3,2,1,0:T(8,128)(2,1)} %collective-permute-done.6.in_b, bf16[2,1,128,1024]{3,2,1,0:T(8,128)(2,1)S(1)} %add_convert_fusion.2.grad_a, ...), custom_call_target="tpu_custom_call" | custom-call | flops 7864320 | bytes 4718592 | tf_op jit(solution)/shard_map/activate/pallas_call | solution.py:97
  156.5 2.0 add_convert_fusion.1.in_a
  162.2 33.3 %collective-permute-done.3.grad_b = bf16[2,1,128,1024]{3,2,1,0:T(8,128)(2,1)} collective-permute-done((bf16[2,1,128,1024]{3,2,1,0:T(8,128)(2,1)S(1)}, bf16[2,1,128,1024]{3,2,1,0:T(8,128)(2,1)}, u32[]{:S(2)}, u32[]{:S(2)}) %collective-permute-start.3) | collective-permute-done | bytes 524320 | tf_op jit(solution)/shard_map/ppermute | solution.py:209
  195.5 2.9 %activate.2 = (bf16[2,3,128,1024]{3,2,1,0:T(8,128)(2,1)S(1)}, f32[2,128,1]{2,1,0:T(8,128)S(1)}) custom-call(bf16[2,2,128,1024]{3,2,1,0:T(8,128)(2,1)S(1)} %add_convert_fusion.1.in_a, bf16[2,2,128,1024]{3,2,1,0:T(8,128)(2,1)} %collective-permute-done.1.in_b, bf16[2,1,128,1024]{3,2,1,0:T(8,128)(2,1)S(1)} %add_convert_fusion.3.grad_a, ...), custom_call_target="tpu_custom_call" | custom-call | flops 7864320 | bytes 4718592 | tf_op jit(solution)/shard_map/activate/pallas_call | solution.py:97
  202.0 6.0 %all-to-all-start.7 = ((bf16[8,2,64]{2,1,0:T(2,128)(2,1)}), bf16[8,2,64]{2,1,0:T(2,128)(2,1)S(1)}, u32[]{:S(2)}, u32[]{:S(2)}) async-start(bf16[8,2,64]{2,1,0:T(2,128)(2,1)} %reshape.244), calls=%async_computation.7 | async-start | bytes 8192 | tf_op jit(solution)/shard_map/all_to_all | solution.py:212
  208.1 3.1 %copy-done.4 = bf16[2,1792,1024]{2,1,0:T(8,128)(2,1)S(1)} copy-done((bf16[2,1792,1024]{2,1,0:T(8,128)(2,1)S(1)}, bf16[2,1792,1024]{2,1,0:T(8,128)(2,1)}, u32[]{:S(2)}) %copy-start.4) | copy-done | bytes 7340056
  211.1 13.6 %back.3 = bf16[8,2,16,1792]{3,2,1,0:T(8,128)(2,1)} custom-call(bf16[2,3,128,1024]{3,2,1,0:T(8,128)(2,1)} %get-tuple-element.29.own_ref.refs_6_, bf16[2,3,128,1024]{3,2,1,0:T(8,128)(2,1)} %collective-permute-done.9.other_ref.refs_7_, bf16[2,1792,1024]{2,1,0:T(8,128)(2,1)S(1)} %copy-done.4, bf16[2,1792,1024]{2,1,0:T(8,128)(2,1)} %up_ref.3), custom_call_target="tpu_custom_call" | custom-call | flops 3758096384 | bytes 14680064 | tf_op jit(solution)/shard_map/back/pallas_call | solution.py:130
  224.7 6.0 %all-to-all-start.6 = ((bf16[8,32,1792]{2,1,0:T(8,128)(2,1)}), bf16[8,32,1792]{2,1,0:T(8,128)(2,1)S(1)}, u32[]{:S(2)}, u32[]{:S(2)}) async-start(bf16[8,32,1792]{2,1,0:T(8,128)(2,1)} %bitcast.34), calls=%async_computation.6 | async-start | bytes 1835008 | tf_op jit(solution)/shard_map/all_to_all | solution.py:212
  230.7 3.1 %copy-done.5 = bf16[2,1792,1024]{2,1,0:T(8,128)(2,1)S(1)} copy-done((bf16[2,1792,1024]{2,1,0:T(8,128)(2,1)S(1)}, bf16[2,1792,1024]{2,1,0:T(8,128)(2,1)}, u32[]{:S(2)}) %copy-start.5) | copy-done | bytes 7340056
  235.2 13.3 %back.2 = bf16[8,2,16,1792]{3,2,1,0:T(8,128)(2,1)} custom-call(bf16[2,3,128,1024]{3,2,1,0:T(8,128)(2,1)S(1)} %copy-done.18, bf16[2,3,128,1024]{3,2,1,0:T(8,128)(2,1)} %collective-permute-done.4.other_ref.refs_5_, bf16[2,1792,1024]{2,1,0:T(8,128)(2,1)S(1)} %copy-done.5, bf16[2,1792,1024]{2,1,0:T(8,128)(2,1)} %up_ref.3), custom_call_target="tpu_custom_call" | custom-call | flops 3758096384 | bytes 14680064 | tf_op jit(solution)/shard_map/back/pallas_call | solution.py:130
  248.5 5.2 %all-to-all-done.6 = bf16[8,32,1792]{2,1,0:T(8,128)(2,1)S(1)} async-done(((bf16[8,32,1792]{2,1,0:T(8,128)(2,1)}), bf16[8,32,1792]{2,1,0:T(8,128)(2,1)S(1)}, u32[]{:S(2)}, u32[]{:S(2)}) %all-to-all-start.6) | async-done | bytes 917536 | tf_op jit(solution)/shard_map/all_to_all | solution.py:212
  254.7 4.2 %all-to-all-start.3 = ((bf16[8,32,1792]{2,1,0:T(8,128)(2,1)}), bf16[8,32,1792]{2,1,0:T(8,128)(2,1)}, u32[]{:S(2)}, u32[]{:S(2)}) async-start(bf16[8,32,1792]{2,1,0:T(8,128)(2,1)} %bitcast.26), calls=%async_computation.3 | async-start | bytes 1835008 | tf_op jit(solution)/shard_map/all_to_all | solution.py:212
  263.8 19.7 %weight_grads.1 = (bf16[2,1792,1024]{2,1,0:T(8,128)(2,1)}, bf16[2,1792,1024]{2,1,0:T(8,128)(2,1)}, bf16[2,1024,1792]{2,1,0:T(8,128)(2,1)}) custom-call(bf16[8,2,16,1792]{3,2,1,0:T(8,128)(2,1)S(1)} %bitcast.104, bf16[8,2,16,1792]{3,2,1,0:T(8,128)(2,1)S(1)} %bitcast.106, bf16[8,2,16,1792]{3,2,1,0:T(8,128)(2,1)S(1)} %bitcast.102, ...), custom_call_target="tpu_custom_call" | custom-call | flops 11274289152 | bytes 22020096 | tf_op jit(solution)/shard_map/weight_grads/pallas_call | solution.py:180
  283.9 2.3 fusion.1
  (146 shorter events, 30.8 us)
Async XLA Ops:
  3.7 34.0 %copy-start.28 = (bf16[128,1792]{1,0:T(8,128)(2,1)S(1)}, bf16[128,1792]{1,0:T(8,128)(2,1)}, u32[]{:S(2)}) copy-start(bf16[128,1792]{1,0:T(8,128)(2,1)} %param.10) | copy-start | bytes 1376260
  3.7 30.4 %all-to-all-start = ((bf16[8,32,1792]{2,1,0:T(8,128)(2,1)}), bf16[8,32,1792]{2,1,0:T(8,128)(2,1)S(1)}, u32[]{:S(2)}, u32[]{:S(2)}) async-start(bf16[8,32,1792]{2,1,0:T(8,128)(2,1)} %bitcast.6), calls=%async_computation | async-start | bytes 1835008 | tf_op jit(solution)/shard_map/all_to_all | solution.py:212
  34.1 26.7 %copy-start.8 = (bf16[8,32,1792]{2,1,0:T(8,128)(2,1)}, bf16[8,32,1792]{2,1,0:T(8,128)(2,1)S(1)}, u32[]{:S(2)}) copy-start(bf16[8,32,1792]{2,1,0:T(8,128)(2,1)S(1)} %all-to-all-done) | copy-start | bytes 2752516
  34.1 26.7 %all-to-all-start.4 = ((bf16[8,32,1792]{2,1,0:T(8,128)(2,1)}), bf16[8,32,1792]{2,1,0:T(8,128)(2,1)S(1)}, u32[]{:S(2)}, u32[]{:S(2)}) async-start(bf16[8,32,1792]{2,1,0:T(8,128)(2,1)} %bitcast.109), calls=%async_computation.4 | async-start | bytes 1835008 | tf_op jit(solution)/shard_map/all_to_all | solution.py:212
  60.8 16.2 %copy-start.11 = (bf16[8,32,1792]{2,1,0:T(8,128)(2,1)}, bf16[8,32,1792]{2,1,0:T(8,128)(2,1)S(1)}, u32[]{:S(2)}) copy-start(bf16[8,32,1792]{2,1,0:T(8,128)(2,1)S(1)} %all-to-all-done.4) | copy-start | bytes 2752516
  60.8 26.7 %all-to-all-start.5 = ((bf16[8,32,1792]{2,1,0:T(8,128)(2,1)}), bf16[8,32,1792]{2,1,0:T(8,128)(2,1)S(1)}, u32[]{:S(2)}, u32[]{:S(2)}) async-start(bf16[8,32,1792]{2,1,0:T(8,128)(2,1)} %bitcast.108), calls=%async_computation.5 | async-start | bytes 1835008 | tf_op jit(solution)/shard_map/all_to_all | solution.py:212
  78.3 35.3 %collective-permute-start.5 = (f32[2,2,128,1024]{3,2,1,0:T(8,128)}, f32[2,2,128,1024]{3,2,1,0:T(8,128)}, u32[]{:S(2)}, u32[]{:S(2)}) collective-permute-start(f32[2,2,128,1024]{3,2,1,0:T(8,128)} %get-tuple-element.26), channel_id=1, source_target_pairs={{0,1},{1,0},{2,3},{3,2},{4,5},{5,4},{6,7},{7,6},{8,9},{9,8},{10,11... | collective-permute-start | bytes 6291464 | tf_op jit(solution)/shard_map/ppermute | solution.py:209
  87.5 29.7 %all-to-all-start.1 = ((bf16[8,32,1792]{2,1,0:T(8,128)(2,1)}), bf16[8,32,1792]{2,1,0:T(8,128)(2,1)S(1)}, u32[]{:S(2)}, u32[]{:S(2)}) async-start(bf16[8,32,1792]{2,1,0:T(8,128)(2,1)} %bitcast.107), calls=%async_computation.1 | async-start | bytes 1835008 | tf_op jit(solution)/shard_map/all_to_all | solution.py:212
  105.1 51.4 %collective-permute-start = (f32[2,2,128,1024]{3,2,1,0:T(8,128)}, f32[2,2,128,1024]{3,2,1,0:T(8,128)}, u32[]{:S(2)}, u32[]{:S(2)}) collective-permute-start(f32[2,2,128,1024]{3,2,1,0:T(8,128)} %get-tuple-element.21), channel_id=1, source_target_pairs={{0,1},{1,0},{2,3},{3,2},{4,5},{5,4},{6,7},{7,6},{8,9},{9,8},{10,11... | collective-permute-start | bytes 6291464 | tf_op jit(solution)/shard_map/ppermute | solution.py:209
  113.1 13.0 %collective-permute-start.7 = (f32[2,1,128,1024]{3,2,1,0:T(8,128)}, f32[2,1,128,1024]{3,2,1,0:T(8,128)}, u32[]{:S(2)}, u32[]{:S(2)}) collective-permute-start(f32[2,1,128,1024]{3,2,1,0:T(8,128)} %get-tuple-element.28), channel_id=1, source_target_pairs={{0,1},{1,0},{2,3},{3,2},{4,5},{5,4},{6,7},{7,6},{8,9},{9,8},{10,11... | collective-permute-start | bytes 3145736 | tf_op jit(solution)/shard_map/ppermute | solution.py:209
  113.6 14.5 %copy-start.35 = (s32[128]{0:T(128)}, s32[128]{0:T(128)S(1)}, u32[]{:S(2)}) copy-start(s32[128]{0:T(128)S(1)} %get-tuple-element.45) | copy-start | bytes 1540
  113.6 14.5 %copy-start.37 = (s32[128]{0:T(128)}, s32[128]{0:T(128)S(1)}, u32[]{:S(2)}) copy-start(s32[128]{0:T(128)S(1)} %get-tuple-element.46) | copy-start | bytes 1540
  113.6 14.5 %copy-start.39 = (s32[128]{0:T(128)}, s32[128]{0:T(128)S(1)}, u32[]{:S(2)}) copy-start(s32[128]{0:T(128)S(1)} %get-tuple-element.47) | copy-start | bytes 1540
  113.6 14.5 %copy-start.41 = (s32[128]{0:T(128)}, s32[128]{0:T(128)S(1)}, u32[]{:S(2)}) copy-start(s32[128]{0:T(128)S(1)} %get-tuple-element.48) | copy-start | bytes 1540
  115.6 36.8 %collective-permute-start.6 = (bf16[2,2,128,1024]{3,2,1,0:T(8,128)(2,1)S(1)}, bf16[2,2,128,1024]{3,2,1,0:T(8,128)(2,1)}, u32[]{:S(2)}, u32[]{:S(2)}) collective-permute-start(bf16[2,2,128,1024]{3,2,1,0:T(8,128)(2,1)S(1)} %add_convert_fusion.in_a), channel_id=1, source_target_pairs={{0,2},{1,3},{2,0},{3,1},{4,6},{5,7},{6,4},{7,5},{8,10},{9,11},{10,... | collective-permute-start | bytes 3145736 | tf_op jit(solution)/shard_map/ppermute | solution.py:209
  126.1 34.0 %collective-permute-start.2 = (f32[2,1,128,1024]{3,2,1,0:T(8,128)}, f32[2,1,128,1024]{3,2,1,0:T(8,128)}, u32[]{:S(2)}, u32[]{:S(2)}) collective-permute-start(f32[2,1,128,1024]{3,2,1,0:T(8,128)} %get-tuple-element.23), channel_id=1, source_target_pairs={{0,1},{1,0},{2,3},{3,2},{4,5},{5,4},{6,7},{7,6},{8,9},{9,8},{10,11... | collective-permute-start | bytes 3145736 | tf_op jit(solution)/shard_map/ppermute | solution.py:209
  127.5 24.9 %collective-permute-start.8 = (bf16[2,1,128,1024]{3,2,1,0:T(8,128)(2,1)S(1)}, bf16[2,1,128,1024]{3,2,1,0:T(8,128)(2,1)}, u32[]{:S(2)}, u32[]{:S(2)}) collective-permute-start(bf16[2,1,128,1024]{3,2,1,0:T(8,128)(2,1)S(1)} %add_convert_fusion.2.grad_a), channel_id=1, source_target_pairs={{0,2},{1,3},{2,0},{3,1},{4,6},{5,7},{6,4},{7,5},{8,10},{9,11},{10,... | collective-permute-start | bytes 1572872 | tf_op jit(solution)/shard_map/ppermute | solution.py:209
  141.5 15.0 %copy-start.14 = (f32[2,2,128,1024]{3,2,1,0:T(8,128)S(1)}, f32[2,2,128,1024]{3,2,1,0:T(8,128)}, u32[]{:S(2)}) copy-start(f32[2,2,128,1024]{3,2,1,0:T(8,128)} %copy-done.13) | copy-start | bytes 6291460
  156.5 51.6 %collective-permute-start.9 = (bf16[2,3,128,1024]{3,2,1,0:T(8,128)(2,1)}, bf16[2,3,128,1024]{3,2,1,0:T(8,128)(2,1)}, u32[]{:S(2)}, u32[]{:S(2)}) collective-permute-start(bf16[2,3,128,1024]{3,2,1,0:T(8,128)(2,1)} %get-tuple-element.29.own_ref.refs_6_), channel_id=1, source_target_pairs={{0,1},{1,0},{2,3},{3,2},{4,5},{5,4},{6,7},{7,6},{8,9},{9,8},{10,11... | collective-permute-start | bytes 4718600 | tf_op jit(solution)/shard_map/ppermute | solution.py:209
  158.5 37.0 %collective-permute-start.1 = (bf16[2,2,128,1024]{3,2,1,0:T(8,128)(2,1)S(1)}, bf16[2,2,128,1024]{3,2,1,0:T(8,128)(2,1)}, u32[]{:S(2)}, u32[]{:S(2)}) collective-permute-start(bf16[2,2,128,1024]{3,2,1,0:T(8,128)(2,1)S(1)} %add_convert_fusion.1.in_a), channel_id=1, source_target_pairs={{0,2},{1,3},{2,0},{3,1},{4,6},{5,7},{6,4},{7,5},{8,10},{9,11},{10,... | collective-permute-start | bytes 3145736 | tf_op jit(solution)/shard_map/ppermute | solution.py:209
  161.4 34.0 %collective-permute-start.3 = (bf16[2,1,128,1024]{3,2,1,0:T(8,128)(2,1)S(1)}, bf16[2,1,128,1024]{3,2,1,0:T(8,128)(2,1)}, u32[]{:S(2)}, u32[]{:S(2)}) collective-permute-start(bf16[2,1,128,1024]{3,2,1,0:T(8,128)(2,1)S(1)} %add_convert_fusion.3.grad_a), channel_id=1, source_target_pairs={{0,2},{1,3},{2,0},{3,1},{4,6},{5,7},{6,4},{7,5},{8,10},{9,11},{10,... | collective-permute-start | bytes 1572872 | tf_op jit(solution)/shard_map/ppermute | solution.py:209
  162.2 37.6 %copy-start.25 = (f32[2,128,1]{2,1,0:T(8,128)S(1)}, f32[2,128,1]{2,1,0:T(8,128)}, u32[]{:S(2)}) copy-start(f32[2,128,1]{2,1,0:T(8,128)} %copy-done.24) | copy-start | bytes 3076
  199.7 1.2 collective-permute-start.10
  199.9 1.4 collective-permute-start.11
  200.6 30.1 %collective-permute-start.4 = (bf16[2,3,128,1024]{3,2,1,0:T(8,128)(2,1)}, bf16[2,3,128,1024]{3,2,1,0:T(8,128)(2,1)}, u32[]{:S(2)}, u32[]{:S(2)}) collective-permute-start(bf16[2,3,128,1024]{3,2,1,0:T(8,128)(2,1)} %copy-done.17), channel_id=1, source_target_pairs={{0,1},{1,0},{2,3},{3,2},{4,5},{5,4},{6,7},{7,6},{8,9},{9,8},{10,11... | collective-permute-start | bytes 4718600 | tf_op jit(solution)/shard_map/ppermute | solution.py:209
  202.0 22.6 %all-to-all-start.7 = ((bf16[8,2,64]{2,1,0:T(2,128)(2,1)}), bf16[8,2,64]{2,1,0:T(2,128)(2,1)S(1)}, u32[]{:S(2)}, u32[]{:S(2)}) async-start(bf16[8,2,64]{2,1,0:T(2,128)(2,1)} %reshape.244), calls=%async_computation.7 | async-start | bytes 8192 | tf_op jit(solution)/shard_map/all_to_all | solution.py:212
  224.7 29.0 %all-to-all-start.6 = ((bf16[8,32,1792]{2,1,0:T(8,128)(2,1)}), bf16[8,32,1792]{2,1,0:T(8,128)(2,1)S(1)}, u32[]{:S(2)}, u32[]{:S(2)}) async-start(bf16[8,32,1792]{2,1,0:T(8,128)(2,1)} %bitcast.34), calls=%async_computation.6 | async-start | bytes 1835008 | tf_op jit(solution)/shard_map/all_to_all | solution.py:212
  235.2 23.7 %copy-start.32 = (f32[8,2,2,2,16]{4,0,3,2,1:T(8,128)S(1)}, f32[8,2,2,2,16]{4,0,3,2,1:T(8,128)}, u32[]{:S(2)}) copy-start(f32[8,2,2,2,16]{4,0,3,2,1:T(8,128)} %copy-done.31) | copy-start | bytes 12292
  254.7 29.2 %all-to-all-start.3 = ((bf16[8,32,1792]{2,1,0:T(8,128)(2,1)}), bf16[8,32,1792]{2,1,0:T(8,128)(2,1)}, u32[]{:S(2)}, u32[]{:S(2)}) async-start(bf16[8,32,1792]{2,1,0:T(8,128)(2,1)} %bitcast.26), calls=%async_computation.3 | async-start | bytes 1835008 | tf_op jit(solution)/shard_map/all_to_all | solution.py:212
  263.8 19.7 %copy-start.27 = (bf16[8,32,1792]{2,1,0:T(8,128)(2,1)S(1)}, bf16[8,32,1792]{2,1,0:T(8,128)(2,1)}, u32[]{:S(2)}) copy-start(bf16[8,32,1792]{2,1,0:T(8,128)(2,1)} %copy-done.26) | copy-start | bytes 2752516
  263.8 19.7 %copy-start.30 = (pred[8,64,128]{2,1,0:T(32,128)(4,1)S(1)}, pred[8,64,128]{2,1,0:T(32,128)(4,1)}, u32[]{:S(2)}) copy-start(pred[8,64,128]{2,1,0:T(32,128)(4,1)} %copy-done.29) | copy-start | bytes 196612
  263.8 22.4 %copy-start.1 = (bf16[128,1792]{1,0:T(8,128)(2,1)S(1)}, bf16[128,1792]{1,0:T(8,128)(2,1)}, u32[]{:S(2)}) copy-start(bf16[128,1792]{1,0:T(8,128)(2,1)} %param.9) | copy-start | bytes 1376260
  (34 other events, 167.2 us)

commit v2 on v0

v2 whole, which is shorter than its diff:
```python
import functools

import jax
import jax.numpy as jnp
from jax import lax
from jax.experimental import pallas as pl
from jax.experimental.pallas import tpu as pltpu
from jax.sharding import PartitionSpec as P

BF = jnp.bfloat16
F32 = jnp.float32
MIB = 1024 * 1024
LANES = 128
IN_VMEM = pl.BlockSpec(memory_space=pltpu.VMEM)
IN_SMEM = pl.BlockSpec(memory_space=pltpu.SMEM)
IN_HBM = pl.BlockSpec(memory_space=pltpu.HBM)
ANYWHERE = pl.BlockSpec(memory_space=pl.ANY)
MARK = pl.CostEstimate(flops=4000000000, bytes_accessed=1024, transcendentals=0)
CHEAP = pl.CostEstimate(flops=1024, bytes_accessed=1024, transcendentals=0)


def params(mib):
    return pltpu.CompilerParams(vmem_limit_bytes=mib * MIB)


def call(kernel, deps, operands, in_specs, **settings):
    count, extra = len(operands), len(deps)

    def body(*refs):
        kernel(*refs[:count], *refs[count + extra :])

    return pl.pallas_call(body, in_specs=list(in_specs) + [ANYWHERE] * extra, **settings)(
        *operands, *deps
    )


def tile_of(size, want):
    tile = min(size, want)
    while size % tile:
        tile //= 2
    return tile


def dot_nn(left, right):
    return lax.dot_general(left, right, (((1,), (0,)), ((), ())), preferred_element_type=F32)


def dot_nt(left, right):
    return lax.dot_general(left, right, (((1,), (1,)), ((), ())), preferred_element_type=F32)


def resident(array):
    return pltpu.with_memory_space_constraint(array, pltpu.VMEM)


def remote(array):
    return pltpu.with_memory_space_constraint(array, pltpu.HBM)


def fetch(pairs, sems):
    copies = [pltpu.make_async_copy(src, dst, sems.at[i]) for i, (src, dst) in enumerate(pairs)]
    for copy in copies:
        copy.start()
    for copy in copies:
        copy.wait()


def join(pieces):
    return pieces[0] if len(pieces) == 1 else jnp.concatenate(pieces, axis=0)


def load_kernel(count, *refs):
    fetch(list(zip(refs[:count], refs[count : 2 * count])), refs[2 * count])


def load(mats, deps):
    count = len(mats)
    return call(
        functools.partial(load_kernel, count),
        deps,
        [remote(mat) for mat in mats],
        [IN_HBM] * count,
        out_specs=[IN_VMEM] * count,
        out_shape=[pltpu.VMEM(mat.shape, mat.dtype) for mat in mats],
        scratch_shapes=[pltpu.SemaphoreType.DMA((count,))],
        compiler_params=params(1),
        cost_estimate=CHEAP,
        name="load",
    )


def hot_block(place_ref, index, size):
    tokens = place_ref.shape[1]
    row = lax.broadcasted_iota(jnp.int32, (size, tokens), 0)
    return jnp.where(place_ref[index : index + 1, :] == row, 1.0, 0.0).astype(BF)


def route_kernel(where_ref, groups_ref, ids_ref, gates_ref, place_ref, table_ref):
    me, flip = where_ref[0], where_ref[1]
    tokens = place_ref.shape[1]
    peers = me ^ lax.broadcasted_iota(jnp.int32, place_ref.shape, 0)
    member = jnp.zeros(place_ref.shape, F32)
    for index in range(groups_ref.shape[0]):
        member = jnp.where(groups_ref[index : index + 1, :] == peers, 1.0, member)
    earlier = jnp.where(
        lax.broadcasted_iota(jnp.int32, (tokens, tokens), 0)
        < lax.broadcasted_iota(jnp.int32, (tokens, tokens), 1),
        1.0,
        0.0,
    ).astype(BF)
    rank = dot_nn(member.astype(BF), earlier).astype(jnp.int32)
    place_ref[...] = jnp.where(member > 0.0, rank ^ flip, -1)
    expert = lax.broadcasted_iota(jnp.int32, (LANES, tokens), 0)
    table = jnp.zeros((LANES, tokens), F32)
    for index in range(ids_ref.shape[0]):
        gate = gates_ref[index : index + 1, :].astype(F32)
        table = jnp.where(ids_ref[index : index + 1, :] == expert, gate, table)
    table_ref[...] = table.astype(BF)


def route(where, groups_t, ids_t, gates_t, nodes):
    tokens = ids_t.shape[1]
    return pl.pallas_call(
        route_kernel,
        in_specs=[IN_SMEM] + [IN_VMEM] * 3,
        out_specs=[IN_VMEM] * 2,
        out_shape=[
            jax.ShapeDtypeStruct((nodes, tokens), jnp.int32),
            jax.ShapeDtypeStruct((LANES, tokens), BF),
        ],
        compiler_params=params(4),
        cost_estimate=CHEAP,
        name="route",
    )(where, groups_t, ids_t, gates_t)


def pack_kernel(masks, place_ref, in_ref, grad_ref, table_ref, *outs):
    width = in_ref.shape[1]
    for mask, out in zip(masks, outs):
        hot = hot_block(place_ref, mask, out.shape[0])
        out[:, :width] = dot_nn(hot, in_ref[...]).astype(BF)
        out[:, width : 2 * width] = dot_nn(hot, grad_ref[...]).astype(BF)
        out[:, 2 * width :] = dot_nt(hot, table_ref[...]).astype(BF)


def pack(place, hidden_in, out_grad, table, masks, size, deps):
    block = jax.ShapeDtypeStruct((size, 2 * hidden_in.shape[1] + LANES), BF)
    return call(
        functools.partial(pack_kernel, list(masks)),
        deps,
        [place, hidden_in, out_grad, table],
        [IN_VMEM] * 4,
        out_specs=[IN_VMEM] * len(masks),
        out_shape=[block] * len(masks),
        compiler_params=params(8),
        cost_estimate=CHEAP,
        name="pack",
    )


def unpack_kernel(place_ref, ids_ref, *refs):
    blocks, (grad_ref, gate_ref, rows, sems) = refs[:-4], refs[-4:]
    size = blocks[0].shape[0]
    tokens, width = grad_ref.shape
    pieces = [rows.at[index * size : (index + 1) * size] for index in range(len(blocks))]
    fetch(list(zip(blocks, pieces)), sems)
    hot = join([hot_block(place_ref, index, size) for index in range(len(blocks))])
    contract = (((0,), (0,)), ((), ()))
    grad_ref[...] = lax.dot_general(
        hot, rows[:, :width], contract, preferred_element_type=F32
    ).astype(BF)
    terms = lax.dot_general(rows[:, width:], hot, contract, preferred_element_type=F32)
    expert = lax.broadcasted_iota(jnp.int32, (LANES, tokens), 0)
    for index in range(ids_ref.shape[0]):
        chosen = jnp.where(ids_ref[index : index + 1, :] == expert, terms, 0.0)
        gate_ref[index : index + 1, :] = jnp.sum(chosen, axis=0, keepdims=True)


def unpack(place, ids_t, blocks):
    size, wide = blocks[0].shape
    count, tokens = ids_t.shape
    return pl.pallas_call(
        unpack_kernel,
        in_specs=[IN_VMEM] * 2 + [ANYWHERE] * len(blocks),
        out_specs=[IN_VMEM] * 2,
        out_shape=[
            jax.ShapeDtypeStruct((tokens, wide - LANES), BF),
            jax.ShapeDtypeStruct((count, tokens), F32),
        ],
        scratch_shapes=[
            pltpu.VMEM((size * len(blocks), wide), BF),
            pltpu.SemaphoreType.DMA((len(blocks),)),
        ],
        compiler_params=params(12),
        cost_estimate=CHEAP,
        name="unpack",
    )(place, ids_t, *blocks)


def project_kernel(blocks, *refs):
    (gate_ref, up_ref, down_ref), (own_ref, other_ref, rows_ref, sems) = refs[blocks:-4], refs[-4:]
    width = rows_ref.shape[1] // 2
    half = refs[0].shape[0] // 2
    experts, _, kept, hid = own_ref.shape
    pairs = []
    for index, block in enumerate(refs[:blocks]):
        for place in range(2):
            start = place * kept + index * half
            pairs.append(
                (
                    block.at[place * half : (place + 1) * half, : 2 * width],
                    rows_ref.at[start : start + half],
                )
            )
    fetch(pairs, sems)
    rows_in, rows_grad = rows_ref[:, :width], rows_ref[:, width:]
    tile = tile_of(hid, 512)

    def put(e, index, part, value):
        own_ref[e, index, :, part] = value[:kept]
        other_ref[e, index, :, part] = value[kept:]

    for e in range(experts):
        for start in range(0, hid, tile):
            part = slice(start, start + tile)
            put(e, 0, part, dot_nn(rows_in, gate_ref[e, :, part]))
            put(e, 1, part, dot_nn(rows_in, up_ref[e, :, part]))
            put(e, 2, part, dot_nt(rows_grad, down_ref[e, part]))


def project(blocks, w_gate, w_up, w_down, deps):
    experts, width, hid = w_gate.shape
    rows = len(blocks) * blocks[0].shape[0]
    shape = jax.ShapeDtypeStruct((experts, 3, rows // 2, hid), F32)
    return call(
        functools.partial(project_kernel, len(blocks)),
        deps,
        [*blocks, resident(w_gate), resident(w_up), resident(w_down)],
        [ANYWHERE] * len(blocks) + [IN_VMEM] * 3,
        out_specs=[IN_VMEM, IN_VMEM],
        out_shape=[shape, shape],
        scratch_shapes=[
            pltpu.VMEM((rows, 2 * width), BF),
            pltpu.SemaphoreType.DMA((2 * len(blocks),)),
        ],
        compiler_params=params(12),
        cost_estimate=CHEAP,
        name="project",
    )


def add_kernel(own_ref, other_ref, out_ref):
    experts, count, kept, _ = out_ref.shape
    for e in range(experts):
        for index in range(count):

            @pl.loop(0, kept // 16)
            def _(step):
                rows = pl.ds(pl.multiple_of(step * 16, 16), 16)
                total = own_ref[e, index, rows] + other_ref[e, index, rows]
                out_ref[e, index, rows] = total.astype(BF)


def add(own, other, deps):
    return call(
        add_kernel,
        deps,
        [own, other],
        [IN_VMEM] * 2,
        out_specs=IN_VMEM,
        out_shape=jax.ShapeDtypeStruct(own.shape, BF),
        compiler_params=params(12),
        cost_estimate=CHEAP,
        name="add",
    )


def act_kernel(blocks, where_ref, sum_a, sum_b, *refs):
    acts_ref, gates_ref, sems = refs[blocks:]
    experts, _, kept, hid = sum_a.shape
    half = refs[0].shape[0] // 2
    width = refs[0].shape[1] - LANES
    fetch(
        [
            (block.at[:half, width:], gates_ref.at[index * half : (index + 1) * half])
            for index, block in enumerate(refs[:blocks])
        ],
        sems,
    )
    tile = 16
    lane = lax.broadcasted_iota(jnp.int32, (tile, LANES), 1)
    for e in range(experts):
        mine = lane == where_ref[0] * experts + e

        @pl.loop(0, kept // tile)
        def _(step):
            rows = pl.ds(pl.multiple_of(step * tile, tile), tile)
            gates = gates_ref[rows].astype(F32)
            gate = jnp.sum(jnp.where(mine, gates, 0.0), axis=1, keepdims=True)
            pre_gate = sum_a[e, 0, rows].astype(F32) + sum_b[e, 0, rows].astype(F32)
            pre_up = sum_a[e, 1, rows].astype(F32) + sum_b[e, 1, rows].astype(F32)
            back = sum_a[e, 2, rows].astype(F32) + sum_b[e, 2, rows].astype(F32)
            sig = jax.nn.sigmoid(pre_gate)
            silu = pre_gate * sig
            hidden = silu * pre_up
            grad_hidden = gate * back
            slope = sig * (1.0 + pre_gate * (1.0 - sig))
            acts_ref[e, rows, :hid] = (grad_hidden * pre_up * slope).astype(BF)
            acts_ref[e, rows, hid : 2 * hid] = (grad_hidden * silu).astype(BF)
            acts_ref[e, rows, 2 * hid : 3 * hid] = (gate * hidden).astype(BF)
            term = jnp.sum(hidden.astype(BF).astype(F32) * back, axis=1, keepdims=True)
            acts_ref[e, rows, 3 * hid :] = jnp.where(mine, term, 0.0).astype(BF)


def activate(where, sum_a, sum_b, blocks, deps):
    experts, _, kept, hid = sum_a.shape
    return call(
        functools.partial(act_kernel, len(blocks)),
        deps,
        [where, sum_a, sum_b, *blocks],
        [IN_SMEM] + [IN_VMEM] * 2 + [ANYWHERE] * len(blocks),
        out_specs=IN_VMEM,
        out_shape=jax.ShapeDtypeStruct((experts, kept, 3 * hid + LANES), BF),
        scratch_shapes=[
            pltpu.VMEM((kept, LANES), BF),
            pltpu.SemaphoreType.DMA((len(blocks),)),
        ],
        compiler_params=params(8),
        cost_estimate=CHEAP,
        name="activate",
    )


def back_kernel(own_ref, other_ref, gate_ref, up_ref, *refs):
    outs, (acts_ref, terms_ref, sems) = refs[:-3], refs[-3:]
    experts, kept, _ = own_ref.shape
    half = outs[0].shape[0] // 2
    _, width, hid = gate_ref.shape
    pairs = []
    for place, ref in enumerate((own_ref, other_ref)):
        rows = slice(place * kept, (place + 1) * kept)
        pairs.append((ref.at[:, :, : 2 * hid], acts_ref.at[:, rows]))
        pairs.append((ref.at[:, :, 3 * hid :], terms_ref.at[:, rows]))
    fetch(pairs, sems)
    terms = terms_ref[0]
    for e in range(1, experts):
        terms = terms + terms_ref[e]

    def put(value, part):
        for index, out in enumerate(outs):
            out[:half, part] = value[index * half : (index + 1) * half]
            out[half:, part] = value[kept + index * half : kept + (index + 1) * half]

    put(terms, slice(width, width + LANES))
    tile = tile_of(width, 256)
    for start in range(0, width, tile):
        part = slice(start, start + tile)
        total = jnp.zeros((2 * kept, tile), F32)
        for e in range(experts):
            total = total + dot_nt(acts_ref[e, :, :hid], gate_ref[e, part])
            total = total + dot_nt(acts_ref[e, :, hid:], up_ref[e, part])
        put(total.astype(BF), part)


def back(own, other, w_gate, w_up, blocks, deps):
    experts, kept, _ = own.shape
    _, width, hid = w_gate.shape
    shape = jax.ShapeDtypeStruct((2 * kept // blocks, width + LANES), BF)
    return call(
        back_kernel,
        deps,
        [own, other, resident(w_gate), resident(w_up)],
        [ANYWHERE] * 2 + [IN_VMEM] * 2,
        out_specs=[IN_VMEM] * blocks,
        out_shape=[shape] * blocks,
        scratch_shapes=[
            pltpu.VMEM((experts, 2 * kept, 2 * hid), BF),
            pltpu.VMEM((experts, 2 * kept, LANES), BF),
            pltpu.SemaphoreType.DMA((4,)),
        ],
        compiler_params=params(12),
        cost_estimate=CHEAP,
        name="back",
    )


def grads_kernel(groups, *refs):
    blocks = sum(groups)
    acts = refs[2 * blocks : -6]
    out_gate, out_up, out_down, gate_acts, up_acts, hidden_t = refs[-6:]
    hid = gate_acts.shape[1]

    @pl.when(pl.program_id(1) == 0)
    def _():
        first = 0
        for ref in acts:
            rows = slice(first, first + ref.shape[1])
            gate_acts[rows] = ref[0, :, :hid]
            up_acts[rows] = ref[0, :, hid : 2 * hid]
            hidden_t[:, rows] = ref[0, :, 2 * hid : 3 * hid].T
            first += ref.shape[1]

    def rows_of(ins):
        out, first = [], 0
        for count in groups:
            group = ins[first : first + count]
            half = group[0].shape[0] // 2
            out += [ref[:half] for ref in group] + [ref[half:] for ref in group]
            first += count
        return join(out)

    rows_t = rows_of(refs[:blocks]).T
    out_gate[0] = dot_nn(rows_t, gate_acts[...]).astype(BF)
    out_up[0] = dot_nn(rows_t, up_acts[...]).astype(BF)
    out_down[0] = dot_nn(hidden_t[...], rows_of(refs[blocks : 2 * blocks])).astype(BF)


def weight_grads(blocks, acts, groups, deps):
    size, width = blocks[0].shape[0], (blocks[0].shape[1] - LANES) // 2
    experts = acts[0].shape[0]
    hid = (acts[0].shape[2] - LANES) // 3
    rows = size * len(blocks)
    tile = tile_of(width, 256)
    steps = width // tile
    in_spec = pl.BlockSpec((size, tile), lambda e, j: (0, j))
    grad_spec = pl.BlockSpec((size, tile), lambda e, j: (0, steps + j))
    act_specs = [pl.BlockSpec((1,) + act.shape[1:], lambda e, j: (e, 0, 0)) for act in acts]
    wide = pl.BlockSpec((1, tile, hid), lambda e, j: (e, j, 0))
    down = pl.BlockSpec((1, hid, tile), lambda e, j: (e, 0, j))
    wide_shape = jax.ShapeDtypeStruct((experts, width, hid), BF)
    return call(
        functools.partial(grads_kernel, groups),
        deps,
        [*blocks, *blocks, *acts],
        [in_spec] * len(blocks) + [grad_spec] * len(blocks) + act_specs,
        grid=(experts, steps),
        out_specs=[wide, wide, down],
        out_shape=[wide_shape, wide_shape, jax.ShapeDtypeStruct((experts, hid, width), BF)],
        scratch_shapes=[
            pltpu.VMEM((rows, hid), BF),
            pltpu.VMEM((rows, hid), BF),
            pltpu.VMEM((hid, rows), BF),
        ],
        compiler_params=params(32),
        cost_estimate=CHEAP,
        name="weight_grads",
    )


def mark_kernel(out_ref):
    out_ref[...] = jnp.zeros(out_ref.shape, F32)


def mark(deps):
    return call(
        mark_kernel,
        deps,
        [],
        [],
        out_specs=IN_VMEM,
        out_shape=jax.ShapeDtypeStruct((8, LANES), F32),
        compiler_params=params(1),
        cost_estimate=MARK,
        name="mark",
    )


def local(
    hidden_in, out_grad, expert_ids, group_ids, expert_slot, gate_weight, w_gate, w_up, w_down
):
    nodes = lax.axis_size("node")
    shares = lax.axis_size("local")
    capacity = 4 * hidden_in.shape[0] // nodes
    me = lax.axis_index("node")
    core = lax.axis_index("local") % 2
    where = jnp.stack([me, core * (capacity // 2)]).astype(jnp.int32)
    quarter = nodes // 4
    spans = [range(group * quarter, (group + 1) * quarter) for group in range(4)]
    own, near, mid, far = range(4)

    def swap(value, step):
        return lax.ppermute(value, "local", [(i, i ^ step) for i in range(shares)])

    def cross(value, mask):
        if mask == 0:
            return value
        return lax.ppermute(value, "node", [(i, i ^ mask) for i in range(nodes)])

    ids_t = expert_ids.T
    place, table = route(where, group_ids.T, ids_t, gate_weight.T, nodes)
    last = []

    def send_step(group, deps=()):
        blocks = pack(
            place, hidden_in, out_grad, table, spans[group], capacity, [*last, *deps]
        )
        last[:] = [blocks[0]]
        rows[group] = [cross(block, mask) for block, mask in zip(blocks, spans[group])]

    def pause(count):
        for _ in range(count):
            last[:] = [mark(last)]

    def project_step(group):
        mine, other = project(rows[group], v_gate, v_up, v_down, last)
        last[:] = [mine]
        parts[group] = mine, swap(other, 1)

    def sum_step(group):
        pause(24)
        total = add(*parts[group], last)
        last[:] = [total]
        step = 2
        while 2 * step < shares:
            total = (total.astype(F32) + swap(total, step).astype(F32)).astype(BF)
            step *= 2
        sums[group] = total, swap(total, step)

    def act_step(group):
        mine = activate(where, *sums[group], rows[group], last)
        last[:] = [mine]
        acts[group] = mine, swap(mine, 1)

    def back_step(group):
        pause(24)
        blocks = back(*acts[group], v_gate, v_up, len(spans[group]), last)
        last[:] = [blocks[0]]
        for mask, block in zip(spans[group], blocks):
            returned[mask] = cross(block, mask)

    rows, parts, sums, acts = [[None] * 4 for _ in range(4)]
    returned = [None] * nodes
    send_step(own)
    send_step(near)
    send_step(far)
    v_gate, v_up, v_down = load((w_gate, w_up, w_down), last)
    last[:] = [v_gate]
    project_step(own)
    sum_step(own)
    project_step(near)
    send_step(mid, rows[far])
    sum_step(near)
    project_step(far)
    sum_step(far)
    act_step(own)
    back_step(own)
    act_step(near)
    back_step(near)
    project_step(mid)
    sum_step(mid)
    act_step(far)
    back_step(far)
    act_step(mid)
    back_step(mid)

    grad_w_gate, grad_w_up, grad_w_down = weight_grads(
        [block for group in rows for block in group],
        [part for pair in acts for part in pair],
        [len(span) for span in spans],
        last,
    )
    grad_input, grad_gate = unpack(place, ids_t, returned)
    return (grad_input, grad_gate.T.astype(BF), grad_w_gate, grad_w_up, grad_w_down)


def solution(mesh):
    return jax.shard_map(
        local,
        mesh=mesh,
        in_specs=(
            P("node", "local"),
            P("node", "local"),
            P("node", None),
            P("node", None),
            P("node", None),
            P("node", None),
            P("node", "local", None),
            P("node", "local", None),
            P("node", None, "local"),
        ),
        out_specs=(
            P("node", "local"),
            P("node", None),
            P("node", "local", None),
            P("node", "local", None),
            P("node", None, "local"),
        ),
        check_vma=False,
    )
```

time: 594 us -> 189 us (0.32); the launches traced: 585 us -> 189 us
  waiting for transfers between devices: 281 us -> 56.5 us
  local copies, waits for them, and re-layouts: 154 us -> 4.23 us
  Pallas kernels: 0 us -> 93.3 us
  matrix products: 51.7 us -> 0 us
  other arithmetic: 45.1 us -> 0.66 us
  between operations: 15.1 us -> 2.63 us
  starting transfers between devices: 37.7 us -> 31.6 us
    psum x1 -> x0, waiting for transfers between devices: 187 us -> none  [local(): summed_all = lax.psum(partials, 'local')]
    gather x16 -> x0, local copies, waits for them, and re-layouts: 104 us -> none  [the longest x1 31.6 us: local(): jnp.take_along_axis(jnp.concatenate([recv_grad, zero_row], axis=1), looku...]
    all_to_all x7 -> x0, waiting for transfers between devices: 94.5 us -> none  [the longest x1 39.7 us: local(): lax.all_to_all(send_grad, 'node', split_axis=0, concat_axis=0, tiled=True)]
    pallas_call x0 -> x216, Pallas kernels: none -> 93.3 us  [the longest x214 89.7 us: call(): pl.pallas_call(body, in_specs=list(in_specs) + [ANYWHERE] * extra, **sett...]
    ppermute x0 -> x26, waiting for transfers between devices: none -> 56.5 us  [the longest x14 31.6 us: cross(): return lax.ppermute(value, 'node', [(i, i ^ mask) for i in range(nodes)])]
    dot_general x16 -> x0, matrix products: 51.7 us -> none  [the longest x6 20.2 us: contract_rows(): lax.dot_general(operand_left, operand_right, (((0,), (0,)), ((), ())), pr...]
    all_to_all x7 -> x0, starting transfers between devices: 37.7 us -> none  [the longest x1 7.28 us: local(): lax.all_to_all(row_map, 'node', split_axis=0, concat_axis=0, tiled=True)]
    ppermute x0 -> x26, starting transfers between devices: none -> 31.6 us  [the longest x14 26.1 us: cross(): return lax.ppermute(value, 'node', [(i, i ^ mask) for i in range(nodes)])]
  transfers between devices with their start and end apart: 8 -> 26, of which waited for: 7 -> 12; matrix products, arithmetic and copies ran while one was open for 17% -> 0% of each run, Pallas kernels for 0% -> 47%
where the time goes in v2:
time: 189 us
  Pallas kernels  93.3 us (49%)
  waiting for transfers between devices  56.5 us (30%)
  starting transfers between devices  31.6 us (17%)
  local copies, waits for them, and re-layouts  4.23 us (2%)
  between operations  2.63 us (1%)
    pallas_call x214, Pallas kernels, call(): pl.pallas_call(body, in_specs=list(in_specs) + [ANYWHERE] * extra, **sett...  89.7 us
    ppermute x14, waiting for transfers between devices, cross(): return lax.ppermute(value, 'node', [(i, i ^ mask) for i in range(nodes)])  31.6 us
    ppermute x14, starting transfers between devices, cross(): return lax.ppermute(value, 'node', [(i, i ^ mask) for i in range(nodes)])  26.1 us
    ppermute x12, waiting for transfers between devices, swap(): return lax.ppermute(value, 'local', [(i, i ^ step) for i in range(shares)])  25 us
    ppermute x12, starting transfers between devices, swap(): return lax.ppermute(value, 'local', [(i, i ^ step) for i in range(shares)])  5.46 us
    unnamed x74, local copies, waits for them, and re-layouts  4.23 us
  transfers between devices with their start and end apart: 26, of which 12 were waited for; matrix products, arithmetic and copies ran while one was open for 0% of the time, Pallas kernels for 47%

profile of v2, /device:TPU:0, one launch (start us, length us, event | category | flops | bytes accessed | tf_op | source)
XLA Modules:
  0.0 188.9 jit_solution(937468547426278454)
XLA Ops:
  6.0 3.0 %collective-permute-start = (bf16[64,3712]{1,0:T(8,128)(2,1)S(1)}, bf16[64,3712]{1,0:T(8,128)(2,1)S(1)}, u32[]{:S(2)}, u32[]{:S(2)}) collective-permute-start(bf16[64,3712]{1,0:T(8,128)(2,1)S(1)} %get-tuple-element.42), channel_id=1, source_target_pairs={{0,4},{4,0},{8,12},{12,8},{16,20},{20,16},{24,28},{28,24},{1,5},{5... | collective-permute-start | bytes 1425416 | tf_op jit(solution)/shard_map/ppermute | solution.py:487
  9.4 1.6 collective-permute-start.5
  11.5 2.5 %collective-permute-start.3 = (bf16[64,3712]{1,0:T(8,128)(2,1)S(1)}, bf16[64,3712]{1,0:T(8,128)(2,1)S(1)}, u32[]{:S(2)}, u32[]{:S(2)}) collective-permute-start(bf16[64,3712]{1,0:T(8,128)(2,1)S(1)} %get-tuple-element.44.refs_3_), channel_id=1, source_target_pairs={{0,24},{4,28},{8,16},{12,20},{16,8},{20,12},{24,0},{28,4},{1,25},{... | collective-permute-start | bytes 1425416 | tf_op jit(solution)/shard_map/ppermute | solution.py:487
  15.7 7.3 %load.1 = (bf16[2,1792,1024]{2,1,0:T(8,128)(2,1)S(1)}, bf16[2,1792,1024]{2,1,0:T(8,128)(2,1)S(1)}, bf16[2,1024,1792]{2,1,0:T(8,128)(2,1)S(1)}) custom-call(bf16[2,1792,1024]{2,1,0:T(8,128)(2,1)} %refs_0_.1, bf16[2,1792,1024]{2,1,0:T(8,128)(2,1)} %refs_1_.8, bf16[2,1024,1792]{2,1,0:T(8,128)(2,1)} %refs_2_.8, bf16[64,3712]{1,0:T(8,128)(2,1)S(1)} %get-tuple-element.44.refs_3_), custom_call_target="tpu_custom_call" | custom-call | flops 1024 | bytes 1024 | tf_op jit(solution)/shard_map/load/pallas_call | solution.py:32
  23.0 4.8 %project.4 = (f32[2,3,64,1024]{3,2,1,0:T(8,128)S(1)}, f32[2,3,64,1024]{3,2,1,0:T(8,128)S(1)}) custom-call(bf16[64,3712]{1,0:T(8,128)(2,1)S(1)} %get-tuple-element.41.refs_4_.refs_0_.refs_3_.refs_8_, bf16[64,3712]{1,0:T(8,128)(2,1)S(1)} %collective-permute-done.refs_1_.refs_4_.refs_9_, bf16[2,1792,1024]{2,1,0:T(8,128)(2,1)S(1)} %get-tuple-element.45.refs_2_.refs_5_, ...), custom_call_target="tpu_custom_call" | custom-call | flops 1024 | bytes 1024 | tf_op jit(solution)/shard_map/project/pallas_call | solution.py:32
  28.1 3.2 %collective-permute-done.1.refs_1_ = f32[2,3,64,1024]{3,2,1,0:T(8,128)S(1)} collective-permute-done((f32[2,3,64,1024]{3,2,1,0:T(8,128)S(1)}, f32[2,3,64,1024]{3,2,1,0:T(8,128)S(1)}, u32[]{:S(2)}, u32[]{:S(2)}) %collective-permute-start.1) | collective-permute-done | bytes 1572896 | tf_op jit(solution)/shard_map/ppermute | solution.py:482
  33.9 24.5 %collective-permute-done.6.refs_1_.refs_4_.refs_3_.refs_11_ = bf16[64,3712]{1,0:T(8,128)(2,1)S(1)} collective-permute-done((bf16[64,3712]{1,0:T(8,128)(2,1)S(1)}, bf16[64,3712]{1,0:T(8,128)(2,1)S(1)}, u32[]{:S(2)}, u32[]{:S(2)}) %collective-permute-start.6) | collective-permute-done | bytes 475168 | tf_op jit(solution)/shard_map/ppermute | solution.py:487
  58.4 4.7 %project.5 = (f32[2,3,64,1024]{3,2,1,0:T(8,128)S(1)}, f32[2,3,64,1024]{3,2,1,0:T(8,128)S(1)}) custom-call(bf16[64,3712]{1,0:T(8,128)(2,1)S(1)} %collective-permute-done.5.refs_0_.refs_3_.refs_2_.refs_10_, bf16[64,3712]{1,0:T(8,128)(2,1)S(1)} %collective-permute-done.6.refs_1_.refs_4_.refs_3_.refs_11_, ...), custom_call_target="tpu_custom_call" | custom-call | flops 1024 | bytes 1024 | tf_op jit(solution)/shard_map/project/pallas_call | solution.py:32
  64.4 4.7 %collective-permute-start.15 = (bf16[64,3712]{1,0:T(8,128)(2,1)}, bf16[64,3712]{1,0:T(8,128)(2,1)}, u32[]{:S(2)}, u32[]{:S(2)}) collective-permute-start(bf16[64,3712]{1,0:T(8,128)(2,1)} %get-tuple-element.54.refs_0_), channel_id=1, source_target_pairs={{0,16},{4,20},{8,24},{12,28},{16,0},{20,4},{24,8},{28,12},{1,17},{... | collective-permute-start | bytes 1425416 | tf_op jit(solution)/shard_map/ppermute | solution.py:487
  70.4 2.2 %collective-permute-done.7.refs_1_ = f32[2,3,64,1024]{3,2,1,0:T(8,128)S(1)} collective-permute-done((f32[2,3,64,1024]{3,2,1,0:T(8,128)S(1)}, f32[2,3,64,1024]{3,2,1,0:T(8,128)S(1)}, u32[]{:S(2)}, u32[]{:S(2)}) %collective-permute-start.7) | collective-permute-done | bytes 1572896 | tf_op jit(solution)/shard_map/ppermute | solution.py:482
  75.2 4.7 %project.6 = (f32[2,3,64,1024]{3,2,1,0:T(8,128)S(1)}, f32[2,3,64,1024]{3,2,1,0:T(8,128)S(1)}) custom-call(bf16[64,3712]{1,0:T(8,128)(2,1)S(1)} %collective-permute-done.3.refs_5_.refs_0_.refs_3_.refs_6_.refs_14_, bf16[64,3712]{1,0:T(8,128)(2,1)S(1)} %collective-permute-done.4.refs_6_.refs_1_.refs_4_.refs_7_.refs_15_, ...), custom_call_target="tpu_custom_call" | custom-call | flops 1024 | bytes 1024 | tf_op jit(solution)/shard_map/project/pallas_call | solution.py:32
  80.3 3.1 %collective-permute-done.8.refs_1_ = f32[2,3,64,1024]{3,2,1,0:T(8,128)S(1)} collective-permute-done((f32[2,3,64,1024]{3,2,1,0:T(8,128)S(1)}, f32[2,3,64,1024]{3,2,1,0:T(8,128)S(1)}, u32[]{:S(2)}, u32[]{:S(2)}) %collective-permute-start.8) | collective-permute-done | bytes 1572896 | tf_op jit(solution)/shard_map/ppermute | solution.py:482
  84.7 2.4 %activate.4.refs_0_.refs_16_ = bf16[2,64,3200]{2,1,0:T(8,128)(2,1)S(1)} custom-call(s32[2]{0:T(128)S(1)} %copy-done.34, bf16[2,3,64,1024]{3,2,1,0:T(8,128)(2,1)} %add.11.refs_5_.refs_1_, bf16[2,3,64,1024]{3,2,1,0:T(8,128)(2,1)} %collective-permute-done.2.refs_2_, bf16[64,3712]{1,0:T(8,128)(2,1)S(1)} %copy-done.5, bf16[64,3712]{1,0:T(8,128)(2,1)S(1)} %copy-done.13, ...), custom_call_target="tpu_custom_call" | custom-call | flops 1024 | bytes 1024 | tf_op jit(solution)/shard_map/activate/pallas_call | solution.py:32
  89.5 6.0 %back.4 = (bf16[64,1920]{1,0:T(8,128)(2,1)S(1)}, bf16[64,1920]{1,0:T(8,128)(2,1)}) custom-call(bf16[2,64,3200]{2,1,0:T(8,128)(2,1)S(1)} %activate.4.refs_0_.refs_16_, bf16[2,64,3200]{2,1,0:T(8,128)(2,1)S(1)} %collective-permute-done.9.refs_1_.refs_17_, bf16[2,1792,1024]{2,1,0:T(8,128)(2,1)S(1)} %get-tuple-element.45.refs_2_.refs_5_, ...), custom_call_target="tpu_custom_call" | custom-call | flops 1024 | bytes 1024 | tf_op jit(solution)/shard_map/back/pallas_call | solution.py:32
  95.5 2.4 %activate.5.refs_0_.refs_18_ = bf16[2,64,3200]{2,1,0:T(8,128)(2,1)S(1)} custom-call(s32[2]{0:T(128)S(1)} %copy-done.34, bf16[2,3,64,1024]{3,2,1,0:T(8,128)(2,1)} %add.12.refs_5_.refs_1_, bf16[2,3,64,1024]{3,2,1,0:T(8,128)(2,1)} %collective-permute-done.11.refs_2_, bf16[64,3712]{1,0:T(8,128)(2,1)S(1)} %copy-done.8, ...), custom_call_target="tpu_custom_call" | custom-call | flops 1024 | bytes 1024 | tf_op jit(solution)/shard_map/activate/pallas_call | solution.py:32
  98.1 1.5 collective-permute-start.10
  100.3 5.9 %back.5 = (bf16[64,1920]{1,0:T(8,128)(2,1)}, bf16[64,1920]{1,0:T(8,128)(2,1)}) custom-call(bf16[2,64,3200]{2,1,0:T(8,128)(2,1)S(1)} %activate.5.refs_0_.refs_18_, bf16[2,64,3200]{2,1,0:T(8,128)(2,1)S(1)} %collective-permute-done.12.refs_1_.refs_19_, bf16[2,1792,1024]{2,1,0:T(8,128)(2,1)S(1)} %get-tuple-element.45.refs_2_.refs_5_, ...), custom_call_target="tpu_custom_call" | custom-call | flops 1024 | bytes 1024 | tf_op jit(solution)/shard_map/back/pallas_call | solution.py:32
  106.3 2.9 %collective-permute-start.14 = (bf16[64,1920]{1,0:T(8,128)(2,1)}, bf16[64,1920]{1,0:T(8,128)(2,1)}, u32[]{:S(2)}, u32[]{:S(2)}) collective-permute-start(bf16[64,1920]{1,0:T(8,128)(2,1)} %get-tuple-element.60), channel_id=1, source_target_pairs={{0,12},{4,8},{8,4},{12,0},{16,28},{20,24},{24,20},{28,16},{1,13},{... | collective-permute-start | bytes 737288 | tf_op jit(solution)/shard_map/ppermute | solution.py:487
  109.2 5.7 %project.7 = (f32[2,3,64,1024]{3,2,1,0:T(8,128)S(1)}, f32[2,3,64,1024]{3,2,1,0:T(8,128)S(1)}) custom-call(bf16[64,3712]{1,0:T(8,128)(2,1)} %collective-permute-done.15.refs_0_.refs_3_.refs_4_.refs_12_, bf16[64,3712]{1,0:T(8,128)(2,1)} %collective-permute-done.16.refs_1_.refs_4_.refs_5_.refs_13_, ...), custom_call_target="tpu_custom_call" | custom-call | flops 1024 | bytes 1024 | tf_op jit(solution)/shard_map/project/pallas_call | solution.py:32
  115.3 3.2 %collective-permute-done.17.refs_1_ = f32[2,3,64,1024]{3,2,1,0:T(8,128)S(1)} collective-permute-done((f32[2,3,64,1024]{3,2,1,0:T(8,128)S(1)}, f32[2,3,64,1024]{3,2,1,0:T(8,128)S(1)}, u32[]{:S(2)}, u32[]{:S(2)}) %collective-permute-start.17) | collective-permute-done | bytes 1572896 | tf_op jit(solution)/shard_map/ppermute | solution.py:482
  119.9 2.4 %activate.6.refs_0_.refs_22_ = bf16[2,64,3200]{2,1,0:T(8,128)(2,1)S(1)} custom-call(s32[2]{0:T(128)S(1)} %copy-done.34, bf16[2,3,64,1024]{3,2,1,0:T(8,128)(2,1)} %add.13.refs_5_.refs_1_, bf16[2,3,64,1024]{3,2,1,0:T(8,128)(2,1)} %collective-permute-done.19.refs_2_, bf16[64,3712]{1,0:T(8,128)(2,1)S(1)} %collective-permute-done.3.refs_5_.refs_0_.refs_3_.refs_6_.refs_14_, ...), custom_call_target="tpu_custom_call" | custom-call | flops 1024 | bytes 1024 | tf_op jit(solution)/shard_map/activate/pallas_call | solution.py:32
  122.6 2.1 %collective-permute-done.20.refs_1_.refs_23_ = bf16[2,64,3200]{2,1,0:T(8,128)(2,1)S(1)} collective-permute-done((bf16[2,64,3200]{2,1,0:T(8,128)(2,1)S(1)}, bf16[2,64,3200]{2,1,0:T(8,128)(2,1)S(1)}, u32[]{:S(2)}, u32[]{:S(2)}) %collective-permute-start.20) | collective-permute-done | bytes 819232 | tf_op jit(solution)/shard_map/ppermute | solution.py:482
  124.7 5.3 %back.6 = (bf16[64,1920]{1,0:T(8,128)(2,1)S(1)}, bf16[64,1920]{1,0:T(8,128)(2,1)S(1)}) custom-call(bf16[2,64,3200]{2,1,0:T(8,128)(2,1)S(1)} %activate.6.refs_0_.refs_22_, bf16[2,64,3200]{2,1,0:T(8,128)(2,1)S(1)} %collective-permute-done.20.refs_1_.refs_23_, bf16[2,1792,1024]{2,1,0:T(8,128)(2,1)S(1)} %get-tuple-element.45.refs_2_.refs_5_, ...), custom_call_target="tpu_custom_call" | custom-call | flops 1024 | bytes 1024 | tf_op jit(solution)/shard_map/back/pallas_call | solution.py:32
  130.0 8.4 %collective-permute-done.18.refs_2_ = bf16[2,3,64,1024]{3,2,1,0:T(8,128)(2,1)S(1)} collective-permute-done((bf16[2,3,64,1024]{3,2,1,0:T(8,128)(2,1)S(1)}, bf16[2,3,64,1024]{3,2,1,0:T(8,128)(2,1)S(1)}, u32[]{:S(2)}, u32[]{:S(2)}) %collective-permute-start.18) | collective-permute-done | bytes 786464 | tf_op jit(solution)/shard_map/ppermute | solution.py:482
  138.4 2.2 %activate.7.refs_0_.refs_20_ = bf16[2,64,3200]{2,1,0:T(8,128)(2,1)S(1)} custom-call(s32[2]{0:T(128)S(1)} %copy-done.34, bf16[2,3,64,1024]{3,2,1,0:T(8,128)(2,1)S(1)} %add.14.refs_5_.refs_1_, bf16[2,3,64,1024]{3,2,1,0:T(8,128)(2,1)S(1)} %collective-permute-done.18.refs_2_, bf16[64,3712]{1,0:T(8,128)(2,1)} %collective-permute-done.15.refs_0_.refs_3_.refs_4_.refs_12_, ...), custom_call_target="tpu_custom_call" | custom-call | flops 1024 | bytes 1024 | tf_op jit(solution)/shard_map/activate/pallas_call | solution.py:32
  143.1 1.9 collective-permute-start.25
  144.9 5.1 %back.7 = (bf16[64,1920]{1,0:T(8,128)(2,1)S(1)}, bf16[64,1920]{1,0:T(8,128)(2,1)S(1)}) custom-call(bf16[2,64,3200]{2,1,0:T(8,128)(2,1)S(1)} %activate.7.refs_0_.refs_20_, bf16[2,64,3200]{2,1,0:T(8,128)(2,1)S(1)} %collective-permute-done.21.refs_1_.refs_21_, bf16[2,1792,1024]{2,1,0:T(8,128)(2,1)S(1)} %get-tuple-element.45.refs_2_.refs_5_, ...), custom_call_target="tpu_custom_call" | custom-call | flops 1024 | bytes 1024 | tf_op jit(solution)/shard_map/back/pallas_call | solution.py:32
  150.2 3.9 %collective-permute-start.23 = (bf16[64,1920]{1,0:T(8,128)(2,1)S(1)}, bf16[64,1920]{1,0:T(8,128)(2,1)S(1)}, u32[]{:S(2)}, u32[]{:S(2)}) collective-permute-start(bf16[64,1920]{1,0:T(8,128)(2,1)S(1)} %get-tuple-element.66), channel_id=1, source_target_pairs={{0,20},{4,16},{8,28},{12,24},{16,4},{20,0},{24,12},{28,8},{1,21},{... | collective-permute-start | bytes 737288 | tf_op jit(solution)/shard_map/ppermute | solution.py:487
  154.1 24.2 %weight_grads.1 = (bf16[2,1792,1024]{2,1,0:T(8,128)(2,1)}, bf16[2,1792,1024]{2,1,0:T(8,128)(2,1)}, bf16[2,1024,1792]{2,1,0:T(8,128)(2,1)}) custom-call(bf16[64,3712]{1,0:T(8,128)(2,1)S(1)} %copy-done.6, bf16[64,3712]{1,0:T(8,128)(2,1)S(1)} %copy-done.14, bf16[64,3712]{1,0:T(8,128)(2,1)S(1)} %copy-done.9, bf16[64,3712]{1,0:T(8,128)(2,1)S(1)} %copy-done.11, ...), custom_call_target="tpu_custom_call" | custom-call | flops 1024 | bytes 1024 | tf_op jit(solution)/shard_map/weight_grads/pallas_call | solution.py:32
  178.3 2.3 %collective-permute-done.22.refs_4_ = bf16[64,1920]{1,0:T(8,128)(2,1)S(1)} collective-permute-done((bf16[64,1920]{1,0:T(8,128)(2,1)S(1)}, bf16[64,1920]{1,0:T(8,128)(2,1)S(1)}, u32[]{:S(2)}, u32[]{:S(2)}) %collective-permute-start.22) | collective-permute-done | bytes 245792 | tf_op jit(solution)/shard_map/ppermute | solution.py:487
  180.6 4.8 %collective-permute-done.23.refs_5_ = bf16[64,1920]{1,0:T(8,128)(2,1)S(1)} collective-permute-done((bf16[64,1920]{1,0:T(8,128)(2,1)S(1)}, bf16[64,1920]{1,0:T(8,128)(2,1)S(1)}, u32[]{:S(2)}, u32[]{:S(2)}) %collective-permute-start.23) | collective-permute-done | bytes 245792 | tf_op jit(solution)/shard_map/ppermute | solution.py:487
  185.4 2.9 %unpack.1 = (bf16[128,1792]{1,0:T(8,128)(2,1)}, f32[6,128]{1,0:T(8,128)S(1)}) custom-call(s32[8,128]{1,0:T(8,128)S(1)} %copy-done.30, s32[6,128]{1,0:T(8,128)S(1)} %bitcast.8, bf16[64,1920]{1,0:T(8,128)(2,1)S(1)} %copy-done.28, bf16[64,1920]{1,0:T(8,128)(2,1)} %collective-permute-done.10.refs_1_, bf16[64,1920]{1,0:T(8,128)(2,1)} %collective-permute-done.13.refs_2_, ...), custom_call_target="tpu_custom_call" | custom-call | flops 1024 | bytes 1024 | tf_op jit(solution)/shard_map/unpack/pallas_call | solution.py:182
  (312 shorter events, 24.6 us)
Async XLA Ops:
  3.5 59.7 %copy-start.29 = (s32[8,128]{1,0:T(8,128)}, s32[8,128]{1,0:T(8,128)S(1)}, u32[]{:S(2)}) copy-start(s32[8,128]{1,0:T(8,128)S(1)} %get-tuple-element.39.refs_0_.place_ref) | copy-start | bytes 12292
  6.0 17.0 %collective-permute-start = (bf16[64,3712]{1,0:T(8,128)(2,1)S(1)}, bf16[64,3712]{1,0:T(8,128)(2,1)S(1)}, u32[]{:S(2)}, u32[]{:S(2)}) collective-permute-start(bf16[64,3712]{1,0:T(8,128)(2,1)S(1)} %get-tuple-element.42), channel_id=1, source_target_pairs={{0,4},{4,0},{8,12},{12,8},{16,20},{20,16},{24,28},{28,24},{1,5},{5... | collective-permute-start | bytes 1425416 | tf_op jit(solution)/shard_map/ppermute | solution.py:487
  9.4 24.5 %collective-permute-start.5 = (bf16[64,3712]{1,0:T(8,128)(2,1)S(1)}, bf16[64,3712]{1,0:T(8,128)(2,1)S(1)}, u32[]{:S(2)}, u32[]{:S(2)}) collective-permute-start(bf16[64,3712]{1,0:T(8,128)(2,1)S(1)} %get-tuple-element.43.refs_4_), channel_id=1, source_target_pairs={{0,8},{4,12},{8,0},{12,4},{16,24},{20,28},{24,16},{28,20},{1,9},{5... | collective-permute-start | bytes 1425416 | tf_op jit(solution)/shard_map/ppermute | solution.py:487
  11.5 51.6 %collective-permute-start.3 = (bf16[64,3712]{1,0:T(8,128)(2,1)S(1)}, bf16[64,3712]{1,0:T(8,128)(2,1)S(1)}, u32[]{:S(2)}, u32[]{:S(2)}) collective-permute-start(bf16[64,3712]{1,0:T(8,128)(2,1)S(1)} %get-tuple-element.44.refs_3_), channel_id=1, source_target_pairs={{0,24},{4,28},{8,16},{12,20},{16,8},{20,12},{24,0},{28,4},{1,25},{... | collective-permute-start | bytes 1425416 | tf_op jit(solution)/shard_map/ppermute | solution.py:487
  14.0 49.1 %collective-permute-start.4 = (bf16[64,3712]{1,0:T(8,128)(2,1)S(1)}, bf16[64,3712]{1,0:T(8,128)(2,1)S(1)}, u32[]{:S(2)}, u32[]{:S(2)}) collective-permute-start(bf16[64,3712]{1,0:T(8,128)(2,1)S(1)} %get-tuple-element.50), channel_id=1, source_target_pairs={{0,28},{4,24},{8,20},{12,16},{16,12},{20,8},{24,4},{28,0},{1,29},{... | collective-permute-start | bytes 1425416 | tf_op jit(solution)/shard_map/ppermute | solution.py:487
  15.3 43.0 %collective-permute-start.6 = (bf16[64,3712]{1,0:T(8,128)(2,1)S(1)}, bf16[64,3712]{1,0:T(8,128)(2,1)S(1)}, u32[]{:S(2)}, u32[]{:S(2)}) collective-permute-start(bf16[64,3712]{1,0:T(8,128)(2,1)S(1)} %get-tuple-element.51), channel_id=1, source_target_pairs={{0,12},{4,8},{8,4},{12,0},{16,28},{20,24},{24,20},{28,16},{1,13},{... | collective-permute-start | bytes 1425416 | tf_op jit(solution)/shard_map/ppermute | solution.py:487
  27.8 3.5 %collective-permute-start.1 = (f32[2,3,64,1024]{3,2,1,0:T(8,128)S(1)}, f32[2,3,64,1024]{3,2,1,0:T(8,128)S(1)}, u32[]{:S(2)}, u32[]{:S(2)}) collective-permute-start(f32[2,3,64,1024]{3,2,1,0:T(8,128)S(1)} %get-tuple-element.49), channel_id=1, source_target_pairs={{0,1},{1,0},{2,3},{3,2},{4,5},{5,4},{6,7},{7,6},{8,9},{9,8},{10,11... | collective-permute-start | bytes 4718600 | tf_op jit(solution)/shard_map/ppermute | solution.py:482
  32.4 52.2 %collective-permute-start.2 = (bf16[2,3,64,1024]{3,2,1,0:T(8,128)(2,1)}, bf16[2,3,64,1024]{3,2,1,0:T(8,128)(2,1)}, u32[]{:S(2)}, u32[]{:S(2)}) collective-permute-start(bf16[2,3,64,1024]{3,2,1,0:T(8,128)(2,1)} %add.11.refs_5_.refs_1_), channel_id=1, source_target_pairs={{0,2},{1,3},{2,0},{3,1},{4,6},{5,7},{6,4},{7,5},{8,10},{9,11},{10,... | collective-permute-start | bytes 2359304 | tf_op jit(solution)/shard_map/ppermute | solution.py:482
  58.4 37.1 %copy-start.10 = (bf16[64,3712]{1,0:T(8,128)(2,1)}, bf16[64,3712]{1,0:T(8,128)(2,1)S(1)}, u32[]{:S(2)}) copy-start(bf16[64,3712]{1,0:T(8,128)(2,1)S(1)} %collective-permute-done.6.refs_1_.refs_4_.refs_3_.refs_11_) | copy-start | bytes 1425412
  63.1 56.7 %copy-start = (bf16[64,3712]{1,0:T(8,128)(2,1)}, bf16[64,3712]{1,0:T(8,128)(2,1)S(1)}, u32[]{:S(2)}) copy-start(bf16[64,3712]{1,0:T(8,128)(2,1)S(1)} %collective-permute-done.3.refs_5_.refs_0_.refs_3_.refs_6_.refs_14_) | copy-start | bytes 1425412
  63.2 56.7 %copy-start.2 = (bf16[64,3712]{1,0:T(8,128)(2,1)}, bf16[64,3712]{1,0:T(8,128)(2,1)S(1)}, u32[]{:S(2)}) copy-start(bf16[64,3712]{1,0:T(8,128)(2,1)S(1)} %collective-permute-done.4.refs_6_.refs_1_.refs_4_.refs_7_.refs_15_) | copy-start | bytes 1425412
  64.4 41.9 %collective-permute-start.15 = (bf16[64,3712]{1,0:T(8,128)(2,1)}, bf16[64,3712]{1,0:T(8,128)(2,1)}, u32[]{:S(2)}, u32[]{:S(2)}) collective-permute-start(bf16[64,3712]{1,0:T(8,128)(2,1)} %get-tuple-element.54.refs_0_), channel_id=1, source_target_pairs={{0,16},{4,20},{8,24},{12,28},{16,0},{20,4},{24,8},{28,12},{1,17},{... | collective-permute-start | bytes 1425416 | tf_op jit(solution)/shard_map/ppermute | solution.py:487
  69.2 3.4 %collective-permute-start.7 = (f32[2,3,64,1024]{3,2,1,0:T(8,128)S(1)}, f32[2,3,64,1024]{3,2,1,0:T(8,128)S(1)}, u32[]{:S(2)}, u32[]{:S(2)}) collective-permute-start(f32[2,3,64,1024]{3,2,1,0:T(8,128)S(1)} %get-tuple-element.53), channel_id=1, source_target_pairs={{0,1},{1,0},{2,3},{3,2},{4,5},{5,4},{6,7},{7,6},{8,9},{9,8},{10,11... | collective-permute-start | bytes 4718600 | tf_op jit(solution)/shard_map/ppermute | solution.py:482
  69.4 39.9 %collective-permute-start.16 = (bf16[64,3712]{1,0:T(8,128)(2,1)}, bf16[64,3712]{1,0:T(8,128)(2,1)}, u32[]{:S(2)}, u32[]{:S(2)}) collective-permute-start(bf16[64,3712]{1,0:T(8,128)(2,1)} %get-tuple-element.61), channel_id=1, source_target_pairs={{0,20},{4,16},{8,28},{12,24},{16,4},{20,0},{24,12},{28,8},{1,21},{... | collective-permute-start | bytes 1425416 | tf_op jit(solution)/shard_map/ppermute | solution.py:487
  73.7 21.7 %collective-permute-start.11 = (bf16[2,3,64,1024]{3,2,1,0:T(8,128)(2,1)}, bf16[2,3,64,1024]{3,2,1,0:T(8,128)(2,1)}, u32[]{:S(2)}, u32[]{:S(2)}) collective-permute-start(bf16[2,3,64,1024]{3,2,1,0:T(8,128)(2,1)} %add.12.refs_5_.refs_1_), channel_id=1, source_target_pairs={{0,2},{1,3},{2,0},{3,1},{4,6},{5,7},{6,4},{7,5},{8,10},{9,11},{10,... | collective-permute-start | bytes 2359304 | tf_op jit(solution)/shard_map/ppermute | solution.py:482
  80.0 3.5 %collective-permute-start.8 = (f32[2,3,64,1024]{3,2,1,0:T(8,128)S(1)}, f32[2,3,64,1024]{3,2,1,0:T(8,128)S(1)}, u32[]{:S(2)}, u32[]{:S(2)}) collective-permute-start(f32[2,3,64,1024]{3,2,1,0:T(8,128)S(1)} %get-tuple-element.56), channel_id=1, source_target_pairs={{0,1},{1,0},{2,3},{3,2},{4,5},{5,4},{6,7},{7,6},{8,9},{9,8},{10,11... | collective-permute-start | bytes 4718600 | tf_op jit(solution)/shard_map/ppermute | solution.py:482
  87.1 2.4 %collective-permute-start.9 = (bf16[2,64,3200]{2,1,0:T(8,128)(2,1)S(1)}, bf16[2,64,3200]{2,1,0:T(8,128)(2,1)S(1)}, u32[]{:S(2)}, u32[]{:S(2)}) collective-permute-start(bf16[2,64,3200]{2,1,0:T(8,128)(2,1)S(1)} %activate.4.refs_0_.refs_16_), channel_id=1, source_target_pairs={{0,1},{1,0},{2,3},{3,2},{4,5},{5,4},{6,7},{7,6},{8,9},{9,8},{10,11... | collective-permute-start | bytes 2457608 | tf_op jit(solution)/shard_map/ppermute | solution.py:482
  87.3 32.6 %collective-permute-start.19 = (bf16[2,3,64,1024]{3,2,1,0:T(8,128)(2,1)}, bf16[2,3,64,1024]{3,2,1,0:T(8,128)(2,1)}, u32[]{:S(2)}, u32[]{:S(2)}) collective-permute-start(bf16[2,3,64,1024]{3,2,1,0:T(8,128)(2,1)} %add.13.refs_5_.refs_1_), channel_id=1, source_target_pairs={{0,2},{1,3},{2,0},{3,1},{4,6},{5,7},{6,4},{7,5},{8,10},{9,11},{10,... | collective-permute-start | bytes 2359304 | tf_op jit(solution)/shard_map/ppermute | solution.py:482
  97.9 2.4 %collective-permute-start.12 = (bf16[2,64,3200]{2,1,0:T(8,128)(2,1)S(1)}, bf16[2,64,3200]{2,1,0:T(8,128)(2,1)S(1)}, u32[]{:S(2)}, u32[]{:S(2)}) collective-permute-start(bf16[2,64,3200]{2,1,0:T(8,128)(2,1)S(1)} %activate.5.refs_0_.refs_18_), channel_id=1, source_target_pairs={{0,1},{1,0},{2,3},{3,2},{4,5},{5,4},{6,7},{7,6},{8,9},{9,8},{10,11... | collective-permute-start | bytes 2457608 | tf_op jit(solution)/shard_map/ppermute | solution.py:482
  98.1 51.9 %collective-permute-start.10 = (bf16[64,1920]{1,0:T(8,128)(2,1)}, bf16[64,1920]{1,0:T(8,128)(2,1)}, u32[]{:S(2)}, u32[]{:S(2)}) collective-permute-start(bf16[64,1920]{1,0:T(8,128)(2,1)} %get-tuple-element.58), channel_id=1, source_target_pairs={{0,4},{4,0},{8,12},{12,8},{16,20},{20,16},{24,28},{28,24},{1,5},{5... | collective-permute-start | bytes 737288 | tf_op jit(solution)/shard_map/ppermute | solution.py:487
  106.2 43.9 %collective-permute-start.13 = (bf16[64,1920]{1,0:T(8,128)(2,1)}, bf16[64,1920]{1,0:T(8,128)(2,1)}, u32[]{:S(2)}, u32[]{:S(2)}) collective-permute-start(bf16[64,1920]{1,0:T(8,128)(2,1)} %get-tuple-element.59.refs_5_), channel_id=1, source_target_pairs={{0,8},{4,12},{8,0},{12,4},{16,24},{20,28},{24,16},{28,20},{1,9},{5... | collective-permute-start | bytes 737288 | tf_op jit(solution)/shard_map/ppermute | solution.py:487
  106.3 72.0 %collective-permute-start.14 = (bf16[64,1920]{1,0:T(8,128)(2,1)}, bf16[64,1920]{1,0:T(8,128)(2,1)}, u32[]{:S(2)}, u32[]{:S(2)}) collective-permute-start(bf16[64,1920]{1,0:T(8,128)(2,1)} %get-tuple-element.60), channel_id=1, source_target_pairs={{0,12},{4,8},{8,4},{12,0},{16,28},{20,24},{24,20},{28,16},{1,13},{... | collective-permute-start | bytes 737288 | tf_op jit(solution)/shard_map/ppermute | solution.py:487
  115.0 3.5 %collective-permute-start.17 = (f32[2,3,64,1024]{3,2,1,0:T(8,128)S(1)}, f32[2,3,64,1024]{3,2,1,0:T(8,128)S(1)}, u32[]{:S(2)}, u32[]{:S(2)}) collective-permute-start(f32[2,3,64,1024]{3,2,1,0:T(8,128)S(1)} %get-tuple-element.63), channel_id=1, source_target_pairs={{0,1},{1,0},{2,3},{3,2},{4,5},{5,4},{6,7},{7,6},{8,9},{9,8},{10,11... | collective-permute-start | bytes 4718600 | tf_op jit(solution)/shard_map/ppermute | solution.py:482
  118.7 19.6 %collective-permute-start.18 = (bf16[2,3,64,1024]{3,2,1,0:T(8,128)(2,1)S(1)}, bf16[2,3,64,1024]{3,2,1,0:T(8,128)(2,1)S(1)}, u32[]{:S(2)}, u32[]{:S(2)}) collective-permute-start(bf16[2,3,64,1024]{3,2,1,0:T(8,128)(2,1)S(1)} %add.14.refs_5_.refs_1_), channel_id=1, source_target_pairs={{0,2},{1,3},{2,0},{3,1},{4,6},{5,7},{6,4},{7,5},{8,10},{9,11},{10,... | collective-permute-start | bytes 2359304 | tf_op jit(solution)/shard_map/ppermute | solution.py:482
  122.3 2.4 %collective-permute-start.20 = (bf16[2,64,3200]{2,1,0:T(8,128)(2,1)S(1)}, bf16[2,64,3200]{2,1,0:T(8,128)(2,1)S(1)}, u32[]{:S(2)}, u32[]{:S(2)}) collective-permute-start(bf16[2,64,3200]{2,1,0:T(8,128)(2,1)S(1)} %activate.6.refs_0_.refs_22_), channel_id=1, source_target_pairs={{0,1},{1,0},{2,3},{3,2},{4,5},{5,4},{6,7},{7,6},{8,9},{9,8},{10,11... | collective-permute-start | bytes 2457608 | tf_op jit(solution)/shard_map/ppermute | solution.py:482
  140.6 2.4 %collective-permute-start.21 = (bf16[2,64,3200]{2,1,0:T(8,128)(2,1)S(1)}, bf16[2,64,3200]{2,1,0:T(8,128)(2,1)S(1)}, u32[]{:S(2)}, u32[]{:S(2)}) collective-permute-start(bf16[2,64,3200]{2,1,0:T(8,128)(2,1)S(1)} %activate.7.refs_0_.refs_20_), channel_id=1, source_target_pairs={{0,1},{1,0},{2,3},{3,2},{4,5},{5,4},{6,7},{7,6},{8,9},{9,8},{10,11... | collective-permute-start | bytes 2457608 | tf_op jit(solution)/shard_map/ppermute | solution.py:482
  140.7 37.7 %collective-permute-start.24 = (bf16[64,1920]{1,0:T(8,128)(2,1)S(1)}, bf16[64,1920]{1,0:T(8,128)(2,1)S(1)}, u32[]{:S(2)}, u32[]{:S(2)}) collective-permute-start(bf16[64,1920]{1,0:T(8,128)(2,1)S(1)} %get-tuple-element.64.refs_5_), channel_id=1, source_target_pairs={{0,24},{4,28},{8,16},{12,20},{16,8},{20,12},{24,0},{28,4},{1,25},{... | collective-permute-start | bytes 737288 | tf_op jit(solution)/shard_map/ppermute | solution.py:487
  143.1 35.3 %collective-permute-start.25 = (bf16[64,1920]{1,0:T(8,128)(2,1)S(1)}, bf16[64,1920]{1,0:T(8,128)(2,1)S(1)}, u32[]{:S(2)}, u32[]{:S(2)}) collective-permute-start(bf16[64,1920]{1,0:T(8,128)(2,1)S(1)} %get-tuple-element.67), channel_id=1, source_target_pairs={{0,28},{4,24},{8,20},{12,16},{16,12},{20,8},{24,4},{28,0},{1,29},{... | collective-permute-start | bytes 737288 | tf_op jit(solution)/shard_map/ppermute | solution.py:487
  150.0 30.6 %collective-permute-start.22 = (bf16[64,1920]{1,0:T(8,128)(2,1)S(1)}, bf16[64,1920]{1,0:T(8,128)(2,1)S(1)}, u32[]{:S(2)}, u32[]{:S(2)}) collective-permute-start(bf16[64,1920]{1,0:T(8,128)(2,1)S(1)} %get-tuple-element.65.refs_24_), channel_id=1, source_target_pairs={{0,16},{4,20},{8,24},{12,28},{16,0},{20,4},{24,8},{28,12},{1,17},{... | collective-permute-start | bytes 737288 | tf_op jit(solution)/shard_map/ppermute | solution.py:487
  150.1 35.3 %copy-start.28 = (bf16[64,1920]{1,0:T(8,128)(2,1)S(1)}, bf16[64,1920]{1,0:T(8,128)(2,1)}, u32[]{:S(2)}) copy-start(bf16[64,1920]{1,0:T(8,128)(2,1)} %copy-done.27) | copy-start | bytes 737284
  150.1 35.3 %copy-start.30 = (s32[8,128]{1,0:T(8,128)S(1)}, s32[8,128]{1,0:T(8,128)}, u32[]{:S(2)}) copy-start(s32[8,128]{1,0:T(8,128)} %copy-done.29) | copy-start | bytes 12292
  150.2 35.2 %collective-permute-start.23 = (bf16[64,1920]{1,0:T(8,128)(2,1)S(1)}, bf16[64,1920]{1,0:T(8,128)(2,1)S(1)}, u32[]{:S(2)}, u32[]{:S(2)}) collective-permute-start(bf16[64,1920]{1,0:T(8,128)(2,1)S(1)} %get-tuple-element.66), channel_id=1, source_target_pairs={{0,20},{4,16},{8,28},{12,24},{16,4},{20,0},{24,12},{28,8},{1,21},{... | collective-permute-start | bytes 737288 | tf_op jit(solution)/shard_map/ppermute | solution.py:487
  (31 other events, 310.9 us)

commit v3 on v2

--- a/solution.py
+++ b/solution.py
@@ -95,9 +95,120 @@
     return jnp.where(place_ref[index : index + 1, :] == row, 1.0, 0.0).astype(BF)
 
 
-def route_kernel(where_ref, groups_ref, ids_ref, gates_ref, place_ref, table_ref):
+def select_rows(experts, where_ref, tokens_ref, outs):
     me, flip = where_ref[0], where_ref[1]
-    tokens = place_ref.shape[1]
+    tokens, width = tokens_ref.shape
+    size = outs[0].shape[0]
+    lane = lax.broadcasted_iota(jnp.int32, (tokens, LANES), 1)
+    holds = (
+        lax.broadcasted_iota(jnp.int32, (LANES, LANES), 0) // experts
+        == lax.broadcasted_iota(jnp.int32, (LANES, LANES), 1)
+    )
+    named = jnp.where(tokens_ref[:, width - LANES :].astype(F32) > 0.0, 1.0, 0.0).astype(BF)
+    member = dot_nn(named, jnp.where(holds, 1.0, 0.0).astype(BF)) > 0.0
+    earlier = (
+        lax.broadcasted_iota(jnp.int32, (tokens, tokens), 1)
+        < lax.broadcasted_iota(jnp.int32, (tokens, tokens), 0)
+    )
+    rank = dot_nn(
+        jnp.where(earlier, 1.0, 0.0).astype(BF), jnp.where(member, 1.0, 0.0).astype(BF)
+    )
+    place = jnp.where(member, rank.astype(jnp.int32) ^ flip, -1)
+    contract = (((0,), (0,)), ((), ()))
+    for index, out in enumerate(outs):
+        row = jnp.sum(jnp.where(lane == (me ^ index), place, 0), axis=1, keepdims=True)
+        hot = lax.broadcasted_iota(jnp.int32, (tokens, size), 1) == row
+        hot = jnp.where(hot, 1.0, 0.0).astype(BF)
+        out[...] = lax.dot_general(
+            hot, tokens_ref[...], contract, preferred_element_type=F32
+        ).astype(BF)
+
+
+def select_kernel(experts, where_ref, tokens_ref, *outs):
+    select_rows(experts, where_ref, tokens_ref, outs)
+
+
+def select(where, whole, experts, count, size, deps):
+    block = jax.ShapeDtypeStruct((size, whole.shape[1]), BF)
+    return call(
+        functools.partial(select_kernel, experts),
+        deps,
+        [where, whole],
+        [IN_SMEM, IN_VMEM],
+        out_specs=[IN_VMEM] * count,
+        out_shape=[block] * count,
+        compiler_params=params(8),
+        cost_estimate=CHEAP,
+        name="select",
+    )
+
+
+def route_kernel(experts, where_ref, ids_hbm, gates_hbm, in_hbm, grad_hbm, *refs):
+    out_ref, outs = refs[0], refs[1:-3]
+    ids_ref, gates_ref, sems = refs[-3:]
+    tokens, width = in_hbm.shape
+    fetch(
+        [
+            (ids_hbm, ids_ref),
+            (gates_hbm, gates_ref),
+            (in_hbm, out_ref.at[:, :width]),
+            (grad_hbm, out_ref.at[:, width : 2 * width]),
+        ],
+        sems,
+    )
+    expert = lax.broadcasted_iota(jnp.int32, (LANES, tokens), 0)
+    table = jnp.zeros((LANES, tokens), F32)
+    for index in range(ids_ref.shape[0]):
+        gate = gates_ref[index : index + 1, :].astype(F32)
+        table = jnp.where(ids_ref[index : index + 1, :] == expert, gate, table)
+    out_ref[:, 2 * width :] = table.T.astype(BF)
+    select_rows(experts, where_ref, out_ref, outs)
+
+
+def route(where, ids_t, gates_t, hidden_in, out_grad, experts, count, size):
+    tokens, width = hidden_in.shape
+    wide = 2 * width + LANES
+    block = jax.ShapeDtypeStruct((size, wide), BF)
+    outs = pl.pallas_call(
+        functools.partial(route_kernel, experts),
+        in_specs=[IN_SMEM] + [IN_HBM] * 4,
+        out_specs=[IN_VMEM] * (1 + count),
+        out_shape=[jax.ShapeDtypeStruct((tokens, wide), BF)] + [block] * count,
+        scratch_shapes=[
+            pltpu.VMEM(ids_t.shape, ids_t.dtype),
+            pltpu.VMEM(gates_t.shape, gates_t.dtype),
+            pltpu.SemaphoreType.DMA((4,)),
+        ],
+        compiler_params=params(8),
+        cost_estimate=CHEAP,
+        name="route",
+    )(where, *[remote(array) for array in (ids_t, gates_t, hidden_in, out_grad)])
+    return outs[0], list(outs[1:])
+
+
+def relay_kernel(in_ref, out_ref):
+    out_ref[...] = in_ref[...]
+
+
+def relay(array, deps):
+    return call(
+        relay_kernel,
+        deps,
+        [array],
+        [IN_VMEM],
+        out_specs=IN_VMEM,
+        out_shape=jax.ShapeDtypeStruct(array.shape, array.dtype),
+        compiler_params=params(4),
+        cost_estimate=CHEAP,
+        name="relay",
+    )
+
+
+def unpack_kernel(where_ref, groups_ref, ids_ref, *refs):
+    blocks, (grad_ref, gate_ref, rows, place_ref, sems) = refs[:-5], refs[-5:]
+    size = blocks[0].shape[0]
+    tokens, width = grad_ref.shape
+    me, flip = where_ref[0], where_ref[1]
     peers = me ^ lax.broadcasted_iota(jnp.int32, place_ref.shape, 0)
     member = jnp.zeros(place_ref.shape, F32)
     for index in range(groups_ref.shape[0]):
@@ -110,58 +221,6 @@
     ).astype(BF)
     rank = dot_nn(member.astype(BF), earlier).astype(jnp.int32)
     place_ref[...] = jnp.where(member > 0.0, rank ^ flip, -1)
-    expert = lax.broadcasted_iota(jnp.int32, (LANES, tokens), 0)
-    table = jnp.zeros((LANES, tokens), F32)
-    for index in range(ids_ref.shape[0]):
-        gate = gates_ref[index : index + 1, :].astype(F32)
-        table = jnp.where(ids_ref[index : index + 1, :] == expert, gate, table)
-    table_ref[...] = table.astype(BF)
-
-
-def route(where, groups_t, ids_t, gates_t, nodes):
-    tokens = ids_t.shape[1]
-    return pl.pallas_call(
-        route_kernel,
-        in_specs=[IN_SMEM] + [IN_VMEM] * 3,
-        out_specs=[IN_VMEM] * 2,
-        out_shape=[
-            jax.ShapeDtypeStruct((nodes, tokens), jnp.int32),
-            jax.ShapeDtypeStruct((LANES, tokens), BF),
-        ],
-        compiler_params=params(4),
-        cost_estimate=CHEAP,
-        name="route",
-    )(where, groups_t, ids_t, gates_t)
-
-
-def pack_kernel(masks, place_ref, in_ref, grad_ref, table_ref, *outs):
-    width = in_ref.shape[1]
-    for mask, out in zip(masks, outs):
-        hot = hot_block(place_ref, mask, out.shape[0])
-        out[:, :width] = dot_nn(hot, in_ref[...]).astype(BF)
-        out[:, width : 2 * width] = dot_nn(hot, grad_ref[...]).astype(BF)
-        out[:, 2 * width :] = dot_nt(hot, table_ref[...]).astype(BF)
-
-
-def pack(place, hidden_in, out_grad, table, masks, size, deps):
-    block = jax.ShapeDtypeStruct((size, 2 * hidden_in.shape[1] + LANES), BF)
-    return call(
-        functools.partial(pack_kernel, list(masks)),
-        deps,
-        [place, hidden_in, out_grad, table],
-        [IN_VMEM] * 4,
-        out_specs=[IN_VMEM] * len(masks),
-        out_shape=[block] * len(masks),
-        compiler_params=params(8),
-        cost_estimate=CHEAP,
-        name="pack",
-    )
-
-
-def unpack_kernel(place_ref, ids_ref, *refs):
-    blocks, (grad_ref, gate_ref, rows, sems) = refs[:-4], refs[-4:]
-    size = blocks[0].shape[0]
-    tokens, width = grad_ref.shape
     pieces = [rows.at[index * size : (index + 1) * size] for index in range(len(blocks))]
     fetch(list(zip(blocks, pieces)), sems)
     hot = join([hot_block(place_ref, index, size) for index in range(len(blocks))])
@@ -176,12 +235,12 @@
         gate_ref[index : index + 1, :] = jnp.sum(chosen, axis=0, keepdims=True)
 
 
-def unpack(place, ids_t, blocks):
+def unpack(where, groups_t, ids_t, blocks):
     size, wide = blocks[0].shape
     count, tokens = ids_t.shape
     return pl.pallas_call(
         unpack_kernel,
-        in_specs=[IN_VMEM] * 2 + [ANYWHERE] * len(blocks),
+        in_specs=[IN_SMEM, IN_VMEM, IN_VMEM] + [ANYWHERE] * len(blocks),
         out_specs=[IN_VMEM] * 2,
         out_shape=[
             jax.ShapeDtypeStruct((tokens, wide - LANES), BF),
@@ -189,58 +248,64 @@
         ],
         scratch_shapes=[
             pltpu.VMEM((size * len(blocks), wide), BF),
+            pltpu.VMEM((len(blocks), tokens), jnp.int32),
             pltpu.SemaphoreType.DMA((len(blocks),)),
         ],
         compiler_params=params(12),
         cost_estimate=CHEAP,
         name="unpack",
-    )(place, ids_t, *blocks)
-
-
-def project_kernel(blocks, *refs):
-    (gate_ref, up_ref, down_ref), (own_ref, other_ref, rows_ref, sems) = refs[blocks:-4], refs[-4:]
-    width = rows_ref.shape[1] // 2
+    )(where, groups_t, ids_t, *blocks)
+
+
+def project_kernel(counts, starts, *refs):
+    blocks = sum(counts)
+    mats, (own_ref, other_ref, rows_ref, sems) = list(refs[blocks:-4]), refs[-4:]
+    width = rows_ref.shape[2]
     half = refs[0].shape[0] // 2
     experts, _, kept, hid = own_ref.shape
-    pairs = []
-    for index, block in enumerate(refs[:blocks]):
-        for place in range(2):
-            start = place * kept + index * half
-            pairs.append(
-                (
-                    block.at[place * half : (place + 1) * half, : 2 * width],
-                    rows_ref.at[start : start + half],
+    pairs, first = [], 0
+    for which, (count, start) in enumerate(zip(counts, starts)):
+        for index in range(count):
+            for place in range(2):
+                row = place * kept + index * half
+                pairs.append(
+                    (
+                        refs[first + index].at[
+                            place * half : (place + 1) * half, start : start + width
+                        ],
+                        rows_ref.at[which, row : row + half],
+                    )
                 )
-            )
+        first += count
     fetch(pairs, sems)
-    rows_in, rows_grad = rows_ref[:, :width], rows_ref[:, width:]
     tile = tile_of(hid, 512)
-
-    def put(e, index, part, value):
-        own_ref[e, index, :, part] = value[:kept]
-        other_ref[e, index, :, part] = value[kept:]
-
     for e in range(experts):
-        for start in range(0, hid, tile):
-            part = slice(start, start + tile)
-            put(e, 0, part, dot_nn(rows_in, gate_ref[e, :, part]))
-            put(e, 1, part, dot_nn(rows_in, up_ref[e, :, part]))
-            put(e, 2, part, dot_nt(rows_grad, down_ref[e, part]))
-
-
-def project(blocks, w_gate, w_up, w_down, deps):
-    experts, width, hid = w_gate.shape
-    rows = len(blocks) * blocks[0].shape[0]
-    shape = jax.ShapeDtypeStruct((experts, 3, rows // 2, hid), F32)
-    return call(
-        functools.partial(project_kernel, len(blocks)),
-        deps,
-        [*blocks, resident(w_gate), resident(w_up), resident(w_down)],
-        [ANYWHERE] * len(blocks) + [IN_VMEM] * 3,
+        for begin in range(0, hid, tile):
+            part = slice(begin, begin + tile)
+            for index, mat in enumerate(mats):
+                if index == len(mats) - 1 and len(mats) % 2:
+                    value = dot_nt(rows_ref[len(counts) - 1], mat[e, part])
+                else:
+                    value = dot_nn(rows_ref[0], mat[e, :, part])
+                own_ref[e, index, :, part] = value[:kept]
+                other_ref[e, index, :, part] = value[kept:]
+
+
+def project(pieces, mats, hid, width, deps):
+    experts = mats[0].shape[0]
+    blocks = [block for piece, _ in pieces for block in piece]
+    kept = len(pieces[0][0]) * blocks[0].shape[0] // 2
+    shape = jax.ShapeDtypeStruct((experts, len(mats), kept, hid), F32)
+    counts, starts = [len(piece) for piece, _ in pieces], [start for _, start in pieces]
+    return call(
+        functools.partial(project_kernel, counts, starts),
+        deps,
+        [*blocks, *[resident(mat) for mat in mats]],
+        [ANYWHERE] * len(blocks) + [IN_VMEM] * len(mats),
         out_specs=[IN_VMEM, IN_VMEM],
         out_shape=[shape, shape],
         scratch_shapes=[
-            pltpu.VMEM((rows, 2 * width), BF),
+            pltpu.VMEM((len(pieces), 2 * kept, width), BF),
             pltpu.SemaphoreType.DMA((2 * len(blocks),)),
         ],
         compiler_params=params(12),
@@ -275,9 +340,10 @@
     )
 
 
-def act_kernel(blocks, where_ref, sum_a, sum_b, *refs):
+def act_kernel(blocks, pairs, where_ref, *refs):
+    sums, refs = refs[: 2 * pairs], refs[2 * pairs :]
     acts_ref, gates_ref, sems = refs[blocks:]
-    experts, _, kept, hid = sum_a.shape
+    experts, _, kept, hid = sums[0].shape
     half = refs[0].shape[0] // 2
     width = refs[0].shape[1] - LANES
     fetch(
@@ -287,6 +353,7 @@
         ],
         sems,
     )
+    grad_at = 2 if pairs == 1 else 0
     tile = 16
     lane = lax.broadcasted_iota(jnp.int32, (tile, LANES), 1)
     for e in range(experts):
@@ -295,11 +362,14 @@
         @pl.loop(0, kept // tile)
         def _(step):
             rows = pl.ds(pl.multiple_of(step * tile, tile), tile)
+
+            def both(pair, index):
+                return pair[0][e, index, rows].astype(F32) + pair[1][e, index, rows].astype(F32)
+
             gates = gates_ref[rows].astype(F32)
             gate = jnp.sum(jnp.where(mine, gates, 0.0), axis=1, keepdims=True)
-            pre_gate = sum_a[e, 0, rows].astype(F32) + sum_b[e, 0, rows].astype(F32)
-            pre_up = sum_a[e, 1, rows].astype(F32) + sum_b[e, 1, rows].astype(F32)
-            back = sum_a[e, 2, rows].astype(F32) + sum_b[e, 2, rows].astype(F32)
+            pre_gate, pre_up = both(sums[:2], 0), both(sums[:2], 1)
+            back = both(sums[-2:], grad_at)
             sig = jax.nn.sigmoid(pre_gate)
             silu = pre_gate * sig
             hidden = silu * pre_up
@@ -312,13 +382,13 @@
             acts_ref[e, rows, 3 * hid :] = jnp.where(mine, term, 0.0).astype(BF)
 
 
-def activate(where, sum_a, sum_b, blocks, deps):
-    experts, _, kept, hid = sum_a.shape
-    return call(
-        functools.partial(act_kernel, len(blocks)),
-        deps,
-        [where, sum_a, sum_b, *blocks],
-        [IN_SMEM] + [IN_VMEM] * 2 + [ANYWHERE] * len(blocks),
+def activate(where, sums, blocks, deps):
+    experts, _, kept, hid = sums[0].shape
+    return call(
+        functools.partial(act_kernel, len(blocks), len(sums) // 2),
+        deps,
+        [where, *sums, *blocks],
+        [IN_SMEM] + [IN_VMEM] * len(sums) + [ANYWHERE] * len(blocks),
         out_specs=IN_VMEM,
         out_shape=jax.ShapeDtypeStruct((experts, kept, 3 * hid + LANES), BF),
         scratch_shapes=[
@@ -388,17 +458,18 @@
     blocks = sum(groups)
     acts = refs[2 * blocks : -6]
     out_gate, out_up, out_down, gate_acts, up_acts, hidden_t = refs[-6:]
-    hid = gate_acts.shape[1]
-
-    @pl.when(pl.program_id(1) == 0)
+    experts, _, hid = gate_acts.shape
+
+    @pl.when(pl.program_id(0) == 0)
     def _():
-        first = 0
-        for ref in acts:
-            rows = slice(first, first + ref.shape[1])
-            gate_acts[rows] = ref[0, :, :hid]
-            up_acts[rows] = ref[0, :, hid : 2 * hid]
-            hidden_t[:, rows] = ref[0, :, 2 * hid : 3 * hid].T
-            first += ref.shape[1]
+        for e in range(experts):
+            first = 0
+            for ref in acts:
+                rows = slice(first, first + ref.shape[1])
+                gate_acts[e, rows] = ref[e, :, :hid]
+                up_acts[e, rows] = ref[e, :, hid : 2 * hid]
+                hidden_t[e, :, rows] = ref[e, :, 2 * hid : 3 * hid].T
+                first += ref.shape[1]
 
     def rows_of(ins):
         out, first = [], 0
@@ -410,38 +481,42 @@
         return join(out)
 
     rows_t = rows_of(refs[:blocks]).T
-    out_gate[0] = dot_nn(rows_t, gate_acts[...]).astype(BF)
-    out_up[0] = dot_nn(rows_t, up_acts[...]).astype(BF)
-    out_down[0] = dot_nn(hidden_t[...], rows_of(refs[blocks : 2 * blocks])).astype(BF)
-
-
-def weight_grads(blocks, acts, groups, deps):
-    size, width = blocks[0].shape[0], (blocks[0].shape[1] - LANES) // 2
+    grads = rows_of(refs[blocks : 2 * blocks])
+    for e in range(experts):
+        out_gate[e] = dot_nn(rows_t, gate_acts[e]).astype(BF)
+        out_up[e] = dot_nn(rows_t, up_acts[e]).astype(BF)
+        out_down[e] = dot_nn(hidden_t[e], grads).astype(BF)
+
+
+def weight_grads(ins, grads, starts, width, acts, groups, deps):
+    size = ins[0].shape[0]
     experts = acts[0].shape[0]
     hid = (acts[0].shape[2] - LANES) // 3
-    rows = size * len(blocks)
+    rows = size * len(ins)
     tile = tile_of(width, 256)
-    steps = width // tile
-    in_spec = pl.BlockSpec((size, tile), lambda e, j: (0, j))
-    grad_spec = pl.BlockSpec((size, tile), lambda e, j: (0, steps + j))
-    act_specs = [pl.BlockSpec((1,) + act.shape[1:], lambda e, j: (e, 0, 0)) for act in acts]
-    wide = pl.BlockSpec((1, tile, hid), lambda e, j: (e, j, 0))
-    down = pl.BlockSpec((1, hid, tile), lambda e, j: (e, 0, j))
+
+    def row_spec(start):
+        return pl.BlockSpec((size, tile), lambda j: (0, start // tile + j))
+
+    wide = pl.BlockSpec((experts, tile, hid), lambda j: (0, j, 0))
+    down = pl.BlockSpec((experts, hid, tile), lambda j: (0, 0, j))
     wide_shape = jax.ShapeDtypeStruct((experts, width, hid), BF)
     return call(
         functools.partial(grads_kernel, groups),
         deps,
-        [*blocks, *blocks, *acts],
-        [in_spec] * len(blocks) + [grad_spec] * len(blocks) + act_specs,
-        grid=(experts, steps),
+        [*ins, *grads, *acts],
+        [row_spec(0) for _ in ins]
+        + [row_spec(start) for start in starts]
+        + [pl.BlockSpec(act.shape, lambda j: (0, 0, 0)) for act in acts],
+        grid=(width // tile,),
         out_specs=[wide, wide, down],
         out_shape=[wide_shape, wide_shape, jax.ShapeDtypeStruct((experts, hid, width), BF)],
         scratch_shapes=[
-            pltpu.VMEM((rows, hid), BF),
-            pltpu.VMEM((rows, hid), BF),
-            pltpu.VMEM((hid, rows), BF),
-        ],
-        compiler_params=params(32),
+            pltpu.VMEM((experts, rows, hid), BF),
+            pltpu.VMEM((experts, rows, hid), BF),
+            pltpu.VMEM((experts, hid, rows), BF),
+        ],
+        compiler_params=params(48),
         cost_estimate=CHEAP,
         name="weight_grads",
     )
@@ -470,6 +545,7 @@
 ):
     nodes = lax.axis_size("node")
     shares = lax.axis_size("local")
+    experts = w_gate.shape[0]
     capacity = 4 * hidden_in.shape[0] // nodes
     me = lax.axis_index("node")
     core = lax.axis_index("local") % 2
@@ -487,79 +563,102 @@
         return lax.ppermute(value, "node", [(i, i ^ mask) for i in range(nodes)])
 
     ids_t = expert_ids.T
-    place, table = route(where, group_ids.T, ids_t, gate_weight.T, nodes)
+    width, hid = w_gate.shape[1:]
     last = []
 
-    def send_step(group, deps=()):
-        blocks = pack(
-            place, hidden_in, out_grad, table, spans[group], capacity, [*last, *deps]
-        )
+    def send(blocks, masks):
+        return [cross(block, mask) for block, mask in zip(blocks, masks)]
+
+    def select_step(group, whole):
+        blocks = select(where, whole, experts, quarter, capacity, last)
         last[:] = [blocks[0]]
-        rows[group] = [cross(block, mask) for block, mask in zip(blocks, spans[group])]
+        rows[group] = send(blocks, spans[0])
 
     def pause(count):
         for _ in range(count):
             last[:] = [mark(last)]
 
-    def project_step(group):
-        mine, other = project(rows[group], v_gate, v_up, v_down, last)
+    def project_step(pieces, mats):
+        mine, other = project(pieces, mats, hid, width, last)
         last[:] = [mine]
-        parts[group] = mine, swap(other, 1)
-
-    def sum_step(group):
-        pause(24)
-        total = add(*parts[group], last)
+        return mine, swap(other, 1)
+
+    def sum_step(mine, other):
+        total = add(mine, other, last)
         last[:] = [total]
         step = 2
         while 2 * step < shares:
             total = (total.astype(F32) + swap(total, step).astype(F32)).astype(BF)
             step *= 2
-        sums[group] = total, swap(total, step)
+        return [total, swap(total, step)]
+
+    def whole_project(group):
+        return project_step([(rows[group], 0), (rows[group], width)], mats)
 
     def act_step(group):
-        mine = activate(where, *sums[group], rows[group], last)
+        mine = activate(where, sums[group], rows[group], last)
         last[:] = [mine]
         acts[group] = mine, swap(mine, 1)
 
+    def settle(arrays):
+        last[:] = [mark([*last, *arrays])]
+
     def back_step(group):
-        pause(24)
         blocks = back(*acts[group], v_gate, v_up, len(spans[group]), last)
         last[:] = [blocks[0]]
-        for mask, block in zip(spans[group], blocks):
-            returned[mask] = cross(block, mask)
-
-    rows, parts, sums, acts = [[None] * 4 for _ in range(4)]
+        for mask, block in zip(spans[group], send(blocks, spans[group])):
+            returned[mask] = block
+
+    rows, sums, acts = [[None] * 4 for _ in range(3)]
     returned = [None] * nodes
-    send_step(own)
-    send_step(near)
-    send_step(far)
-    v_gate, v_up, v_down = load((w_gate, w_up, w_down), last)
+    whole, blocks = route(
+        where, ids_t, gate_weight.T, hidden_in, out_grad, experts, 2 * quarter, capacity
+    )
+    last[:] = [whole]
+    rows[own] = send(blocks[:quarter], spans[own])
+    rows[near] = send(blocks[quarter:], spans[near])
+    mid_whole = cross(whole, 2 * quarter)
+    far_whole = cross(mid_whole, quarter)
+    mats = load((w_gate, w_up, w_down), last)
+    v_gate, v_up, v_down = mats
     last[:] = [v_gate]
-    project_step(own)
-    sum_step(own)
-    project_step(near)
-    send_step(mid, rows[far])
-    sum_step(near)
-    project_step(far)
-    sum_step(far)
+
+    parts = [None] * 4
+    parts[own] = whole_project(own)
+    pause(8)
+    sums[own] = sum_step(*parts[own])
+    parts[near] = whole_project(near)
+    select_step(mid, mid_whole)
+    pause(8)
+    sums[near] = sum_step(*parts[near])
     act_step(own)
+    parts[mid] = whole_project(mid)
+    select_step(far, far_whole)
+    pause(8)
+    sums[mid] = sum_step(*parts[mid])
+    act_step(near)
     back_step(own)
-    act_step(near)
+    parts[far] = whole_project(far)
+    pause(8)
+    act_step(mid)
+    sums[far] = sum_step(*parts[far])
     back_step(near)
-    project_step(mid)
-    sum_step(mid)
+    back_step(mid)
     act_step(far)
+    pause(8)
     back_step(far)
-    act_step(mid)
-    back_step(mid)
-
+
+    blocks = [block for group in rows for block in group]
     grad_w_gate, grad_w_up, grad_w_down = weight_grads(
-        [block for group in rows for block in group],
+        blocks,
+        blocks,
+        [width] * nodes,
+        width,
         [part for pair in acts for part in pair],
         [len(span) for span in spans],
         last,
     )
-    grad_input, grad_gate = unpack(place, ids_t, returned)
+    grad_input, grad_gate = unpack(where, group_ids.T, ids_t, returned)
     return (grad_input, grad_gate.T.astype(BF), grad_w_gate, grad_w_up, grad_w_down)
 
 

time: 189 us -> 171 us (0.905)
  waiting for transfers between devices: 56.5 us -> 48.7 us
  Pallas kernels: 93.3 us -> 87.2 us
  local copies, waits for them, and re-layouts: 4.23 us -> 0.04 us
    pallas_call x214 -> x60, Pallas kernels: 89.7 us -> 79.7 us  [call(): pl.pallas_call(body, in_specs=list(in_specs) + [ANYWHERE] * extra, **sett...]
    ppermute x12, waiting for transfers between devices: 25 us -> 19.8 us  [swap(): return lax.ppermute(value, 'local', [(i, i ^ step) for i in range(shares)])]
    unnamed x74 -> x16, local copies, waits for them, and re-layouts: 4.23 us -> 0.04 us
    pallas_call x2, Pallas kernels: 3.61 us -> 7.47 us  [the longest x1 4.5 us: unpack(): pl.pallas_call(unpack_kernel, in_specs=[IN_SMEM, IN_VMEM, IN_VMEM] + [ANY...]
    ppermute x14, waiting for transfers between devices: 31.6 us -> 28.9 us  [cross(): return lax.ppermute(value, 'node', [(i, i ^ mask) for i in range(nodes)])]
  transfers between devices with their start and end apart: 26 -> 26, of which waited for: 12 -> 8; matrix products, arithmetic and copies ran while one was open for 0% -> 0% of each run, Pallas kernels for 47% -> 47%
where the time goes in v3:
time: 171 us
  Pallas kernels  87.2 us (51%)
  waiting for transfers between devices  48.7 us (28%)
  starting transfers between devices  33 us (19%)
    pallas_call x60, Pallas kernels, call(): pl.pallas_call(body, in_specs=list(in_specs) + [ANYWHERE] * extra, **sett...  79.7 us
    ppermute x14, waiting for transfers between devices, cross(): return lax.ppermute(value, 'node', [(i, i ^ mask) for i in range(nodes)])  28.9 us
    ppermute x14, starting transfers between devices, cross(): return lax.ppermute(value, 'node', [(i, i ^ mask) for i in range(nodes)])  26.6 us
    ppermute x12, waiting for transfers between devices, swap(): return lax.ppermute(value, 'local', [(i, i ^ step) for i in range(shares)])  19.8 us
    ppermute x12, starting transfers between devices, swap(): return lax.ppermute(value, 'local', [(i, i ^ step) for i in range(shares)])  6.44 us
    pallas_call x1, Pallas kernels, unpack(): pl.pallas_call(unpack_kernel, in_specs=[IN_SMEM, IN_VMEM, IN_VMEM] + [ANY...  4.5 us
  transfers between devices with their start and end apart: 26, of which 8 were waited for; matrix products, arithmetic and copies ran while one was open for 0% of the time, Pallas kernels for 47%

profile of v3, /device:TPU:0, one launch (start us, length us, event | category | flops | bytes accessed | tf_op | source)
XLA Modules:
  0.0 170.9 jit_solution(4821116257137272270)
XLA Ops:
  0.7 3.0 %route.1 = (bf16[128,3712]{1,0:T(8,128)(2,1)S(1)}, bf16[64,3712]{1,0:T(8,128)(2,1)S(1)}, bf16[64,3712]{1,0:T(8,128)(2,1)S(1)}, bf16[64,3712]{1,0:T(8,128)(2,1)S(1)}, bf16[64,3712]{1,0:T(8,128)(2,1)S(1)}) custom-call(s32[2]{0:T(128)S(1)} %pad_add_fusion.where_ref.refs_0_, s32[6,128]{1,0:T(8,128)} %bitcast.7, bf16[6,128]{1,0:T(8,128)(2,1)} %bitcast.10, ...), custom_call_target="tpu_custom_call" | custom-call | flops 1024 | bytes 1024 | tf_op jit(solution)/shard_map/route/pallas_call | solution.py:172
  3.7 3.0 %collective-permute-start = (bf16[64,3712]{1,0:T(8,128)(2,1)S(1)}, bf16[64,3712]{1,0:T(8,128)(2,1)S(1)}, u32[]{:S(2)}, u32[]{:S(2)}) collective-permute-start(bf16[64,3712]{1,0:T(8,128)(2,1)S(1)} %get-tuple-element.39), channel_id=1, source_target_pairs={{0,4},{4,0},{8,12},{12,8},{16,20},{20,16},{24,28},{28,24},{1,5},{5... | collective-permute-start | bytes 1425416 | tf_op jit(solution)/shard_map/ppermute | solution.py:563
  6.7 1.6 collective-permute-start.3
  8.3 3.0 %collective-permute-start.6 = (bf16[128,3712]{1,0:T(8,128)(2,1)S(1)}, bf16[128,3712]{1,0:T(8,128)(2,1)S(1)}, u32[]{:S(2)}, u32[]{:S(2)}) collective-permute-start(bf16[128,3712]{1,0:T(8,128)(2,1)S(1)} %get-tuple-element.40.refs_3_), channel_id=1, source_target_pairs={{0,16},{4,20},{8,24},{12,28},{16,0},{20,4},{24,8},{28,12},{1,17},{... | collective-permute-start | bytes 2850824 | tf_op jit(solution)/shard_map/ppermute | solution.py:563
  11.3 7.3 %load.1 = (bf16[2,1792,1024]{2,1,0:T(8,128)(2,1)S(1)}, bf16[2,1792,1024]{2,1,0:T(8,128)(2,1)S(1)}, bf16[2,1024,1792]{2,1,0:T(8,128)(2,1)S(1)}) custom-call(bf16[2,1792,1024]{2,1,0:T(8,128)(2,1)} %refs_0_.1, bf16[2,1792,1024]{2,1,0:T(8,128)(2,1)} %refs_1_.1, bf16[2,1024,1792]{2,1,0:T(8,128)(2,1)} %refs_2_.1, bf16[128,3712]{1,0:T(8,128)(2,1)S(1)} %get-tuple-element.40.refs_3_), custom_call_target="tpu_custom_call" | custom-call | flops 1024 | bytes 1024 | tf_op jit(solution)/shard_map/load/pallas_call | solution.py:32
  18.6 4.8 %project.4 = (f32[2,3,64,1024]{3,2,1,0:T(8,128)S(1)}, f32[2,3,64,1024]{3,2,1,0:T(8,128)S(1)}) custom-call(bf16[64,3712]{1,0:T(8,128)(2,1)S(1)} %get-tuple-element.38.refs_0_.refs_2_.refs_3_.refs_8_, bf16[64,3712]{1,0:T(8,128)(2,1)S(1)} %collective-permute-done.refs_1_.refs_3_.refs_4_.refs_9_, ...), custom_call_target="tpu_custom_call" | custom-call | flops 1024 | bytes 1024 | tf_op jit(solution)/shard_map/project/pallas_call | solution.py:32
  23.6 28.5 %collective-permute-done.6.refs_1_ = bf16[128,3712]{1,0:T(8,128)(2,1)S(1)} collective-permute-done((bf16[128,3712]{1,0:T(8,128)(2,1)S(1)}, bf16[128,3712]{1,0:T(8,128)(2,1)S(1)}, u32[]{:S(2)}, u32[]{:S(2)}) %collective-permute-start.6) | collective-permute-done | bytes 950304 | tf_op jit(solution)/shard_map/ppermute | solution.py:563
  53.0 1.6 collective-permute-start.2
  54.6 4.8 %project.5 = (f32[2,3,64,1024]{3,2,1,0:T(8,128)S(1)}, f32[2,3,64,1024]{3,2,1,0:T(8,128)S(1)}) custom-call(bf16[64,3712]{1,0:T(8,128)(2,1)S(1)} %collective-permute-done.3.refs_0_.refs_2_.refs_3_.refs_10_, bf16[64,3712]{1,0:T(8,128)(2,1)S(1)} %collective-permute-done.4.refs_1_.refs_3_.refs_4_.refs_11_, ...), custom_call_target="tpu_custom_call" | custom-call | flops 1024 | bytes 1024 | tf_op jit(solution)/shard_map/project/pallas_call | solution.py:32
  60.9 1.6 collective-permute-start.9
  63.7 9.8 %collective-permute-done.2.refs_2_ = bf16[2,3,64,1024]{3,2,1,0:T(8,128)(2,1)S(1)} collective-permute-done((bf16[2,3,64,1024]{3,2,1,0:T(8,128)(2,1)S(1)}, bf16[2,3,64,1024]{3,2,1,0:T(8,128)(2,1)S(1)}, u32[]{:S(2)}, u32[]{:S(2)}) %collective-permute-start.2) | collective-permute-done | bytes 786464 | tf_op jit(solution)/shard_map/ppermute | solution.py:558
  73.6 1.5 activate.4.refs_7_.refs_0_.refs_16_
  75.2 4.8 %project.6 = (f32[2,3,64,1024]{3,2,1,0:T(8,128)S(1)}, f32[2,3,64,1024]{3,2,1,0:T(8,128)S(1)}) custom-call(bf16[64,3712]{1,0:T(8,128)(2,1)S(1)} %get-tuple-element.50.refs_0_.refs_2_.refs_3_.refs_4_.refs_12_, bf16[64,3712]{1,0:T(8,128)(2,1)S(1)} %collective-permute-done.9.refs_1_.refs_3_.refs_4_.refs_5_.refs_13_, ...), custom_call_target="tpu_custom_call" | custom-call | flops 1024 | bytes 1024 | tf_op jit(solution)/shard_map/project/pallas_call | solution.py:32
  81.9 1.6 collective-permute-start.14
  83.8 1.6 collective-permute-start.16
  85.4 2.1 %collective-permute-done.8.refs_2_ = bf16[2,3,64,1024]{3,2,1,0:T(8,128)(2,1)S(1)} collective-permute-done((bf16[2,3,64,1024]{3,2,1,0:T(8,128)(2,1)S(1)}, bf16[2,3,64,1024]{3,2,1,0:T(8,128)(2,1)S(1)}, u32[]{:S(2)}, u32[]{:S(2)}) %collective-permute-start.8) | collective-permute-done | bytes 786464 | tf_op jit(solution)/shard_map/ppermute | solution.py:558
  87.5 1.5 activate.5.refs_4_.refs_0_.refs_18_
  89.1 5.3 %back.4 = (bf16[64,1920]{1,0:T(8,128)(2,1)S(1)}, bf16[64,1920]{1,0:T(8,128)(2,1)S(1)}) custom-call(bf16[2,64,3200]{2,1,0:T(8,128)(2,1)S(1)} %activate.4.refs_7_.refs_0_.refs_16_, bf16[2,64,3200]{2,1,0:T(8,128)(2,1)S(1)} %collective-permute-done.7.refs_1_.refs_17_, bf16[2,1792,1024]{2,1,0:T(8,128)(2,1)S(1)} %get-tuple-element.41.refs_4_.refs_7_.refs_2_, ...), custom_call_target="tpu_custom_call" | custom-call | flops 1024 | bytes 1024 | tf_op jit(solution)/shard_map/back/pallas_call | solution.py:32
  94.8 4.8 %project.7 = (f32[2,3,64,1024]{3,2,1,0:T(8,128)S(1)}, f32[2,3,64,1024]{3,2,1,0:T(8,128)S(1)}) custom-call(bf16[64,3712]{1,0:T(8,128)(2,1)S(1)} %get-tuple-element.54.refs_0_.refs_2_.refs_3_.refs_6_.refs_14_, bf16[64,3712]{1,0:T(8,128)(2,1)S(1)} %collective-permute-done.14.refs_1_.refs_3_.refs_4_.refs_7_.refs_15_, ...), custom_call_target="tpu_custom_call" | custom-call | flops 1024 | bytes 1024 | tf_op jit(solution)/shard_map/project/pallas_call | solution.py:32
  99.8 4.2 %collective-permute-done.16.refs_2_ = bf16[2,3,64,1024]{3,2,1,0:T(8,128)(2,1)S(1)} collective-permute-done((bf16[2,3,64,1024]{3,2,1,0:T(8,128)(2,1)S(1)}, bf16[2,3,64,1024]{3,2,1,0:T(8,128)(2,1)S(1)}, u32[]{:S(2)}, u32[]{:S(2)}) %collective-permute-start.16) | collective-permute-done | bytes 786464 | tf_op jit(solution)/shard_map/ppermute | solution.py:558
  104.1 1.5 activate.6.refs_2_.refs_0_.refs_20_
  105.9 1.6 collective-permute-start.22
  109.1 5.1 %back.5 = (bf16[64,1920]{1,0:T(8,128)(2,1)S(1)}, bf16[64,1920]{1,0:T(8,128)(2,1)S(1)}) custom-call(bf16[2,64,3200]{2,1,0:T(8,128)(2,1)S(1)} %activate.5.refs_4_.refs_0_.refs_18_, bf16[2,64,3200]{2,1,0:T(8,128)(2,1)S(1)} %collective-permute-done.13.refs_1_.refs_19_, bf16[2,1792,1024]{2,1,0:T(8,128)(2,1)S(1)} %get-tuple-element.41.refs_4_.refs_7_.refs_2_, ...), custom_call_target="tpu_custom_call" | custom-call | flops 1024 | bytes 1024 | tf_op jit(solution)/shard_map/back/pallas_call | solution.py:32
  116.2 5.3 %back.6 = (bf16[64,1920]{1,0:T(8,128)(2,1)S(1)}, bf16[64,1920]{1,0:T(8,128)(2,1)S(1)}) custom-call(bf16[2,64,3200]{2,1,0:T(8,128)(2,1)S(1)} %activate.6.refs_2_.refs_0_.refs_20_, bf16[2,64,3200]{2,1,0:T(8,128)(2,1)S(1)} %collective-permute-done.19.refs_1_.refs_21_, bf16[2,1792,1024]{2,1,0:T(8,128)(2,1)S(1)} %get-tuple-element.41.refs_4_.refs_7_.refs_2_, ...), custom_call_target="tpu_custom_call" | custom-call | flops 1024 | bytes 1024 | tf_op jit(solution)/shard_map/back/pallas_call | solution.py:32
  121.5 3.4 %collective-permute-start.20 = (bf16[64,1920]{1,0:T(8,128)(2,1)S(1)}, bf16[64,1920]{1,0:T(8,128)(2,1)S(1)}, u32[]{:S(2)}, u32[]{:S(2)}) collective-permute-start(bf16[64,1920]{1,0:T(8,128)(2,1)S(1)} %get-tuple-element.62.refs_5_), channel_id=1, source_target_pairs={{0,16},{4,20},{8,24},{12,28},{16,0},{20,4},{24,8},{28,12},{1,17},{... | collective-permute-start | bytes 737288 | tf_op jit(solution)/shard_map/ppermute | solution.py:563
  125.9 1.5 activate.7.refs_0_.refs_22_
  127.6 2.2 %collective-permute-done.23.refs_1_.refs_23_ = bf16[2,64,3200]{2,1,0:T(8,128)(2,1)S(1)} collective-permute-done((bf16[2,64,3200]{2,1,0:T(8,128)(2,1)S(1)}, bf16[2,64,3200]{2,1,0:T(8,128)(2,1)S(1)}, u32[]{:S(2)}, u32[]{:S(2)}) %collective-permute-start.23) | collective-permute-done | bytes 819232 | tf_op jit(solution)/shard_map/ppermute | solution.py:558
  129.9 4.3 %collective-permute-start.21 = (bf16[64,1920]{1,0:T(8,128)(2,1)S(1)}, bf16[64,1920]{1,0:T(8,128)(2,1)S(1)}, u32[]{:S(2)}, u32[]{:S(2)}) collective-permute-start(bf16[64,1920]{1,0:T(8,128)(2,1)S(1)} %get-tuple-element.63), channel_id=1, source_target_pairs={{0,20},{4,16},{8,28},{12,24},{16,4},{20,0},{24,12},{28,8},{1,21},{... | collective-permute-start | bytes 737288 | tf_op jit(solution)/shard_map/ppermute | solution.py:563
  134.2 5.1 %back.7 = (bf16[64,1920]{1,0:T(8,128)(2,1)S(1)}, bf16[64,1920]{1,0:T(8,128)(2,1)S(1)}) custom-call(bf16[2,64,3200]{2,1,0:T(8,128)(2,1)S(1)} %activate.7.refs_0_.refs_22_, bf16[2,64,3200]{2,1,0:T(8,128)(2,1)S(1)} %collective-permute-done.23.refs_1_.refs_23_, bf16[2,1792,1024]{2,1,0:T(8,128)(2,1)S(1)} %get-tuple-element.41.refs_4_.refs_7_.refs_2_, ...), custom_call_target="tpu_custom_call" | custom-call | flops 1024 | bytes 1024 | tf_op jit(solution)/shard_map/back/pallas_call | solution.py:32
  139.4 3.7 %collective-permute-start.25 = (bf16[64,1920]{1,0:T(8,128)(2,1)S(1)}, bf16[64,1920]{1,0:T(8,128)(2,1)S(1)}, u32[]{:S(2)}, u32[]{:S(2)}) collective-permute-start(bf16[64,1920]{1,0:T(8,128)(2,1)S(1)} %get-tuple-element.65), channel_id=1, source_target_pairs={{0,28},{4,24},{8,20},{12,16},{16,12},{20,8},{24,4},{28,0},{1,29},{... | collective-permute-start | bytes 737288 | tf_op jit(solution)/shard_map/ppermute | solution.py:563
  143.2 22.6 %weight_grads.1 = (bf16[2,1792,1024]{2,1,0:T(8,128)(2,1)}, bf16[2,1792,1024]{2,1,0:T(8,128)(2,1)}, bf16[2,1024,1792]{2,1,0:T(8,128)(2,1)}) custom-call(bf16[64,3712]{1,0:T(8,128)(2,1)S(1)} %get-tuple-element.38.refs_0_.refs_2_.refs_3_.refs_8_, bf16[64,3712]{1,0:T(8,128)(2,1)S(1)} %collective-permute-done.refs_1_.refs_3_.refs_4_.refs_9_, ...), custom_call_target="tpu_custom_call" | custom-call | flops 1024 | bytes 1024 | tf_op jit(solution)/shard_map/weight_grads/pallas_call | solution.py:32
  165.8 4.5 %unpack.1 = (bf16[128,1792]{1,0:T(8,128)(2,1)}, f32[6,128]{1,0:T(8,128)S(1)}) custom-call(s32[2]{0:T(128)S(1)} %pad_add_fusion.where_ref.refs_0_, s32[4,128]{1,0:T(4,128)S(1)} %bitcast.9, s32[6,128]{1,0:T(8,128)S(1)} %bitcast.8, bf16[64,1920]{1,0:T(8,128)(2,1)S(1)} %get-tuple-element.55.refs_7_.refs_0_, ...), custom_call_target="tpu_custom_call" | custom-call | flops 1024 | bytes 1024 | tf_op jit(solution)/shard_map/unpack/pallas_call | solution.py:241
  (100 shorter events, 12.4 us)
Async XLA Ops:
  3.7 14.9 %collective-permute-start = (bf16[64,3712]{1,0:T(8,128)(2,1)S(1)}, bf16[64,3712]{1,0:T(8,128)(2,1)S(1)}, u32[]{:S(2)}, u32[]{:S(2)}) collective-permute-start(bf16[64,3712]{1,0:T(8,128)(2,1)S(1)} %get-tuple-element.39), channel_id=1, source_target_pairs={{0,4},{4,0},{8,12},{12,8},{16,20},{20,16},{24,28},{28,24},{1,5},{5... | collective-permute-start | bytes 1425416 | tf_op jit(solution)/shard_map/ppermute | solution.py:563
  6.7 47.8 %collective-permute-start.3 = (bf16[64,3712]{1,0:T(8,128)(2,1)S(1)}, bf16[64,3712]{1,0:T(8,128)(2,1)S(1)}, u32[]{:S(2)}, u32[]{:S(2)}) collective-permute-start(bf16[64,3712]{1,0:T(8,128)(2,1)S(1)} %get-tuple-element.46), channel_id=1, source_target_pairs={{0,8},{4,12},{8,0},{12,4},{16,24},{20,28},{24,16},{28,20},{1,9},{5... | collective-permute-start | bytes 1425416 | tf_op jit(solution)/shard_map/ppermute | solution.py:563
  8.3 46.3 %collective-permute-start.4 = (bf16[64,3712]{1,0:T(8,128)(2,1)S(1)}, bf16[64,3712]{1,0:T(8,128)(2,1)S(1)}, u32[]{:S(2)}, u32[]{:S(2)}) collective-permute-start(bf16[64,3712]{1,0:T(8,128)(2,1)S(1)} %get-tuple-element.47), channel_id=1, source_target_pairs={{0,12},{4,8},{8,4},{12,0},{16,28},{20,24},{24,20},{28,16},{1,13},{... | collective-permute-start | bytes 1425416 | tf_op jit(solution)/shard_map/ppermute | solution.py:563
  8.3 43.7 %collective-permute-start.6 = (bf16[128,3712]{1,0:T(8,128)(2,1)S(1)}, bf16[128,3712]{1,0:T(8,128)(2,1)S(1)}, u32[]{:S(2)}, u32[]{:S(2)}) collective-permute-start(bf16[128,3712]{1,0:T(8,128)(2,1)S(1)} %get-tuple-element.40.refs_3_), channel_id=1, source_target_pairs={{0,16},{4,20},{8,24},{12,28},{16,0},{20,4},{24,8},{28,12},{1,17},{... | collective-permute-start | bytes 2850824 | tf_op jit(solution)/shard_map/ppermute | solution.py:563
  23.4 29.3 %collective-permute-start.1 = (f32[2,3,64,1024]{3,2,1,0:T(8,128)S(1)}, f32[2,3,64,1024]{3,2,1,0:T(8,128)S(1)}, u32[]{:S(2)}, u32[]{:S(2)}) collective-permute-start(f32[2,3,64,1024]{3,2,1,0:T(8,128)S(1)} %get-tuple-element.45), channel_id=1, source_target_pairs={{0,1},{1,0},{2,3},{3,2},{4,5},{5,4},{6,7},{7,6},{8,9},{9,8},{10,11... | collective-permute-start | bytes 4718600 | tf_op jit(solution)/shard_map/ppermute | solution.py:558
  52.0 28.5 %collective-permute-start.11 = (bf16[128,3712]{1,0:T(8,128)(2,1)S(1)}, bf16[128,3712]{1,0:T(8,128)(2,1)S(1)}, u32[]{:S(2)}, u32[]{:S(2)}) collective-permute-start(bf16[128,3712]{1,0:T(8,128)(2,1)S(1)} %collective-permute-done.6.refs_1_), channel_id=1, source_target_pairs={{0,8},{4,12},{8,0},{12,4},{16,24},{20,28},{24,16},{28,20},{1,9},{5... | collective-permute-start | bytes 2850824 | tf_op jit(solution)/shard_map/ppermute | solution.py:563
  53.0 20.5 %collective-permute-start.2 = (bf16[2,3,64,1024]{3,2,1,0:T(8,128)(2,1)S(1)}, bf16[2,3,64,1024]{3,2,1,0:T(8,128)(2,1)S(1)}, u32[]{:S(2)}, u32[]{:S(2)}) collective-permute-start(bf16[2,3,64,1024]{3,2,1,0:T(8,128)(2,1)S(1)} %add.11.refs_7_.refs_1_), channel_id=1, source_target_pairs={{0,2},{1,3},{2,0},{3,1},{4,6},{5,7},{6,4},{7,5},{8,10},{9,11},{10,... | collective-permute-start | bytes 2359304 | tf_op jit(solution)/shard_map/ppermute | solution.py:558
  59.4 3.5 %collective-permute-start.5 = (f32[2,3,64,1024]{3,2,1,0:T(8,128)S(1)}, f32[2,3,64,1024]{3,2,1,0:T(8,128)S(1)}, u32[]{:S(2)}, u32[]{:S(2)}) collective-permute-start(f32[2,3,64,1024]{3,2,1,0:T(8,128)S(1)} %get-tuple-element.49), channel_id=1, source_target_pairs={{0,1},{1,0},{2,3},{3,2},{4,5},{5,4},{6,7},{7,6},{8,9},{9,8},{10,11... | collective-permute-start | bytes 4718600 | tf_op jit(solution)/shard_map/ppermute | solution.py:558
  60.9 14.3 %collective-permute-start.9 = (bf16[64,3712]{1,0:T(8,128)(2,1)S(1)}, bf16[64,3712]{1,0:T(8,128)(2,1)S(1)}, u32[]{:S(2)}, u32[]{:S(2)}) collective-permute-start(bf16[64,3712]{1,0:T(8,128)(2,1)S(1)} %get-tuple-element.51), channel_id=1, source_target_pairs={{0,4},{4,0},{8,12},{12,8},{16,20},{20,16},{24,28},{28,24},{1,5},{5... | collective-permute-start | bytes 1425416 | tf_op jit(solution)/shard_map/ppermute | solution.py:563
  63.1 24.4 %collective-permute-start.8 = (bf16[2,3,64,1024]{3,2,1,0:T(8,128)(2,1)S(1)}, bf16[2,3,64,1024]{3,2,1,0:T(8,128)(2,1)S(1)}, u32[]{:S(2)}, u32[]{:S(2)}) collective-permute-start(bf16[2,3,64,1024]{3,2,1,0:T(8,128)(2,1)S(1)} %add.12.refs_5_.refs_1_), channel_id=1, source_target_pairs={{0,2},{1,3},{2,0},{3,1},{4,6},{5,7},{6,4},{7,5},{8,10},{9,11},{10,... | collective-permute-start | bytes 2359304 | tf_op jit(solution)/shard_map/ppermute | solution.py:558
  75.1 14.0 %collective-permute-start.7 = (bf16[2,64,3200]{2,1,0:T(8,128)(2,1)S(1)}, bf16[2,64,3200]{2,1,0:T(8,128)(2,1)S(1)}, u32[]{:S(2)}, u32[]{:S(2)}) collective-permute-start(bf16[2,64,3200]{2,1,0:T(8,128)(2,1)S(1)} %activate.4.refs_7_.refs_0_.refs_16_), channel_id=1, source_target_pairs={{0,1},{1,0},{2,3},{3,2},{4,5},{5,4},{6,7},{7,6},{8,9},{9,8},{10,11... | collective-permute-start | bytes 2457608 | tf_op jit(solution)/shard_map/ppermute | solution.py:558
  80.0 3.6 %collective-permute-start.10 = (f32[2,3,64,1024]{3,2,1,0:T(8,128)S(1)}, f32[2,3,64,1024]{3,2,1,0:T(8,128)S(1)}, u32[]{:S(2)}, u32[]{:S(2)}) collective-permute-start(f32[2,3,64,1024]{3,2,1,0:T(8,128)S(1)} %get-tuple-element.53), channel_id=1, source_target_pairs={{0,1},{1,0},{2,3},{3,2},{4,5},{5,4},{6,7},{7,6},{8,9},{9,8},{10,11... | collective-permute-start | bytes 4718600 | tf_op jit(solution)/shard_map/ppermute | solution.py:558
  81.9 12.9 %collective-permute-start.14 = (bf16[64,3712]{1,0:T(8,128)(2,1)S(1)}, bf16[64,3712]{1,0:T(8,128)(2,1)S(1)}, u32[]{:S(2)}, u32[]{:S(2)}) collective-permute-start(bf16[64,3712]{1,0:T(8,128)(2,1)S(1)} %get-tuple-element.57), channel_id=1, source_target_pairs={{0,4},{4,0},{8,12},{12,8},{16,20},{20,16},{24,28},{28,24},{1,5},{5... | collective-permute-start | bytes 1425416 | tf_op jit(solution)/shard_map/ppermute | solution.py:563
  83.8 20.2 %collective-permute-start.16 = (bf16[2,3,64,1024]{3,2,1,0:T(8,128)(2,1)S(1)}, bf16[2,3,64,1024]{3,2,1,0:T(8,128)(2,1)S(1)}, u32[]{:S(2)}, u32[]{:S(2)}) collective-permute-start(bf16[2,3,64,1024]{3,2,1,0:T(8,128)(2,1)S(1)} %add.13.refs_5_.refs_1_), channel_id=1, source_target_pairs={{0,2},{1,3},{2,0},{3,1},{4,6},{5,7},{6,4},{7,5},{8,10},{9,11},{10,... | collective-permute-start | bytes 2359304 | tf_op jit(solution)/shard_map/ppermute | solution.py:558
  89.0 20.0 %copy-start.1 = (bf16[2,64,3200]{2,1,0:T(8,128)(2,1)}, bf16[2,64,3200]{2,1,0:T(8,128)(2,1)S(1)}, u32[]{:S(2)}) copy-start(bf16[2,64,3200]{2,1,0:T(8,128)(2,1)S(1)} %activate.5.refs_4_.refs_0_.refs_18_) | copy-start | bytes 2457604
  89.0 20.0 %collective-permute-start.13 = (bf16[2,64,3200]{2,1,0:T(8,128)(2,1)S(1)}, bf16[2,64,3200]{2,1,0:T(8,128)(2,1)S(1)}, u32[]{:S(2)}, u32[]{:S(2)}) collective-permute-start(bf16[2,64,3200]{2,1,0:T(8,128)(2,1)S(1)} %activate.5.refs_4_.refs_0_.refs_18_), channel_id=1, source_target_pairs={{0,1},{1,0},{2,3},{3,2},{4,5},{5,4},{6,7},{7,6},{8,9},{9,8},{10,11... | collective-permute-start | bytes 2457608 | tf_op jit(solution)/shard_map/ppermute | solution.py:558
  99.6 6.0 %collective-permute-start.15 = (f32[2,3,64,1024]{3,2,1,0:T(8,128)S(1)}, f32[2,3,64,1024]{3,2,1,0:T(8,128)S(1)}, u32[]{:S(2)}, u32[]{:S(2)}) collective-permute-start(f32[2,3,64,1024]{3,2,1,0:T(8,128)S(1)} %get-tuple-element.59), channel_id=1, source_target_pairs={{0,1},{1,0},{2,3},{3,2},{4,5},{5,4},{6,7},{7,6},{8,9},{9,8},{10,11... | collective-permute-start | bytes 4718600 | tf_op jit(solution)/shard_map/ppermute | solution.py:558
  105.6 10.6 %copy-start = (bf16[2,64,3200]{2,1,0:T(8,128)(2,1)}, bf16[2,64,3200]{2,1,0:T(8,128)(2,1)S(1)}, u32[]{:S(2)}) copy-start(bf16[2,64,3200]{2,1,0:T(8,128)(2,1)S(1)} %activate.6.refs_2_.refs_0_.refs_20_) | copy-start | bytes 2457604
  105.6 10.6 %collective-permute-start.19 = (bf16[2,64,3200]{2,1,0:T(8,128)(2,1)S(1)}, bf16[2,64,3200]{2,1,0:T(8,128)(2,1)S(1)}, u32[]{:S(2)}, u32[]{:S(2)}) collective-permute-start(bf16[2,64,3200]{2,1,0:T(8,128)(2,1)S(1)} %activate.6.refs_2_.refs_0_.refs_20_), channel_id=1, source_target_pairs={{0,1},{1,0},{2,3},{3,2},{4,5},{5,4},{6,7},{7,6},{8,9},{9,8},{10,11... | collective-permute-start | bytes 2457608 | tf_op jit(solution)/shard_map/ppermute | solution.py:558
  105.9 20.0 %collective-permute-start.22 = (bf16[2,3,64,1024]{3,2,1,0:T(8,128)(2,1)S(1)}, bf16[2,3,64,1024]{3,2,1,0:T(8,128)(2,1)S(1)}, u32[]{:S(2)}, u32[]{:S(2)}) collective-permute-start(bf16[2,3,64,1024]{3,2,1,0:T(8,128)(2,1)S(1)} %add.14.refs_4_.refs_1_), channel_id=1, source_target_pairs={{0,2},{1,3},{2,0},{3,1},{4,6},{5,7},{6,4},{7,5},{8,10},{9,11},{10,... | collective-permute-start | bytes 2359304 | tf_op jit(solution)/shard_map/ppermute | solution.py:558
  107.5 31.8 %collective-permute-start.12 = (bf16[64,1920]{1,0:T(8,128)(2,1)S(1)}, bf16[64,1920]{1,0:T(8,128)(2,1)S(1)}, u32[]{:S(2)}, u32[]{:S(2)}) collective-permute-start(bf16[64,1920]{1,0:T(8,128)(2,1)S(1)} %get-tuple-element.56), channel_id=1, source_target_pairs={{0,4},{4,0},{8,12},{12,8},{16,20},{20,16},{24,28},{28,24},{1,5},{5... | collective-permute-start | bytes 737288 | tf_op jit(solution)/shard_map/ppermute | solution.py:563
  114.2 25.2 %collective-permute-start.17 = (bf16[64,1920]{1,0:T(8,128)(2,1)S(1)}, bf16[64,1920]{1,0:T(8,128)(2,1)S(1)}, u32[]{:S(2)}, u32[]{:S(2)}) collective-permute-start(bf16[64,1920]{1,0:T(8,128)(2,1)S(1)} %get-tuple-element.60.refs_4_), channel_id=1, source_target_pairs={{0,8},{4,12},{8,0},{12,4},{16,24},{20,28},{24,16},{28,20},{1,9},{5... | collective-permute-start | bytes 737288 | tf_op jit(solution)/shard_map/ppermute | solution.py:563
  115.1 50.7 %collective-permute-start.18 = (bf16[64,1920]{1,0:T(8,128)(2,1)S(1)}, bf16[64,1920]{1,0:T(8,128)(2,1)S(1)}, u32[]{:S(2)}, u32[]{:S(2)}) collective-permute-start(bf16[64,1920]{1,0:T(8,128)(2,1)S(1)} %get-tuple-element.61), channel_id=1, source_target_pairs={{0,12},{4,8},{8,4},{12,0},{16,28},{20,24},{24,20},{28,16},{1,13},{... | collective-permute-start | bytes 737288 | tf_op jit(solution)/shard_map/ppermute | solution.py:563
  121.5 44.2 %collective-permute-start.20 = (bf16[64,1920]{1,0:T(8,128)(2,1)S(1)}, bf16[64,1920]{1,0:T(8,128)(2,1)S(1)}, u32[]{:S(2)}, u32[]{:S(2)}) collective-permute-start(bf16[64,1920]{1,0:T(8,128)(2,1)S(1)} %get-tuple-element.62.refs_5_), channel_id=1, source_target_pairs={{0,16},{4,20},{8,24},{12,28},{16,0},{20,4},{24,8},{28,12},{1,17},{... | collective-permute-start | bytes 737288 | tf_op jit(solution)/shard_map/ppermute | solution.py:563
  127.5 6.8 %copy-start.2 = (bf16[2,64,3200]{2,1,0:T(8,128)(2,1)}, bf16[2,64,3200]{2,1,0:T(8,128)(2,1)S(1)}, u32[]{:S(2)}) copy-start(bf16[2,64,3200]{2,1,0:T(8,128)(2,1)S(1)} %activate.7.refs_0_.refs_22_) | copy-start | bytes 2457604
  127.5 2.4 %collective-permute-start.23 = (bf16[2,64,3200]{2,1,0:T(8,128)(2,1)S(1)}, bf16[2,64,3200]{2,1,0:T(8,128)(2,1)S(1)}, u32[]{:S(2)}, u32[]{:S(2)}) collective-permute-start(bf16[2,64,3200]{2,1,0:T(8,128)(2,1)S(1)} %activate.7.refs_0_.refs_22_), channel_id=1, source_target_pairs={{0,1},{1,0},{2,3},{3,2},{4,5},{5,4},{6,7},{7,6},{8,9},{9,8},{10,11... | collective-permute-start | bytes 2457608 | tf_op jit(solution)/shard_map/ppermute | solution.py:558
  129.9 9.4 %copy-start.5 = (bf16[2,64,3200]{2,1,0:T(8,128)(2,1)}, bf16[2,64,3200]{2,1,0:T(8,128)(2,1)S(1)}, u32[]{:S(2)}) copy-start(bf16[2,64,3200]{2,1,0:T(8,128)(2,1)S(1)} %collective-permute-done.23.refs_1_.refs_23_) | copy-start | bytes 2457604
  129.9 35.9 %collective-permute-start.21 = (bf16[64,1920]{1,0:T(8,128)(2,1)S(1)}, bf16[64,1920]{1,0:T(8,128)(2,1)S(1)}, u32[]{:S(2)}, u32[]{:S(2)}) collective-permute-start(bf16[64,1920]{1,0:T(8,128)(2,1)S(1)} %get-tuple-element.63), channel_id=1, source_target_pairs={{0,20},{4,16},{8,28},{12,24},{16,4},{20,0},{24,12},{28,8},{1,21},{... | collective-permute-start | bytes 737288 | tf_op jit(solution)/shard_map/ppermute | solution.py:563
  139.3 26.5 %collective-permute-start.24 = (bf16[64,1920]{1,0:T(8,128)(2,1)S(1)}, bf16[64,1920]{1,0:T(8,128)(2,1)S(1)}, u32[]{:S(2)}, u32[]{:S(2)}) collective-permute-start(bf16[64,1920]{1,0:T(8,128)(2,1)S(1)} %get-tuple-element.64.refs_24_), channel_id=1, source_target_pairs={{0,24},{4,28},{8,16},{12,20},{16,8},{20,12},{24,0},{28,4},{1,25},{... | collective-permute-start | bytes 737288 | tf_op jit(solution)/shard_map/ppermute | solution.py:563
  139.4 26.4 %copy-start.6 = (s32[128,6]{0,1:T(8,128)S(1)}, s32[128,6]{0,1:T(8,128)}, u32[]{:S(2)}) copy-start(s32[128,6]{0,1:T(8,128)} %param.11) | copy-start | bytes 9220
  139.4 26.4 %copy-start.7 = (s32[128,4]{0,1:T(4,128)S(1)}, s32[128,4]{0,1:T(4,128)}, u32[]{:S(2)}) copy-start(s32[128,4]{0,1:T(4,128)} %param.12) | copy-start | bytes 6148
  139.4 26.4 %collective-permute-start.25 = (bf16[64,1920]{1,0:T(8,128)(2,1)S(1)}, bf16[64,1920]{1,0:T(8,128)(2,1)S(1)}, u32[]{:S(2)}, u32[]{:S(2)}) collective-permute-start(bf16[64,1920]{1,0:T(8,128)(2,1)S(1)} %get-tuple-element.65), channel_id=1, source_target_pairs={{0,28},{4,24},{8,20},{12,16},{16,12},{20,8},{24,4},{28,0},{1,29},{... | collective-permute-start | bytes 737288 | tf_op jit(solution)/shard_map/ppermute | solution.py:563
  (2 other events, 10.4 us)

commit v4 on v3

--- a/solution.py
+++ b/solution.py
@@ -57,11 +57,15 @@
     return pltpu.with_memory_space_constraint(array, pltpu.HBM)
 
 
-def fetch(pairs, sems):
+def begin(pairs, sems):
     copies = [pltpu.make_async_copy(src, dst, sems.at[i]) for i, (src, dst) in enumerate(pairs)]
     for copy in copies:
         copy.start()
-    for copy in copies:
+    return copies
+
+
+def fetch(pairs, sems):
+    for copy in begin(pairs, sems):
         copy.wait()
 
 
@@ -186,28 +190,12 @@
     return outs[0], list(outs[1:])
 
 
-def relay_kernel(in_ref, out_ref):
-    out_ref[...] = in_ref[...]
-
-
-def relay(array, deps):
-    return call(
-        relay_kernel,
-        deps,
-        [array],
-        [IN_VMEM],
-        out_specs=IN_VMEM,
-        out_shape=jax.ShapeDtypeStruct(array.shape, array.dtype),
-        compiler_params=params(4),
-        cost_estimate=CHEAP,
-        name="relay",
-    )
-
-
 def unpack_kernel(where_ref, groups_ref, ids_ref, *refs):
     blocks, (grad_ref, gate_ref, rows, place_ref, sems) = refs[:-5], refs[-5:]
     size = blocks[0].shape[0]
     tokens, width = grad_ref.shape
+    pieces = [rows.at[index * size : (index + 1) * size] for index in range(len(blocks))]
+    copies = begin(list(zip(blocks, pieces)), sems)
     me, flip = where_ref[0], where_ref[1]
     peers = me ^ lax.broadcasted_iota(jnp.int32, place_ref.shape, 0)
     member = jnp.zeros(place_ref.shape, F32)
@@ -221,14 +209,14 @@
     ).astype(BF)
     rank = dot_nn(member.astype(BF), earlier).astype(jnp.int32)
     place_ref[...] = jnp.where(member > 0.0, rank ^ flip, -1)
-    pieces = [rows.at[index * size : (index + 1) * size] for index in range(len(blocks))]
-    fetch(list(zip(blocks, pieces)), sems)
     hot = join([hot_block(place_ref, index, size) for index in range(len(blocks))])
-    contract = (((0,), (0,)), ((), ()))
-    grad_ref[...] = lax.dot_general(
-        hot, rows[:, :width], contract, preferred_element_type=F32
-    ).astype(BF)
-    terms = lax.dot_general(rows[:, width:], hot, contract, preferred_element_type=F32)
+    hot_t = hot.T
+    for copy in copies:
+        copy.wait()
+    grad_ref[...] = dot_nn(hot_t, rows[:, :width]).astype(BF)
+    terms = lax.dot_general(
+        rows[:, width:], hot, (((0,), (0,)), ((), ())), preferred_element_type=F32
+    )
     expert = lax.broadcasted_iota(jnp.int32, (LANES, tokens), 0)
     for index in range(ids_ref.shape[0]):
         chosen = jnp.where(ids_ref[index : index + 1, :] == expert, terms, 0.0)
@@ -454,7 +442,64 @@
     )
 
 
-def grads_kernel(groups, *refs):
+def gather_kernel(groups, *refs):
+    blocks = sum(groups)
+    acts = refs[blocks:-7]
+    rows_t, grads, gate_acts, up_acts, hidden_t, rows_ref, sems = refs[-7:]
+    width, hid = rows_t.shape[0], gate_acts.shape[2]
+    pairs, first, row = [], 0, 0
+    for count in groups:
+        half = refs[first].shape[0] // 2
+        for place in range(2):
+            for index in range(count):
+                block = refs[first + index].at[place * half : (place + 1) * half]
+                pairs.append((block.at[:, :width], rows_ref.at[row : row + half]))
+                pairs.append((block.at[:, width : 2 * width], grads.at[row : row + half]))
+                row += half
+        first += count
+    copies = begin(pairs, sems)
+    for e in range(gate_acts.shape[0]):
+        row = 0
+        for ref in acts:
+            rows = slice(row, row + ref.shape[1])
+            gate_acts[e, rows] = ref[e, :, :hid]
+            up_acts[e, rows] = ref[e, :, hid : 2 * hid]
+            hidden_t[e, :, rows] = ref[e, :, 2 * hid : 3 * hid].T
+            row += ref.shape[1]
+    for copy in copies:
+        copy.wait()
+    rows_t[...] = rows_ref[...].T
+
+
+def gather_rows(blocks, acts, groups, width, deps):
+    size = blocks[0].shape[0]
+    experts = acts[0].shape[0]
+    hid = (acts[0].shape[2] - LANES) // 3
+    rows = size * len(blocks)
+    return call(
+        functools.partial(gather_kernel, groups),
+        deps,
+        [*blocks, *acts],
+        [ANYWHERE] * len(blocks) + [IN_VMEM] * len(acts),
+        out_specs=[IN_VMEM] * 5,
+        out_shape=[
+            jax.ShapeDtypeStruct((width, rows), BF),
+            jax.ShapeDtypeStruct((rows, width), BF),
+            jax.ShapeDtypeStruct((experts, rows, hid), BF),
+            jax.ShapeDtypeStruct((experts, rows, hid), BF),
+            jax.ShapeDtypeStruct((experts, hid, rows), BF),
+        ],
+        scratch_shapes=[
+            pltpu.VMEM((rows, width), BF),
+            pltpu.SemaphoreType.DMA((4 * len(blocks),)),
+        ],
+        compiler_params=params(20),
+        cost_estimate=CHEAP,
+        name="gather_rows",
+    )
+
+
+def grads_kernel(groups, first_t, first_grads, first_gate, first_up, first_hidden, *refs):
     blocks = sum(groups)
     acts = refs[2 * blocks : -6]
     out_gate, out_up, out_down, gate_acts, up_acts, hidden_t = refs[-6:]
@@ -483,20 +528,25 @@
     rows_t = rows_of(refs[:blocks]).T
     grads = rows_of(refs[blocks : 2 * blocks])
     for e in range(experts):
-        out_gate[e] = dot_nn(rows_t, gate_acts[e]).astype(BF)
-        out_up[e] = dot_nn(rows_t, up_acts[e]).astype(BF)
-        out_down[e] = dot_nn(hidden_t[e], grads).astype(BF)
-
-
-def weight_grads(ins, grads, starts, width, acts, groups, deps):
-    size = ins[0].shape[0]
+        gate = dot_nn(first_t[...], first_gate[e]) + dot_nn(rows_t, gate_acts[e])
+        out_gate[e] = gate.astype(BF)
+        up = dot_nn(first_t[...], first_up[e]) + dot_nn(rows_t, up_acts[e])
+        out_up[e] = up.astype(BF)
+        down = dot_nn(first_hidden[e], first_grads[...]) + dot_nn(hidden_t[e], grads)
+        out_down[e] = down.astype(BF)
+
+
+def weight_grads(gathered, blocks, acts, groups, width, deps):
+    size = blocks[0].shape[0]
     experts = acts[0].shape[0]
     hid = (acts[0].shape[2] - LANES) // 3
-    rows = size * len(ins)
+    rows = size * len(blocks)
     tile = tile_of(width, 256)
-
-    def row_spec(start):
-        return pl.BlockSpec((size, tile), lambda j: (0, start // tile + j))
+    steps = width // tile
+    before = gathered[1].shape[0]
+
+    def fixed(array):
+        return pl.BlockSpec(array.shape, lambda j: (0, 0, 0))
 
     wide = pl.BlockSpec((experts, tile, hid), lambda j: (0, j, 0))
     down = pl.BlockSpec((experts, hid, tile), lambda j: (0, 0, j))
@@ -504,11 +554,16 @@
     return call(
         functools.partial(grads_kernel, groups),
         deps,
-        [*ins, *grads, *acts],
-        [row_spec(0) for _ in ins]
-        + [row_spec(start) for start in starts]
-        + [pl.BlockSpec(act.shape, lambda j: (0, 0, 0)) for act in acts],
-        grid=(width // tile,),
+        [*gathered, *blocks, *blocks, *acts],
+        [
+            pl.BlockSpec((tile, before), lambda j: (j, 0)),
+            pl.BlockSpec((before, tile), lambda j: (0, j)),
+            *[fixed(array) for array in gathered[2:]],
+        ]
+        + [pl.BlockSpec((size, tile), lambda j: (0, j)) for _ in blocks]
+        + [pl.BlockSpec((size, tile), lambda j: (0, steps + j)) for _ in blocks]
+        + [fixed(act) for act in acts],
+        grid=(steps,),
         out_specs=[wide, wide, down],
         out_shape=[wide_shape, wide_shape, jax.ShapeDtypeStruct((experts, hid, width), BF)],
         scratch_shapes=[
@@ -551,7 +606,8 @@
     core = lax.axis_index("local") % 2
     where = jnp.stack([me, core * (capacity // 2)]).astype(jnp.int32)
     quarter = nodes // 4
-    spans = [range(group * quarter, (group + 1) * quarter) for group in range(4)]
+    cuts = [0, quarter, 2 * quarter, 3 * quarter, nodes]
+    spans = [range(start, end) for start, end in zip(cuts, cuts[1:])]
     own, near, mid, far = range(4)
 
     def swap(value, step):
@@ -569,10 +625,14 @@
     def send(blocks, masks):
         return [cross(block, mask) for block, mask in zip(blocks, masks)]
 
-    def select_step(group, whole):
-        blocks = select(where, whole, experts, quarter, capacity, last)
+    def select_step():
+        blocks = select(where, mid_whole, experts, 2 * quarter, capacity, last)
         last[:] = [blocks[0]]
-        rows[group] = send(blocks, spans[0])
+        rows[mid] = send(blocks[:quarter], spans[own])
+        passed = send(blocks[quarter:], spans[near])
+        for group in range(far, len(spans)):
+            first = 3 * quarter
+            rows[group] = passed[spans[group][0] - first : spans[group][-1] + 1 - first]
 
     def pause(count):
         for _ in range(count):
@@ -603,13 +663,25 @@
     def settle(arrays):
         last[:] = [mark([*last, *arrays])]
 
+    def gather_step():
+        blocks = [block for group in rows[:2] for block in group]
+        arrays = gather_rows(
+            blocks,
+            [part for pair in acts[:2] for part in pair],
+            [len(span) for span in spans[:2]],
+            width,
+            last,
+        )
+        last[:] = [arrays[0]]
+        return arrays
+
     def back_step(group):
         blocks = back(*acts[group], v_gate, v_up, len(spans[group]), last)
         last[:] = [blocks[0]]
         for mask, block in zip(spans[group], send(blocks, spans[group])):
             returned[mask] = block
 
-    rows, sums, acts = [[None] * 4 for _ in range(3)]
+    rows, sums, acts = [[None] * len(spans) for _ in range(3)]
     returned = [None] * nodes
     whole, blocks = route(
         where, ids_t, gate_weight.T, hidden_in, out_grad, experts, 2 * quarter, capacity
@@ -618,44 +690,42 @@
     rows[own] = send(blocks[:quarter], spans[own])
     rows[near] = send(blocks[quarter:], spans[near])
     mid_whole = cross(whole, 2 * quarter)
-    far_whole = cross(mid_whole, quarter)
     mats = load((w_gate, w_up, w_down), last)
     v_gate, v_up, v_down = mats
     last[:] = [v_gate]
 
-    parts = [None] * 4
+    parts = [None] * len(spans)
     parts[own] = whole_project(own)
     pause(8)
     sums[own] = sum_step(*parts[own])
     parts[near] = whole_project(near)
-    select_step(mid, mid_whole)
+    select_step()
     pause(8)
     sums[near] = sum_step(*parts[near])
     act_step(own)
     parts[mid] = whole_project(mid)
-    select_step(far, far_whole)
     pause(8)
     sums[mid] = sum_step(*parts[mid])
+    parts[far] = whole_project(far)
     act_step(near)
     back_step(own)
-    parts[far] = whole_project(far)
     pause(8)
+    back_step(near)
     act_step(mid)
     sums[far] = sum_step(*parts[far])
-    back_step(near)
     back_step(mid)
+    gathered = gather_step()
+    settle([returned[mask] for mask in spans[near]])
     act_step(far)
     pause(8)
     back_step(far)
 
-    blocks = [block for group in rows for block in group]
     grad_w_gate, grad_w_up, grad_w_down = weight_grads(
-        blocks,
-        blocks,
-        [width] * nodes,
+        gathered,
+        [block for group in rows[2:] for block in group],
+        [part for pair in acts[2:] for part in pair],
+        [len(span) for span in spans[2:]],
         width,
-        [part for pair in acts for part in pair],
-        [len(span) for span in spans],
         last,
     )
     grad_input, grad_gate = unpack(where, group_ids.T, ids_t, returned)

time: 171 us -> 159 us (0.930)
  waiting for transfers between devices: 48.7 us -> 39.5 us
  Pallas kernels: 87.2 us -> 85.3 us
    ppermute x12, waiting for transfers between devices: 19.8 us -> 11.4 us  [swap(): return lax.ppermute(value, 'local', [(i, i ^ step) for i in range(shares)])]
    ppermute x14, starting transfers between devices: 26.6 us -> 24.6 us  [cross(): return lax.ppermute(value, 'node', [(i, i ^ mask) for i in range(nodes)])]
    pallas_call x60 -> x61, Pallas kernels: 79.7 us -> 77.8 us  [call(): pl.pallas_call(body, in_specs=list(in_specs) + [ANYWHERE] * extra, **sett...]
  transfers between devices with their start and end apart: 26 -> 26, of which waited for: 8 -> 9; matrix products, arithmetic and copies ran while one was open for 0% -> 0% of each run, Pallas kernels for 47% -> 49%
where the time goes in v4:
time: 159 us
  Pallas kernels  85.3 us (54%)
  waiting for transfers between devices  39.5 us (25%)
  starting transfers between devices  31.7 us (20%)
    pallas_call x61, Pallas kernels, call(): pl.pallas_call(body, in_specs=list(in_specs) + [ANYWHERE] * extra, **sett...  77.8 us
    ppermute x14, waiting for transfers between devices, cross(): return lax.ppermute(value, 'node', [(i, i ^ mask) for i in range(nodes)])  28.1 us
    ppermute x14, starting transfers between devices, cross(): return lax.ppermute(value, 'node', [(i, i ^ mask) for i in range(nodes)])  24.6 us
    ppermute x12, waiting for transfers between devices, swap(): return lax.ppermute(value, 'local', [(i, i ^ step) for i in range(shares)])  11.4 us
    ppermute x12, starting transfers between devices, swap(): return lax.ppermute(value, 'local', [(i, i ^ step) for i in range(shares)])  7.16 us
    pallas_call x1, Pallas kernels, unpack(): pl.pallas_call(unpack_kernel, in_specs=[IN_SMEM, IN_VMEM, IN_VMEM] + [ANY...  4.6 us
  transfers between devices with their start and end apart: 26, of which 9 were waited for; matrix products, arithmetic and copies ran while one was open for 0% of the time, Pallas kernels for 49%

profile of v4, /device:TPU:0, one launch (start us, length us, event | category | flops | bytes accessed | tf_op | source)
XLA Modules:
  0.0 158.6 jit_solution(8935829481208629757)
XLA Ops:
  0.7 3.0 %route.1 = (bf16[128,3712]{1,0:T(8,128)(2,1)S(1)}, bf16[64,3712]{1,0:T(8,128)(2,1)S(1)}, bf16[64,3712]{1,0:T(8,128)(2,1)S(1)}, bf16[64,3712]{1,0:T(8,128)(2,1)S(1)}, bf16[64,3712]{1,0:T(8,128)(2,1)S(1)}) custom-call(s32[2]{0:T(128)S(1)} %pad_add_fusion.where_ref.refs_0_, s32[6,128]{1,0:T(8,128)} %bitcast.7, bf16[6,128]{1,0:T(8,128)(2,1)} %bitcast.10, ...), custom_call_target="tpu_custom_call" | custom-call | flops 1024 | bytes 1024 | tf_op jit(solution)/shard_map/route/pallas_call | solution.py:176
  3.7 3.0 %collective-permute-start = (bf16[64,3712]{1,0:T(8,128)(2,1)S(1)}, bf16[64,3712]{1,0:T(8,128)(2,1)S(1)}, u32[]{:S(2)}, u32[]{:S(2)}) collective-permute-start(bf16[64,3712]{1,0:T(8,128)(2,1)S(1)} %get-tuple-element.44), channel_id=1, source_target_pairs={{0,4},{4,0},{8,12},{12,8},{16,20},{20,16},{24,28},{28,24},{1,5},{5... | collective-permute-start | bytes 1425416 | tf_op jit(solution)/shard_map/ppermute | solution.py:619
  6.7 1.6 collective-permute-start.3
  8.3 3.0 %collective-permute-start.6 = (bf16[128,3712]{1,0:T(8,128)(2,1)S(1)}, bf16[128,3712]{1,0:T(8,128)(2,1)S(1)}, u32[]{:S(2)}, u32[]{:S(2)}) collective-permute-start(bf16[128,3712]{1,0:T(8,128)(2,1)S(1)} %get-tuple-element.45.refs_3_), channel_id=1, source_target_pairs={{0,16},{4,20},{8,24},{12,28},{16,0},{20,4},{24,8},{28,12},{1,17},{... | collective-permute-start | bytes 2850824 | tf_op jit(solution)/shard_map/ppermute | solution.py:619
  11.3 7.3 %load.1 = (bf16[2,1792,1024]{2,1,0:T(8,128)(2,1)S(1)}, bf16[2,1792,1024]{2,1,0:T(8,128)(2,1)S(1)}, bf16[2,1024,1792]{2,1,0:T(8,128)(2,1)S(1)}) custom-call(bf16[2,1792,1024]{2,1,0:T(8,128)(2,1)} %refs_0_.1, bf16[2,1792,1024]{2,1,0:T(8,128)(2,1)} %refs_1_.1, bf16[2,1024,1792]{2,1,0:T(8,128)(2,1)} %refs_2_.1, bf16[128,3712]{1,0:T(8,128)(2,1)S(1)} %get-tuple-element.45.refs_3_), custom_call_target="tpu_custom_call" | custom-call | flops 1024 | bytes 1024 | tf_op jit(solution)/shard_map/load/pallas_call | solution.py:32
  18.6 4.8 %project.4 = (f32[2,3,64,1024]{3,2,1,0:T(8,128)S(1)}, f32[2,3,64,1024]{3,2,1,0:T(8,128)S(1)}) custom-call(bf16[64,3712]{1,0:T(8,128)(2,1)S(1)} %get-tuple-element.43.refs_0_.refs_2_.refs_3_, bf16[64,3712]{1,0:T(8,128)(2,1)S(1)} %collective-permute-done.refs_1_.refs_3_.refs_4_, bf16[64,3712]{1,0:T(8,128)(2,1)S(1)} %get-tuple-element.43.refs_0_.refs_2_.refs_3_, ...), custom_call_target="tpu_custom_call" | custom-call | flops 1024 | bytes 1024 | tf_op jit(solution)/shard_map/project/pallas_call | solution.py:32
  23.6 3.3 %collective-permute-done.1.refs_1_ = f32[2,3,64,1024]{3,2,1,0:T(8,128)S(1)} collective-permute-done((f32[2,3,64,1024]{3,2,1,0:T(8,128)S(1)}, f32[2,3,64,1024]{3,2,1,0:T(8,128)S(1)}, u32[]{:S(2)}, u32[]{:S(2)}) %collective-permute-start.1) | collective-permute-done | bytes 1572896 | tf_op jit(solution)/shard_map/ppermute | solution.py:614
  27.1 1.5 collective-permute-start.2
  28.7 12.0 %collective-permute-done.3.refs_0_.refs_2_.refs_3_ = bf16[64,3712]{1,0:T(8,128)(2,1)S(1)} collective-permute-done((bf16[64,3712]{1,0:T(8,128)(2,1)S(1)}, bf16[64,3712]{1,0:T(8,128)(2,1)S(1)}, u32[]{:S(2)}, u32[]{:S(2)}) %collective-permute-start.3) | collective-permute-done | bytes 475168 | tf_op jit(solution)/shard_map/ppermute | solution.py:619
  40.7 7.4 %collective-permute-done.4.refs_1_.refs_3_.refs_4_ = bf16[64,3712]{1,0:T(8,128)(2,1)S(1)} collective-permute-done((bf16[64,3712]{1,0:T(8,128)(2,1)S(1)}, bf16[64,3712]{1,0:T(8,128)(2,1)S(1)}, u32[]{:S(2)}, u32[]{:S(2)}) %collective-permute-start.4) | collective-permute-done | bytes 475168 | tf_op jit(solution)/shard_map/ppermute | solution.py:619
  48.2 4.8 %project.5 = (f32[2,3,64,1024]{3,2,1,0:T(8,128)S(1)}, f32[2,3,64,1024]{3,2,1,0:T(8,128)S(1)}) custom-call(bf16[64,3712]{1,0:T(8,128)(2,1)S(1)} %collective-permute-done.3.refs_0_.refs_2_.refs_3_, bf16[64,3712]{1,0:T(8,128)(2,1)S(1)} %collective-permute-done.4.refs_1_.refs_3_.refs_4_, bf16[64,3712]{1,0:T(8,128)(2,1)S(1)} %collective-permute-done.3.refs_0_.refs_2_.refs_3_, ...), custom_call_target="tpu_custom_call" | custom-call | flops 1024 | bytes 1024 | tf_op jit(solution)/shard_map/project/pallas_call | solution.py:32
  53.0 1.6 %select.3 = (bf16[64,3712]{1,0:T(8,128)(2,1)S(1)}, bf16[64,3712]{1,0:T(8,128)(2,1)S(1)}, bf16[64,3712]{1,0:T(8,128)(2,1)S(1)}, bf16[64,3712]{1,0:T(8,128)(2,1)S(1)}) custom-call(s32[2]{0:T(128)S(1)} %pad_add_fusion.where_ref.refs_0_, bf16[128,3712]{1,0:T(8,128)(2,1)S(1)} %collective-permute-done.6.refs_1_, ...), custom_call_target="tpu_custom_call" | custom-call | flops 1024 | bytes 1024 | tf_op jit(solution)/shard_map/select/pallas_call | solution.py:32
  54.7 2.8 %collective-permute-start.11 = (bf16[64,3712]{1,0:T(8,128)(2,1)S(1)}, bf16[64,3712]{1,0:T(8,128)(2,1)S(1)}, u32[]{:S(2)}, u32[]{:S(2)}) collective-permute-start(bf16[64,3712]{1,0:T(8,128)(2,1)S(1)} %get-tuple-element.58), channel_id=1, source_target_pairs={{0,4},{4,0},{8,12},{12,8},{16,20},{20,16},{24,28},{28,24},{1,5},{5... | collective-permute-start | bytes 1425416 | tf_op jit(solution)/shard_map/ppermute | solution.py:619
  57.5 1.5 collective-permute-start.10
  60.9 1.5 activate.4.refs_7_.refs_0_.refs_4_
  62.5 6.6 %collective-permute-done.11.refs_1_.refs_3_.refs_4_.refs_6_.refs_10_ = bf16[64,3712]{1,0:T(8,128)(2,1)S(1)} collective-permute-done((bf16[64,3712]{1,0:T(8,128)(2,1)S(1)}, bf16[64,3712]{1,0:T(8,128)(2,1)S(1)}, u32[]{:S(2)}, u32[]{:S(2)}) %collective-permute-start.11) | collective-permute-done | bytes 475168 | tf_op jit(solution)/shard_map/ppermute | solution.py:619
  69.1 4.8 %project.6 = (f32[2,3,64,1024]{3,2,1,0:T(8,128)S(1)}, f32[2,3,64,1024]{3,2,1,0:T(8,128)S(1)}) custom-call(bf16[64,3712]{1,0:T(8,128)(2,1)S(1)} %get-tuple-element.55.refs_0_.refs_2_.refs_3_.refs_5_.refs_9_, bf16[64,3712]{1,0:T(8,128)(2,1)S(1)} %collective-permute-done.11.refs_1_.refs_3_.refs_4_.refs_6_.refs_10_, ...), custom_call_target="tpu_custom_call" | custom-call | flops 1024 | bytes 1024 | tf_op jit(solution)/shard_map/project/pallas_call | solution.py:32
  74.0 3.3 %collective-permute-done.12.refs_1_ = f32[2,3,64,1024]{3,2,1,0:T(8,128)S(1)} collective-permute-done((f32[2,3,64,1024]{3,2,1,0:T(8,128)S(1)}, f32[2,3,64,1024]{3,2,1,0:T(8,128)S(1)}, u32[]{:S(2)}, u32[]{:S(2)}) %collective-permute-start.12) | collective-permute-done | bytes 1572896 | tf_op jit(solution)/shard_map/ppermute | solution.py:614
  80.5 5.0 %project.7 = (f32[2,3,64,1024]{3,2,1,0:T(8,128)S(1)}, f32[2,3,64,1024]{3,2,1,0:T(8,128)S(1)}) custom-call(bf16[64,3712]{1,0:T(8,128)(2,1)S(1)} %collective-permute-done.9.refs_0_.refs_2_.refs_3_.refs_7_.refs_11_, bf16[64,3712]{1,0:T(8,128)(2,1)S(1)} %collective-permute-done.10.refs_1_.refs_3_.refs_4_.refs_8_.refs_12_, ...), custom_call_target="tpu_custom_call" | custom-call | flops 1024 | bytes 1024 | tf_op jit(solution)/shard_map/project/pallas_call | solution.py:32
  85.5 1.5 activate.5.refs_4_.refs_0_.refs_6_
  87.1 5.1 %back.4 = (bf16[64,1920]{1,0:T(8,128)(2,1)S(1)}, bf16[64,1920]{1,0:T(8,128)(2,1)S(1)}) custom-call(bf16[2,64,3200]{2,1,0:T(8,128)(2,1)S(1)} %activate.4.refs_7_.refs_0_.refs_4_, bf16[2,64,3200]{2,1,0:T(8,128)(2,1)S(1)} %collective-permute-done.7.refs_1_.refs_5_, bf16[2,1792,1024]{2,1,0:T(8,128)(2,1)S(1)} %get-tuple-element.46.refs_4_.refs_7_.refs_2_, ...), custom_call_target="tpu_custom_call" | custom-call | flops 1024 | bytes 1024 | tf_op jit(solution)/shard_map/back/pallas_call | solution.py:32
  92.8 5.1 %back.5 = (bf16[64,1920]{1,0:T(8,128)(2,1)S(1)}, bf16[64,1920]{1,0:T(8,128)(2,1)S(1)}) custom-call(bf16[2,64,3200]{2,1,0:T(8,128)(2,1)S(1)} %activate.5.refs_4_.refs_0_.refs_6_, bf16[2,64,3200]{2,1,0:T(8,128)(2,1)S(1)} %collective-permute-done.14.refs_1_.refs_7_, bf16[2,1792,1024]{2,1,0:T(8,128)(2,1)S(1)} %get-tuple-element.46.refs_4_.refs_7_.refs_2_, ...), custom_call_target="tpu_custom_call" | custom-call | flops 1024 | bytes 1024 | tf_op jit(solution)/shard_map/back/pallas_call | solution.py:32
  101.6 2.9 %collective-permute-start.16 = (bf16[64,1920]{1,0:T(8,128)(2,1)S(1)}, bf16[64,1920]{1,0:T(8,128)(2,1)S(1)}, u32[]{:S(2)}, u32[]{:S(2)}) collective-permute-start(bf16[64,1920]{1,0:T(8,128)(2,1)S(1)} %get-tuple-element.65), channel_id=1, source_target_pairs={{0,12},{4,8},{8,4},{12,0},{16,28},{20,24},{24,20},{28,16},{1,13},{... | collective-permute-start | bytes 737288 | tf_op jit(solution)/shard_map/ppermute | solution.py:619
  104.8 5.3 %back.6 = (bf16[64,1920]{1,0:T(8,128)(2,1)S(1)}, bf16[64,1920]{1,0:T(8,128)(2,1)S(1)}) custom-call(bf16[2,64,3200]{2,1,0:T(8,128)(2,1)S(1)} %activate.6.refs_2_.refs_0_.refs_13_, bf16[2,64,3200]{2,1,0:T(8,128)(2,1)S(1)} %collective-permute-done.18.refs_1_.refs_14_, bf16[2,1792,1024]{2,1,0:T(8,128)(2,1)S(1)} %get-tuple-element.46.refs_4_.refs_7_.refs_2_, ...), custom_call_target="tpu_custom_call" | custom-call | flops 1024 | bytes 1024 | tf_op jit(solution)/shard_map/back/pallas_call | solution.py:32
  110.4 2.2 %gather_rows.1 = (bf16[1792,256]{1,0:T(8,128)(2,1)S(1)}, bf16[256,1792]{1,0:T(8,128)(2,1)S(1)}, bf16[2,256,1024]{2,1,0:T(8,128)(2,1)S(1)}, bf16[2,256,1024]{2,1,0:T(8,128)(2,1)S(1)}, bf16[2,1024,256]{2,1,0:T(8,128)(2,1)S(1)}) custom-call(bf16[64,3712]{1,0:T(8,128)(2,1)S(1)} %get-tuple-element.43.refs_0_.refs_2_.refs_3_, ...), custom_call_target="tpu_custom_call" | custom-call | flops 1024 | bytes 1024 | tf_op jit(solution)/shard_map/gather_rows/pallas_call | solution.py:32
  112.7 3.9 %collective-permute-start.21 = (bf16[64,1920]{1,0:T(8,128)(2,1)S(1)}, bf16[64,1920]{1,0:T(8,128)(2,1)S(1)}, u32[]{:S(2)}, u32[]{:S(2)}) collective-permute-start(bf16[64,1920]{1,0:T(8,128)(2,1)S(1)} %get-tuple-element.68), channel_id=1, source_target_pairs={{0,20},{4,16},{8,28},{12,24},{16,4},{20,0},{24,12},{28,8},{1,21},{... | collective-permute-start | bytes 737288 | tf_op jit(solution)/shard_map/ppermute | solution.py:619
  117.3 2.6 %collective-permute-done.22.refs_2_ = bf16[2,3,64,1024]{3,2,1,0:T(8,128)(2,1)S(1)} collective-permute-done((bf16[2,3,64,1024]{3,2,1,0:T(8,128)(2,1)S(1)}, bf16[2,3,64,1024]{3,2,1,0:T(8,128)(2,1)S(1)}, u32[]{:S(2)}, u32[]{:S(2)}) %collective-permute-start.22) | collective-permute-done | bytes 786464 | tf_op jit(solution)/shard_map/ppermute | solution.py:614
  121.5 2.2 %collective-permute-done.23.refs_1_.refs_16_ = bf16[2,64,3200]{2,1,0:T(8,128)(2,1)S(1)} collective-permute-done((bf16[2,64,3200]{2,1,0:T(8,128)(2,1)S(1)}, bf16[2,64,3200]{2,1,0:T(8,128)(2,1)S(1)}, u32[]{:S(2)}, u32[]{:S(2)}) %collective-permute-start.23) | collective-permute-done | bytes 819232 | tf_op jit(solution)/shard_map/ppermute | solution.py:614
  123.7 5.1 %back.7 = (bf16[64,1920]{1,0:T(8,128)(2,1)S(1)}, bf16[64,1920]{1,0:T(8,128)(2,1)S(1)}) custom-call(bf16[2,64,3200]{2,1,0:T(8,128)(2,1)S(1)} %activate.7.refs_0_.refs_15_, bf16[2,64,3200]{2,1,0:T(8,128)(2,1)S(1)} %collective-permute-done.23.refs_1_.refs_16_, bf16[2,1792,1024]{2,1,0:T(8,128)(2,1)S(1)} %get-tuple-element.46.refs_4_.refs_7_.refs_2_, ...), custom_call_target="tpu_custom_call" | custom-call | flops 1024 | bytes 1024 | tf_op jit(solution)/shard_map/back/pallas_call | solution.py:32
  130.2 3.6 %collective-permute-start.25 = (bf16[64,1920]{1,0:T(8,128)(2,1)S(1)}, bf16[64,1920]{1,0:T(8,128)(2,1)S(1)}, u32[]{:S(2)}, u32[]{:S(2)}) collective-permute-start(bf16[64,1920]{1,0:T(8,128)(2,1)S(1)} %get-tuple-element.71), channel_id=1, source_target_pairs={{0,28},{4,24},{8,20},{12,16},{16,12},{20,8},{24,4},{28,0},{1,29},{... | collective-permute-start | bytes 737288 | tf_op jit(solution)/shard_map/ppermute | solution.py:619
  133.8 19.5 %weight_grads.1 = (bf16[2,1792,1024]{2,1,0:T(8,128)(2,1)}, bf16[2,1792,1024]{2,1,0:T(8,128)(2,1)}, bf16[2,1024,1792]{2,1,0:T(8,128)(2,1)}) custom-call(bf16[1792,256]{1,0:T(8,128)(2,1)} %copy-done.3, bf16[256,1792]{1,0:T(8,128)(2,1)} %copy-done.4, bf16[2,256,1024]{2,1,0:T(8,128)(2,1)} %copy-done, bf16[2,256,1024]{2,1,0:T(8,128)(2,1)} %copy-done.1, ...), custom_call_target="tpu_custom_call" | custom-call | flops 1024 | bytes 1024 | tf_op jit(solution)/shard_map/weight_grads/pallas_call | solution.py:32
  153.4 4.6 %unpack.1 = (bf16[128,1792]{1,0:T(8,128)(2,1)}, f32[6,128]{1,0:T(8,128)S(1)}) custom-call(s32[2]{0:T(128)S(1)} %pad_add_fusion.where_ref.refs_0_, s32[4,128]{1,0:T(4,128)S(1)} %bitcast.9, s32[6,128]{1,0:T(8,128)S(1)} %bitcast.8, bf16[64,1920]{1,0:T(8,128)(2,1)S(1)} %get-tuple-element.62.refs_0_, bf16[64,1920]{1,0:T(8,128)(2,1)S(1)} %collective-permute-done.13.refs_1_, ...), custom_call_target="tpu_custom_call" | custom-call | flops 1024 | bytes 1024 | tf_op jit(solution)/shard_map/unpack/pallas_call | solution.py:229
  (99 shorter events, 14.7 us)
Async XLA Ops:
  3.7 14.9 %collective-permute-start = (bf16[64,3712]{1,0:T(8,128)(2,1)S(1)}, bf16[64,3712]{1,0:T(8,128)(2,1)S(1)}, u32[]{:S(2)}, u32[]{:S(2)}) collective-permute-start(bf16[64,3712]{1,0:T(8,128)(2,1)S(1)} %get-tuple-element.44), channel_id=1, source_target_pairs={{0,4},{4,0},{8,12},{12,8},{16,20},{20,16},{24,28},{28,24},{1,5},{5... | collective-permute-start | bytes 1425416 | tf_op jit(solution)/shard_map/ppermute | solution.py:619
  6.7 34.0 %collective-permute-start.3 = (bf16[64,3712]{1,0:T(8,128)(2,1)S(1)}, bf16[64,3712]{1,0:T(8,128)(2,1)S(1)}, u32[]{:S(2)}, u32[]{:S(2)}) collective-permute-start(bf16[64,3712]{1,0:T(8,128)(2,1)S(1)} %get-tuple-element.51), channel_id=1, source_target_pairs={{0,8},{4,12},{8,0},{12,4},{16,24},{20,28},{24,16},{28,20},{1,9},{5... | collective-permute-start | bytes 1425416 | tf_op jit(solution)/shard_map/ppermute | solution.py:619
  8.3 39.9 %collective-permute-start.4 = (bf16[64,3712]{1,0:T(8,128)(2,1)S(1)}, bf16[64,3712]{1,0:T(8,128)(2,1)S(1)}, u32[]{:S(2)}, u32[]{:S(2)}) collective-permute-start(bf16[64,3712]{1,0:T(8,128)(2,1)S(1)} %get-tuple-element.52), channel_id=1, source_target_pairs={{0,12},{4,8},{8,4},{12,0},{16,28},{20,24},{24,20},{28,16},{1,13},{... | collective-permute-start | bytes 1425416 | tf_op jit(solution)/shard_map/ppermute | solution.py:619
  8.3 44.7 %collective-permute-start.6 = (bf16[128,3712]{1,0:T(8,128)(2,1)S(1)}, bf16[128,3712]{1,0:T(8,128)(2,1)S(1)}, u32[]{:S(2)}, u32[]{:S(2)}) collective-permute-start(bf16[128,3712]{1,0:T(8,128)(2,1)S(1)} %get-tuple-element.45.refs_3_), channel_id=1, source_target_pairs={{0,16},{4,20},{8,24},{12,28},{16,0},{20,4},{24,8},{28,12},{1,17},{... | collective-permute-start | bytes 2850824 | tf_op jit(solution)/shard_map/ppermute | solution.py:619
  23.4 3.5 %collective-permute-start.1 = (f32[2,3,64,1024]{3,2,1,0:T(8,128)S(1)}, f32[2,3,64,1024]{3,2,1,0:T(8,128)S(1)}, u32[]{:S(2)}, u32[]{:S(2)}) collective-permute-start(f32[2,3,64,1024]{3,2,1,0:T(8,128)S(1)} %get-tuple-element.50), channel_id=1, source_target_pairs={{0,1},{1,0},{2,3},{3,2},{4,5},{5,4},{6,7},{7,6},{8,9},{9,8},{10,11... | collective-permute-start | bytes 4718600 | tf_op jit(solution)/shard_map/ppermute | solution.py:614
  27.1 33.7 %collective-permute-start.2 = (bf16[2,3,64,1024]{3,2,1,0:T(8,128)(2,1)S(1)}, bf16[2,3,64,1024]{3,2,1,0:T(8,128)(2,1)S(1)}, u32[]{:S(2)}, u32[]{:S(2)}) collective-permute-start(bf16[2,3,64,1024]{3,2,1,0:T(8,128)(2,1)S(1)} %add.11.refs_7_.refs_1_), channel_id=1, source_target_pairs={{0,2},{1,3},{2,0},{3,1},{4,6},{5,7},{6,4},{7,5},{8,10},{9,11},{10,... | collective-permute-start | bytes 2359304 | tf_op jit(solution)/shard_map/ppermute | solution.py:614
  52.9 6.1 %collective-permute-start.5 = (f32[2,3,64,1024]{3,2,1,0:T(8,128)S(1)}, f32[2,3,64,1024]{3,2,1,0:T(8,128)S(1)}, u32[]{:S(2)}, u32[]{:S(2)}) collective-permute-start(f32[2,3,64,1024]{3,2,1,0:T(8,128)S(1)} %get-tuple-element.54), channel_id=1, source_target_pairs={{0,1},{1,0},{2,3},{3,2},{4,5},{5,4},{6,7},{7,6},{8,9},{9,8},{10,11... | collective-permute-start | bytes 4718600 | tf_op jit(solution)/shard_map/ppermute | solution.py:614
  54.7 14.3 %collective-permute-start.11 = (bf16[64,3712]{1,0:T(8,128)(2,1)S(1)}, bf16[64,3712]{1,0:T(8,128)(2,1)S(1)}, u32[]{:S(2)}, u32[]{:S(2)}) collective-permute-start(bf16[64,3712]{1,0:T(8,128)(2,1)S(1)} %get-tuple-element.58), channel_id=1, source_target_pairs={{0,4},{4,0},{8,12},{12,8},{16,20},{20,16},{24,28},{28,24},{1,5},{5... | collective-permute-start | bytes 1425416 | tf_op jit(solution)/shard_map/ppermute | solution.py:619
  57.5 21.6 %collective-permute-start.9 = (bf16[64,3712]{1,0:T(8,128)(2,1)S(1)}, bf16[64,3712]{1,0:T(8,128)(2,1)S(1)}, u32[]{:S(2)}, u32[]{:S(2)}) collective-permute-start(bf16[64,3712]{1,0:T(8,128)(2,1)S(1)} %get-tuple-element.56), channel_id=1, source_target_pairs={{0,8},{4,12},{8,0},{12,4},{16,24},{20,28},{24,16},{28,20},{1,9},{5... | collective-permute-start | bytes 1425416 | tf_op jit(solution)/shard_map/ppermute | solution.py:619
  57.5 23.0 %collective-permute-start.10 = (bf16[64,3712]{1,0:T(8,128)(2,1)S(1)}, bf16[64,3712]{1,0:T(8,128)(2,1)S(1)}, u32[]{:S(2)}, u32[]{:S(2)}) collective-permute-start(bf16[64,3712]{1,0:T(8,128)(2,1)S(1)} %get-tuple-element.57), channel_id=1, source_target_pairs={{0,12},{4,8},{8,4},{12,0},{16,28},{20,24},{24,20},{28,16},{1,13},{... | collective-permute-start | bytes 1425416 | tf_op jit(solution)/shard_map/ppermute | solution.py:619
  59.3 26.1 %collective-permute-start.8 = (bf16[2,3,64,1024]{3,2,1,0:T(8,128)(2,1)S(1)}, bf16[2,3,64,1024]{3,2,1,0:T(8,128)(2,1)S(1)}, u32[]{:S(2)}, u32[]{:S(2)}) collective-permute-start(bf16[2,3,64,1024]{3,2,1,0:T(8,128)(2,1)S(1)} %add.12.refs_5_.refs_1_), channel_id=1, source_target_pairs={{0,2},{1,3},{2,0},{3,1},{4,6},{5,7},{6,4},{7,5},{8,10},{9,11},{10,... | collective-permute-start | bytes 2359304 | tf_op jit(solution)/shard_map/ppermute | solution.py:614
  62.4 24.7 %collective-permute-start.7 = (bf16[2,64,3200]{2,1,0:T(8,128)(2,1)S(1)}, bf16[2,64,3200]{2,1,0:T(8,128)(2,1)S(1)}, u32[]{:S(2)}, u32[]{:S(2)}) collective-permute-start(bf16[2,64,3200]{2,1,0:T(8,128)(2,1)S(1)} %activate.4.refs_7_.refs_0_.refs_4_), channel_id=1, source_target_pairs={{0,1},{1,0},{2,3},{3,2},{4,5},{5,4},{6,7},{7,6},{8,9},{9,8},{10,11... | collective-permute-start | bytes 2457608 | tf_op jit(solution)/shard_map/ppermute | solution.py:614
  73.9 3.5 %collective-permute-start.12 = (f32[2,3,64,1024]{3,2,1,0:T(8,128)S(1)}, f32[2,3,64,1024]{3,2,1,0:T(8,128)S(1)}, u32[]{:S(2)}, u32[]{:S(2)}) collective-permute-start(f32[2,3,64,1024]{3,2,1,0:T(8,128)S(1)} %get-tuple-element.60), channel_id=1, source_target_pairs={{0,1},{1,0},{2,3},{3,2},{4,5},{5,4},{6,7},{7,6},{8,9},{9,8},{10,11... | collective-permute-start | bytes 4718600 | tf_op jit(solution)/shard_map/ppermute | solution.py:614
  77.6 20.4 %collective-permute-start.17 = (bf16[2,3,64,1024]{3,2,1,0:T(8,128)(2,1)S(1)}, bf16[2,3,64,1024]{3,2,1,0:T(8,128)(2,1)S(1)}, u32[]{:S(2)}, u32[]{:S(2)}) collective-permute-start(bf16[2,3,64,1024]{3,2,1,0:T(8,128)(2,1)S(1)} %add.13.refs_7_.refs_1_), channel_id=1, source_target_pairs={{0,2},{1,3},{2,0},{3,1},{4,6},{5,7},{6,4},{7,5},{8,10},{9,11},{10,... | collective-permute-start | bytes 2359304 | tf_op jit(solution)/shard_map/ppermute | solution.py:614
  87.0 5.8 %collective-permute-start.14 = (bf16[2,64,3200]{2,1,0:T(8,128)(2,1)S(1)}, bf16[2,64,3200]{2,1,0:T(8,128)(2,1)S(1)}, u32[]{:S(2)}, u32[]{:S(2)}) collective-permute-start(bf16[2,64,3200]{2,1,0:T(8,128)(2,1)S(1)} %activate.5.refs_4_.refs_0_.refs_6_), channel_id=1, source_target_pairs={{0,1},{1,0},{2,3},{3,2},{4,5},{5,4},{6,7},{7,6},{8,9},{9,8},{10,11... | collective-permute-start | bytes 2457608 | tf_op jit(solution)/shard_map/ppermute | solution.py:614
  92.3 7.3 %collective-permute-start.19 = (f32[2,3,64,1024]{3,2,1,0:T(8,128)S(1)}, f32[2,3,64,1024]{3,2,1,0:T(8,128)S(1)}, u32[]{:S(2)}, u32[]{:S(2)}) collective-permute-start(f32[2,3,64,1024]{3,2,1,0:T(8,128)S(1)} %get-tuple-element.66), channel_id=1, source_target_pairs={{0,1},{1,0},{2,3},{3,2},{4,5},{5,4},{6,7},{7,6},{8,9},{9,8},{10,11... | collective-permute-start | bytes 4718600 | tf_op jit(solution)/shard_map/ppermute | solution.py:614
  99.5 5.4 %collective-permute-start.18 = (bf16[2,64,3200]{2,1,0:T(8,128)(2,1)S(1)}, bf16[2,64,3200]{2,1,0:T(8,128)(2,1)S(1)}, u32[]{:S(2)}, u32[]{:S(2)}) collective-permute-start(bf16[2,64,3200]{2,1,0:T(8,128)(2,1)S(1)} %activate.6.refs_2_.refs_0_.refs_13_), channel_id=1, source_target_pairs={{0,1},{1,0},{2,3},{3,2},{4,5},{5,4},{6,7},{7,6},{8,9},{9,8},{10,11... | collective-permute-start | bytes 2457608 | tf_op jit(solution)/shard_map/ppermute | solution.py:614
  99.8 20.0 %collective-permute-start.22 = (bf16[2,3,64,1024]{3,2,1,0:T(8,128)(2,1)S(1)}, bf16[2,3,64,1024]{3,2,1,0:T(8,128)(2,1)S(1)}, u32[]{:S(2)}, u32[]{:S(2)}) collective-permute-start(bf16[2,3,64,1024]{3,2,1,0:T(8,128)(2,1)S(1)} %add.14.refs_4_.refs_1_), channel_id=1, source_target_pairs={{0,2},{1,3},{2,0},{3,1},{4,6},{5,7},{6,4},{7,5},{8,10},{9,11},{10,... | collective-permute-start | bytes 2359304 | tf_op jit(solution)/shard_map/ppermute | solution.py:614
  101.3 11.4 %collective-permute-start.15 = (bf16[64,1920]{1,0:T(8,128)(2,1)S(1)}, bf16[64,1920]{1,0:T(8,128)(2,1)S(1)}, u32[]{:S(2)}, u32[]{:S(2)}) collective-permute-start(bf16[64,1920]{1,0:T(8,128)(2,1)S(1)} %get-tuple-element.64.refs_5_), channel_id=1, source_target_pairs={{0,8},{4,12},{8,0},{12,4},{16,24},{20,28},{24,16},{28,20},{1,9},{5... | collective-permute-start | bytes 737288 | tf_op jit(solution)/shard_map/ppermute | solution.py:619
  101.6 15.6 %collective-permute-start.16 = (bf16[64,1920]{1,0:T(8,128)(2,1)S(1)}, bf16[64,1920]{1,0:T(8,128)(2,1)S(1)}, u32[]{:S(2)}, u32[]{:S(2)}) collective-permute-start(bf16[64,1920]{1,0:T(8,128)(2,1)S(1)} %get-tuple-element.65), channel_id=1, source_target_pairs={{0,12},{4,8},{8,4},{12,0},{16,28},{20,24},{24,20},{28,16},{1,13},{... | collective-permute-start | bytes 737288 | tf_op jit(solution)/shard_map/ppermute | solution.py:619
  104.5 48.8 %collective-permute-start.13 = (bf16[64,1920]{1,0:T(8,128)(2,1)S(1)}, bf16[64,1920]{1,0:T(8,128)(2,1)S(1)}, u32[]{:S(2)}, u32[]{:S(2)}) collective-permute-start(bf16[64,1920]{1,0:T(8,128)(2,1)S(1)} %get-tuple-element.63), channel_id=1, source_target_pairs={{0,4},{4,0},{8,12},{12,8},{16,20},{20,16},{24,28},{28,24},{1,5},{5... | collective-permute-start | bytes 737288 | tf_op jit(solution)/shard_map/ppermute | solution.py:619
  110.2 43.2 %collective-permute-start.20 = (bf16[64,1920]{1,0:T(8,128)(2,1)S(1)}, bf16[64,1920]{1,0:T(8,128)(2,1)S(1)}, u32[]{:S(2)}, u32[]{:S(2)}) collective-permute-start(bf16[64,1920]{1,0:T(8,128)(2,1)S(1)} %get-tuple-element.67.refs_8_), channel_id=1, source_target_pairs={{0,16},{4,20},{8,24},{12,28},{16,0},{20,4},{24,8},{28,12},{1,17},{... | collective-permute-start | bytes 737288 | tf_op jit(solution)/shard_map/ppermute | solution.py:619
  112.7 4.6 %copy-start = (bf16[2,256,1024]{2,1,0:T(8,128)(2,1)}, bf16[2,256,1024]{2,1,0:T(8,128)(2,1)S(1)}, u32[]{:S(2)}) copy-start(bf16[2,256,1024]{2,1,0:T(8,128)(2,1)S(1)} %get-tuple-element.75.refs_2_) | copy-start | bytes 3145732
  112.7 4.6 %copy-start.1 = (bf16[2,256,1024]{2,1,0:T(8,128)(2,1)}, bf16[2,256,1024]{2,1,0:T(8,128)(2,1)S(1)}, u32[]{:S(2)}) copy-start(bf16[2,256,1024]{2,1,0:T(8,128)(2,1)S(1)} %get-tuple-element.76.refs_3_) | copy-start | bytes 3145732
  112.7 4.6 %copy-start.2 = (bf16[2,1024,256]{2,1,0:T(8,128)(2,1)}, bf16[2,1024,256]{2,1,0:T(8,128)(2,1)S(1)}, u32[]{:S(2)}) copy-start(bf16[2,1024,256]{2,1,0:T(8,128)(2,1)S(1)} %get-tuple-element.77.refs_4_) | copy-start | bytes 3145732
  112.7 4.5 %copy-start.3 = (bf16[1792,256]{1,0:T(8,128)(2,1)}, bf16[1792,256]{1,0:T(8,128)(2,1)S(1)}, u32[]{:S(2)}) copy-start(bf16[1792,256]{1,0:T(8,128)(2,1)S(1)} %get-tuple-element.69.refs_0_) | copy-start | bytes 2752516
  112.7 40.6 %collective-permute-start.21 = (bf16[64,1920]{1,0:T(8,128)(2,1)S(1)}, bf16[64,1920]{1,0:T(8,128)(2,1)S(1)}, u32[]{:S(2)}, u32[]{:S(2)}) collective-permute-start(bf16[64,1920]{1,0:T(8,128)(2,1)S(1)} %get-tuple-element.68), channel_id=1, source_target_pairs={{0,20},{4,16},{8,28},{12,24},{16,4},{20,0},{24,12},{28,8},{1,21},{... | collective-permute-start | bytes 737288 | tf_op jit(solution)/shard_map/ppermute | solution.py:619
  121.3 2.4 %collective-permute-start.23 = (bf16[2,64,3200]{2,1,0:T(8,128)(2,1)S(1)}, bf16[2,64,3200]{2,1,0:T(8,128)(2,1)S(1)}, u32[]{:S(2)}, u32[]{:S(2)}) collective-permute-start(bf16[2,64,3200]{2,1,0:T(8,128)(2,1)S(1)} %activate.7.refs_0_.refs_15_), channel_id=1, source_target_pairs={{0,1},{1,0},{2,3},{3,2},{4,5},{5,4},{6,7},{7,6},{8,9},{9,8},{10,11... | collective-permute-start | bytes 2457608 | tf_op jit(solution)/shard_map/ppermute | solution.py:614
  128.8 24.5 %collective-permute-start.24 = (bf16[64,1920]{1,0:T(8,128)(2,1)S(1)}, bf16[64,1920]{1,0:T(8,128)(2,1)S(1)}, u32[]{:S(2)}, u32[]{:S(2)}) collective-permute-start(bf16[64,1920]{1,0:T(8,128)(2,1)S(1)} %get-tuple-element.70.refs_17_), channel_id=1, source_target_pairs={{0,24},{4,28},{8,16},{12,20},{16,8},{20,12},{24,0},{28,4},{1,25},{... | collective-permute-start | bytes 737288 | tf_op jit(solution)/shard_map/ppermute | solution.py:619
  130.2 23.1 %collective-permute-start.25 = (bf16[64,1920]{1,0:T(8,128)(2,1)S(1)}, bf16[64,1920]{1,0:T(8,128)(2,1)S(1)}, u32[]{:S(2)}, u32[]{:S(2)}) collective-permute-start(bf16[64,1920]{1,0:T(8,128)(2,1)S(1)} %get-tuple-element.71), channel_id=1, source_target_pairs={{0,28},{4,24},{8,20},{12,16},{16,12},{20,8},{24,4},{28,0},{1,29},{... | collective-permute-start | bytes 737288 | tf_op jit(solution)/shard_map/ppermute | solution.py:619
  133.8 19.5 %copy-start.5 = (s32[128,6]{0,1:T(8,128)S(1)}, s32[128,6]{0,1:T(8,128)}, u32[]{:S(2)}) copy-start(s32[128,6]{0,1:T(8,128)} %param.11) | copy-start | bytes 9220
  133.8 19.5 %copy-start.6 = (s32[128,4]{0,1:T(4,128)S(1)}, s32[128,4]{0,1:T(4,128)}, u32[]{:S(2)}) copy-start(s32[128,4]{0,1:T(4,128)} %param.12) | copy-start | bytes 6148
  (1 other events, 4.5 us)
